TPU v7x, 512 devices: a whole 4x8x8 slice. The times are simulated.
512 devices in a mesh: grp: 16 (over z, y_lo), blk: 32 (over x, y_hi, core).
Axes of the slice: x: 4, y: 8 (y_hi: 4, y_lo: 2; y = y_hi * 2 + y_lo), z: 8, core: 2. Of those that a mesh axis runs over, the one named last changes fastest.
Arguments:
- activations: bfloat16 [16384, 16384], P('grp', 'blk'), may hold values from -8 to 8
- output_grads: bfloat16 [16384, 4096], P('blk', 'grp'), may hold values from -8 to 8
- grad_weight: bfloat16 [16384, 4096], P('blk', 'grp'), may hold values from -96 to 96
Outputs:
- preconditioned: bfloat16 [16384, 4096], P('blk', 'grp')
All inputs are finite; a program needn't handle non-finite values.
Results may differ from a plain program's by a relative error of at most 0.01.
The roundings to bfloat16 on the way count: a program that leaves them out, or rounds other values in their place, can miss the bound.
Values may be sent and summed in bfloat16 or wider, within the bound.
No kernel may reach another device: no remote copies, remote signals or barrier semaphores. Data moves between devices by JAX's collectives and lax.ppermute only.
A program may use at most 64 MiB of HBM per device.

v0:
```python
import jax
import jax.numpy as jnp
from jax import lax
from jax.sharding import PartitionSpec as P

ITERS = 6


DAMP_ROOT = 0.1


def from_partner(value, axis, bit):
    mask = 2**bit
    pairs = [(source, source ^ mask) for source in range(lax.axis_size(axis))]
    return lax.ppermute(value, axis, pairs)


def gram_matrix(data):
    return lax.dot_general(data, data, (((0,), (0,)), ((), ())), preferred_element_type=jnp.float32)


def place_entry(length, position, amount):
    matches = jnp.arange(length, dtype=jnp.int32) == position
    return jnp.where(matches, amount, 0.0).astype(jnp.float32)


def pick_entry(vector, position):
    matches = jnp.arange(vector.shape[0], dtype=jnp.int32) == position
    return jnp.sum(jnp.where(matches, vector, 0.0))


def invert_whole(damped, first_scale, identity):
    iterate = identity * first_scale
    damped_half = damped.astype(jnp.bfloat16)
    for sweep in range(ITERS):
        current = iterate.astype(jnp.bfloat16)
        product = jnp.dot(damped_half, current, preferred_element_type=jnp.float32).astype(
            jnp.bfloat16
        )
        iterate = 2.0 * iterate - jnp.dot(product, current, preferred_element_type=jnp.float32)
    return iterate.astype(jnp.bfloat16)


def shards(activations, output_grads, grad_weight):
    groups = lax.axis_size("grp")
    owners = lax.axis_size("blk")
    group_pos = lax.axis_index("grp")
    owner_pos = lax.axis_index("blk")
    block_width = grad_weight.shape[0]
    half_width = grad_weight.shape[1]
    total_tokens = activations.shape[0] * groups
    out_blocks = groups // 2
    parity = group_pos % 2
    lower_first = parity == 0
    slab_rows = block_width // groups
    first_row = group_pos * slab_rows
    identity = jnp.eye(block_width, dtype=jnp.float32)
    partner_grads, partner_weight = from_partner((output_grads, grad_weight), "grp", 0)
    grads_block = jnp.where(
        lower_first,
        jnp.concatenate([output_grads, partner_grads], axis=1),
        jnp.concatenate([partner_grads, output_grads], axis=1),
    )
    weight_block = jnp.where(
        lower_first,
        jnp.concatenate([grad_weight, partner_weight], axis=1),
        jnp.concatenate([partner_weight, grad_weight], axis=1),
    )
    part_in = gram_matrix(activations) / total_tokens
    part_out = gram_matrix(grads_block) / total_tokens
    covariance_out = lax.psum(part_out, "blk")
    covariance_slab = lax.psum_scatter(part_in, "grp", scatter_dimension=0, tiled=True)
    own_trace = jnp.trace(lax.dynamic_slice_in_dim(covariance_slab, first_row, slab_rows, 1))
    keeper = jnp.logical_and(owner_pos == 0, lower_first)
    energy_out = jnp.where(keeper, jnp.trace(covariance_out), 0.0)
    traces_in, traces_out = lax.psum(
        (
            place_entry(owners, owner_pos, own_trace),
            place_entry(out_blocks, group_pos // 2, energy_out),
        ),
        ("grp", "blk"),
    )
    mean_in = jnp.sum(traces_in) / (owners * block_width)
    mean_out = jnp.sum(traces_out) / (out_blocks * block_width)
    pi_ratio = jnp.sqrt(mean_in / mean_out)
    damping_in = DAMP_ROOT * pi_ratio
    damping_out = DAMP_ROOT / pi_ratio
    scale_in = 1.0 / (pick_entry(traces_in, owner_pos) + block_width * damping_in)
    scale_out = 1.0 / (pick_entry(traces_out, group_pos // 2) + block_width * damping_out)
    inverse_out = invert_whole(covariance_out + damping_out * identity, scale_out, identity)
    row_ids = jnp.arange(slab_rows, dtype=jnp.int32)[:, None] + first_row
    col_ids = jnp.arange(block_width, dtype=jnp.int32)[None, :]
    identity_rows = (row_ids == col_ids).astype(jnp.float32)
    damped_rows = (covariance_slab + damping_in * identity_rows).astype(jnp.bfloat16)
    iterate_rows = identity_rows * scale_in
    current = (identity * scale_in).astype(jnp.bfloat16)
    for sweep in range(ITERS):
        product = jnp.dot(damped_rows, current, preferred_element_type=jnp.float32).astype(
            jnp.bfloat16
        )
        iterate_rows = 2.0 * iterate_rows - jnp.dot(
            product, current, preferred_element_type=jnp.float32
        )
        current = lax.all_gather(iterate_rows.astype(jnp.bfloat16), "grp", axis=0, tiled=True)
    left_part = jnp.dot(current, weight_block, preferred_element_type=jnp.float32).astype(
        jnp.bfloat16
    )
    right_columns = lax.dynamic_slice_in_dim(inverse_out, parity * half_width, half_width, 1)
    return jnp.dot(left_part, right_columns, preferred_element_type=jnp.float32).astype(
        jnp.bfloat16
    )


def solution(mesh):
    in_specs = (P("grp", "blk"), P("blk", "grp"), P("blk", "grp"))
    out_specs = P("blk", "grp")
    return jax.shard_map(shards, mesh=mesh, in_specs=in_specs, out_specs=out_specs, check_vma=False)
```

profile of v0, /device:TPU:8, one launch (start us, length us, event | category | flops | bytes accessed | tf_op | source)
XLA Modules:
  0.0 662.7 jit_solution(3278907153674753868)
XLA Ops:
  7.4 0.0 copy-start
  7.4 0.0 all-reduce.3.cloned.1.call-start
  7.4 7.9 %collective-permute-start = (bf16[512,256]{1,0:T(8,128)(2,1)}, bf16[512,256]{1,0:T(8,128)(2,1)S(1)}, u32[]{:S(2)}, u32[]{:S(2)}) collective-permute-start(bf16[512,256]{1,0:T(8,128)(2,1)} %param.4), channel_id=1, source_target_pairs={{0,32},{32,0},{64,96},{96,64},{128,160},{160,128},{192,224},{224,1... | collective-permute-start | bytes 786440 | tf_op jit(solution)/shard_map/ppermute | solution.py:15
  15.2 4.5 collective-permute-done
  19.8 2.9 convolution_multiply_fusion
  22.7 0.0 all-reduce.3.cloned.1.call-update
  22.7 0.0 reduce-scatter.2.cloned.1.call-start
  22.8 0.0 copy-done
  22.8 1.7 convolution_multiply_fusion.1
  24.5 0.0 copy-start.3
  24.5 0.0 reduce-scatter.2.cloned.1.call-update
  24.5 0.9 copy-done.3
  25.4 3.9 collective-permute-start.1
  29.4 286.5 %all-reduce.3.cloned.1.call-done = f32[512,512]{1,0:T(8,128)} async-done(((f32[512,512]{1,0:T(8,128)}), f32[512,512]{1,0:T(8,128)}) %all-reduce.3.cloned.1.call-update) | async-done | bytes 1048592 | tf_op jit(solution)/shard_map/psum | solution.py:71
  315.9 0.0 copy-start.1
  315.9 2.0 select_reduce_fusion
  318.5 0.0 reduce-scatter.2.cloned.1.call-done
  318.6 1.4 select_reduce_fusion.1
  320.0 0.6 compare_select_fusion.3
  320.6 99.3 %all-reduce = (f32[32]{0:T(128)S(1)}, f32[8]{0:T(128)S(1)}) all-reduce(f32[32]{0:T(128)S(1)} %compare_select_fusion.3, f32[8]{0:T(128)S(1)} %compare_select_fusion.1), channel_id=1, replica_groups=mesh['grp'=16,'blk'=32] {'grp','blk'}, use_global_device_ids=true, to_apply=%region_2.3 | all-reduce | flops 40 | bytes 320 | tf_op jit(solution)/shard_map/psum | solution.py:76
  419.9 0.7 fusion.45
  420.6 0.6 fusion.44
  423.3 0.0 copy-done.1
  423.3 0.1 add_convert_fusion
  423.4 1.7 convolution_subtract_fusion.4
  425.1 2.7 convolution_subtract_fusion.3
  427.8 1.7 convolution_subtract_fusion.2
  429.5 3.8 convolution_subtract_fusion.1
  433.3 2.9 convolution_subtract_fusion
  436.3 0.0 copy-start.2
  436.3 1.7 fusion
  438.7 0.0 copy-done.2
  438.7 0.1 add_convert_fusion.1
  438.8 0.3 fusion.54
  439.1 35.5 %all_gather.18 = bf16[512,512]{1,0:T(8,128)(2,1)S(1)} all-gather(bf16[32,512]{1,0:T(8,128)(2,1)S(1)} %get-tuple-element.11), channel_id=1, replica_groups=mesh['grp'=16,'blk'=32] {'grp'}, dimensions={0}, use_global_device_ids=true | all-gather | bytes 557056 | tf_op jit(solution)/shard_map/all_gather | solution.py:104
  474.6 0.3 fusion.55
  475.0 35.7 %all_gather.19 = bf16[512,512]{1,0:T(8,128)(2,1)S(1)} all-gather(bf16[32,512]{1,0:T(8,128)(2,1)S(1)} %get-tuple-element.13), channel_id=1, replica_groups=mesh['grp'=16,'blk'=32] {'grp'}, dimensions={0}, use_global_device_ids=true | all-gather | bytes 557056 | tf_op jit(solution)/shard_map/all_gather | solution.py:104
  510.6 0.3 fusion.56
  511.0 35.7 %all_gather.20 = bf16[512,512]{1,0:T(8,128)(2,1)S(1)} all-gather(bf16[32,512]{1,0:T(8,128)(2,1)S(1)} %get-tuple-element.15), channel_id=1, replica_groups=mesh['grp'=16,'blk'=32] {'grp'}, dimensions={0}, use_global_device_ids=true | all-gather | bytes 557056 | tf_op jit(solution)/shard_map/all_gather | solution.py:104
  546.7 0.3 fusion.57
  547.0 35.0 %all_gather.21 = bf16[512,512]{1,0:T(8,128)(2,1)S(1)} all-gather(bf16[32,512]{1,0:T(8,128)(2,1)S(1)} %get-tuple-element.17), channel_id=1, replica_groups=mesh['grp'=16,'blk'=32] {'grp'}, dimensions={0}, use_global_device_ids=true | all-gather | bytes 557056 | tf_op jit(solution)/shard_map/all_gather | solution.py:104
  582.1 0.3 fusion.58
  582.4 35.6 %all_gather.22 = bf16[512,512]{1,0:T(8,128)(2,1)S(1)} all-gather(bf16[32,512]{1,0:T(8,128)(2,1)S(1)} %get-tuple-element.19), channel_id=1, replica_groups=mesh['grp'=16,'blk'=32] {'grp'}, dimensions={0}, use_global_device_ids=true | all-gather | bytes 557056 | tf_op jit(solution)/shard_map/all_gather | solution.py:104
  618.0 0.3 fusion.3
  618.3 34.5 %all_gather.23 = bf16[512,512]{1,0:T(8,128)(2,1)S(1)} all-gather(bf16[32,512]{1,0:T(8,128)(2,1)S(1)} %fusion.3), channel_id=1, replica_groups=mesh['grp'=16,'blk'=32] {'grp'}, dimensions={0}, use_global_device_ids=true | all-gather | bytes 557056 | tf_op jit(solution)/shard_map/all_gather | solution.py:104
  652.8 0.0 collective-permute-done.1
  652.8 2.5 fusion.2
  (2 shorter events, 0.0 us)
Async XLA Ops:
  7.4 15.4 %copy-start = (bf16[1024,512]{1,0:T(8,128)(2,1)S(1)}, bf16[1024,512]{1,0:T(8,128)(2,1)}, u32[]{:S(2)}) copy-start(bf16[1024,512]{1,0:T(8,128)(2,1)} %param.3) | copy-start | bytes 3145732
  7.4 308.5 %all-reduce.3.cloned.1.call-start = ((), (), s32[]{:S(2)}) async-start(), calls=%async_computation.2 | async-start | bytes 2097152 | tf_op jit(solution)/shard_map/psum | solution.py:71
  7.4 12.4 %collective-permute-start = (bf16[512,256]{1,0:T(8,128)(2,1)}, bf16[512,256]{1,0:T(8,128)(2,1)S(1)}, u32[]{:S(2)}, u32[]{:S(2)}) collective-permute-start(bf16[512,256]{1,0:T(8,128)(2,1)} %param.4), channel_id=1, source_target_pairs={{0,32},{32,0},{64,96},{96,64},{128,160},{160,128},{192,224},{224,1... | collective-permute-start | bytes 786440 | tf_op jit(solution)/shard_map/ppermute | solution.py:15
  22.7 295.8 %reduce-scatter.2.cloned.1.call-start = ((), (), s32[]{:S(2)}) async-start(), calls=%async_computation.1 | async-start | bytes 1114112 | tf_op jit(solution)/shard_map/reduce_scatter | solution.py:72
  24.5 0.9 copy-start.3
  25.4 627.3 %collective-permute-start.1 = (bf16[512,256]{1,0:T(8,128)(2,1)S(1)}, bf16[512,256]{1,0:T(8,128)(2,1)S(1)}, u32[]{:S(2)}, u32[]{:S(2)}) collective-permute-start(bf16[512,256]{1,0:T(8,128)(2,1)S(1)} %copy-done.3), channel_id=1, source_target_pairs={{0,32},{32,0},{64,96},{96,64},{128,160},{160,128},{192,224},{224,1... | collective-permute-start | bytes 786440 | tf_op jit(solution)/shard_map/ppermute | solution.py:15
  315.9 107.4 %copy-start.1 = (f32[512,512]{1,0:T(8,128)S(1)}, f32[512,512]{1,0:T(8,128)}, u32[]{:S(2)}) copy-start(f32[512,512]{1,0:T(8,128)} %all-reduce.3.cloned.1.call-done) | copy-start | bytes 3145732
  436.3 2.4 copy-start.2
Sparse Core Ops, SparseCore 0:
  22.8 292.9 all-reduce.2
Sparse Core Ops, SparseCore 1:
  26.0 75.3 reduce-scatter.1
where the time goes:
time: 663 us
  blocking collectives  311 us (47%)
  waiting for transfers between devices  291 us (44%)
  matrix products  23.7 us (4%)
  between operations  18.5 us (3%)
  starting transfers between devices  11.8 us (2%)
    psum x1, waiting for transfers between devices, shards(): covariance_out = lax.psum(part_out, 'blk')  286 us
    all_gather x6, blocking collectives, shards(): lax.all_gather(iterate_rows.astype(jnp.bfloat16), 'grp', axis=0, tiled=True)  212 us
    psum x1, blocking collectives, shards(): lax.psum((place_entry(owners, owner_pos, own_trace), place_entry(out_bloc...  99.3 us
    dot_general x6, matrix products, invert_whole(): jnp.dot(product, current, preferred_element_type=jnp.float32)  14.6 us
  transfers between devices with their start and end apart: 4, of which 2 were waited for; matrix products, arithmetic and copies ran while one was open for 4% of the time, Pallas kernels for 0%

commit v1 on v0

v1 whole, which is shorter than its diff:
```python
import jax
import jax.numpy as jnp
from jax import lax
from jax.experimental import pallas as pl
from jax.experimental.pallas import tpu as pltpu
from jax.sharding import PartitionSpec as P

ITERS = 6
DAMP_ROOT = 0.1
TILE = 128
CORES = 2
EXTRA = 8
EXTRA_HALF = 16
VMEM_LIMIT = 48 * 1024 * 1024


def tile_plan(count):
    off = [(i, j) for i in range(count) for j in range(i + 1, count)]
    pairs = [(i, i + 1) for i in range(0, count, 2)]
    return off, pairs


def tile_masks():
    rows = lax.broadcasted_iota(jnp.int32, (TILE, TILE), 0)
    cols = lax.broadcasted_iota(jnp.int32, (TILE, TILE), 1)
    return rows, cols


def gram_tiles(left, right, scale):
    return scale * lax.dot_general(
        left, right, (((0,), (0,)), ((), ())), preferred_element_type=jnp.float32
    )


def packed_gram(data_ref, scale, store):
    width = data_ref.shape[1]
    count = width // TILE
    half = width // 2
    low, high = data_ref[:, :half], data_ref[:, half:]
    parts = {
        (0, 0): gram_tiles(low, low, scale),
        (0, 1): gram_tiles(low, high, scale),
        (1, 1): gram_tiles(high, high, scale),
    }
    per = count // 2

    def tile(i, j):
        part = parts[(i // per, j // per)]
        r, c = (i % per) * TILE, (j % per) * TILE
        return part[r : r + TILE, c : c + TILE]

    off, pairs = tile_plan(count)
    rows, cols = tile_masks()
    for position, (i, j) in enumerate(off):
        store(position, tile(i, j))
    for position, (i, j) in enumerate(pairs):
        store(len(off) + position, jnp.where(cols > rows, tile(i, i), tile(j, j)))
    return jnp.concatenate(
        [
            jnp.sum(jnp.where(rows == cols, tile(i, i), 0.0), axis=0, keepdims=True)
            for i in range(count)
        ],
        axis=0,
    )


def unpack_block(packed_ref, diagonal, damping, out_ref):
    count = out_ref.shape[0] // TILE
    off, pairs = tile_plan(count)
    rows, cols = tile_masks()

    def put(i, j, value):
        out_ref[i * TILE : (i + 1) * TILE, j * TILE : (j + 1) * TILE] = value.astype(jnp.bfloat16)

    def fetch(position):
        return packed_ref[position * TILE : (position + 1) * TILE, :].astype(jnp.float32)

    for position, (i, j) in enumerate(off):
        value = fetch(position)
        put(i, j, value)
        put(j, i, value.T)
    for position, (i, j) in enumerate(pairs):
        value = fetch(len(off) + position)
        other = value.T
        damped_i = diagonal[i : i + 1, :] + damping
        damped_j = diagonal[j : j + 1, :] + damping
        put(i, i, jnp.where(rows == cols, damped_i, jnp.where(cols > rows, value, other)))
        put(j, j, jnp.where(rows == cols, damped_j, jnp.where(cols < rows, value, other)))


def total_of(value):
    return jnp.sum(jnp.sum(value, axis=1, keepdims=True), axis=0, keepdims=True)


def gram_in_kernel(tokens, data_ref, grads_ref, out_ref):
    pieces, piece_rows = out_ref.shape[0], out_ref.shape[1] - EXTRA
    per_tile = TILE // piece_rows
    scale = 1.0 / tokens

    def store(position, value):
        for part in range(per_tile):
            out_ref[position * per_tile + part, :piece_rows, :] = value[
                part * piece_rows : (part + 1) * piece_rows
            ]

    diagonal = packed_gram(data_ref, scale, store)
    grads = grads_ref[...].astype(jnp.float32)
    energy = total_of(grads * grads) * scale
    filler = jnp.zeros((EXTRA - diagonal.shape[0] - 1, TILE), jnp.float32)
    extra = jnp.concatenate(
        [diagonal, jnp.broadcast_to(energy, (1, TILE)), filler], axis=0
    )
    for piece in range(pieces):
        out_ref[piece, piece_rows:, :] = extra


def gram_out_kernel(tokens, own_ref, other_ref, keep_ref, send_ref, data_ref, packed_ref):
    half = own_ref.shape[1]
    parity = lax.axis_index("grp") % 2
    core = lax.axis_index("blk") % CORES
    data_ref[:, pl.ds(pl.multiple_of(parity * half, half), half)] = own_ref[...]
    data_ref[:, pl.ds(pl.multiple_of((1 - parity) * half, half), half)] = other_ref[...]

    def store(position, value):
        packed_ref[position * TILE : (position + 1) * TILE, :] = value

    diagonal = packed_gram(data_ref, 1.0 / tokens, store)
    filler = jnp.zeros((EXTRA - diagonal.shape[0], TILE), jnp.float32)
    extra = jnp.concatenate([diagonal, filler], axis=0)
    pieces, piece_rows = keep_ref.shape[0], keep_ref.shape[1] - EXTRA
    share = pieces * piece_rows
    for ref, owner in ((keep_ref, core), (send_ref, 1 - core)):
        for piece in range(pieces):
            start = pl.multiple_of(owner * share + piece * piece_rows, piece_rows)
            ref[piece, :piece_rows, :] = packed_ref[pl.ds(start, piece_rows), :]
            ref[piece, piece_rows:, :] = extra


def add_kernel(left_ref, right_ref, out_ref):
    out_ref[...] = left_ref[...] + right_ref[...]


def sum_pieces(ref):
    total = ref[0]
    for piece in range(1, ref.shape[0]):
        total = total + ref[piece]
    return total


def sum_in_kernel(got_ref, send_ref, extra_ref):
    total = sum_pieces(got_ref)
    rows = send_ref.shape[1]
    rounded = total[:rows].astype(jnp.bfloat16)
    for piece in range(send_ref.shape[0]):
        send_ref[piece] = rounded
    extra_ref[...] = total[rows:]


def split_rows(value):
    high = value.astype(jnp.bfloat16).astype(jnp.float32)
    rest = value - high
    middle = rest.astype(jnp.bfloat16).astype(jnp.float32)
    return [high, middle, rest - middle]


def sum_out_kernel(count, got_ref, extra_in_ref, send_ref, extra_ref):
    total = sum_pieces(got_ref)
    rows = send_ref.shape[1] - EXTRA_HALF
    trace_in = jnp.broadcast_to(total_of(extra_in_ref[:count, :]), (1, TILE))
    energy_out = extra_in_ref[count : count + 1, :]
    scalars = split_rows(trace_in) + split_rows(energy_out)
    filler = jnp.zeros((EXTRA_HALF - len(scalars), TILE), jnp.float32)
    block = jnp.concatenate([total[:rows]] + scalars + [filler], axis=0).astype(jnp.bfloat16)
    for piece in range(send_ref.shape[0]):
        send_ref[piece] = block
    extra_ref[...] = total[rows:]


def invert_kernel(
    got_in_ref,
    got_out_ref,
    core_out_ref,
    extra_in_ref,
    extra_out_ref,
    weight_ref,
    other_weight_ref,
    result_ref,
    packed_ref,
    damped_in_ref,
    damped_out_ref,
    iterate_in_ref,
    iterate_out_ref,
    weight_block_ref,
):
    width = damped_in_ref.shape[0]
    count = width // TILE
    half = weight_ref.shape[1]
    parity = lax.axis_index("grp") % 2
    core = lax.axis_index("blk") % CORES
    pieces = got_out_ref.shape[0]
    piece_rows = got_out_ref.shape[1] - EXTRA_HALF
    own_column = pl.ds(pl.multiple_of(parity * half, half), half)
    other_column = pl.ds(pl.multiple_of((1 - parity) * half, half), half)
    weight_block_ref[:, own_column] = weight_ref[...]
    weight_block_ref[:, other_column] = other_weight_ref[...]

    scalars = jnp.zeros((EXTRA_HALF, TILE), jnp.float32)
    for ref in (got_out_ref, core_out_ref):
        for piece in range(pieces):
            scalars = scalars + ref[piece, piece_rows:, :].astype(jnp.float32)
    sum_in = scalars[0:1] + scalars[1:2] + scalars[2:3]
    sum_out = scalars[3:4] + scalars[4:5] + scalars[5:6]
    owners = pieces * CORES
    blocks_out = lax.axis_size("grp") // 2
    pi_ratio = jnp.sqrt((sum_in / (owners * width)) / (sum_out / (blocks_out * width)))
    damping_in = DAMP_ROOT * pi_ratio
    damping_out = DAMP_ROOT / pi_ratio
    diagonal_in = extra_in_ref[:count, :]
    diagonal_out = extra_out_ref[:count, :]
    scale_in = 1.0 / (total_of(diagonal_in) + width * damping_in)
    scale_out = 1.0 / (total_of(diagonal_out) + width * damping_out)

    in_rows = got_in_ref.shape[1]
    for piece in range(got_in_ref.shape[0]):
        packed_ref[piece * in_rows : (piece + 1) * in_rows, :] = got_in_ref[piece]
    unpack_block(packed_ref, diagonal_in, damping_in, damped_in_ref)
    share = pieces * piece_rows
    for ref, owner in ((got_out_ref, core), (core_out_ref, 1 - core)):
        for piece in range(pieces):
            start = pl.multiple_of(owner * share + piece * piece_rows, piece_rows)
            packed_ref[pl.ds(start, piece_rows), :] = ref[piece, :piece_rows, :]
    unpack_block(packed_ref, diagonal_out, damping_out, damped_out_ref)

    chains = (
        (damped_in_ref, iterate_in_ref, scale_in),
        (damped_out_ref, iterate_out_ref, scale_out),
    )
    rows, cols = tile_masks()
    for damped, iterate, scale in chains:
        factor = scale.astype(jnp.bfloat16).astype(jnp.float32)
        twice = jnp.where(rows == cols, 2.0 * scale, 0.0)
        for i in range(count):
            for j in range(count):
                place = (slice(i * TILE, (i + 1) * TILE), slice(j * TILE, (j + 1) * TILE))
                product = (damped[place].astype(jnp.float32) * factor).astype(jnp.bfloat16)
                moved = product.astype(jnp.float32) * factor
                iterate[place] = (twice - moved) if i == j else -moved

    def sweep(step, carry):
        currents = [iterate[...].astype(jnp.bfloat16) for _, iterate, _ in chains]
        products = [
            jnp.dot(damped[...], current, preferred_element_type=jnp.float32).astype(jnp.bfloat16)
            for (damped, _, _), current in zip(chains, currents)
        ]
        for (_, iterate, _), product, current in zip(chains, products, currents):
            iterate[...] = 2.0 * iterate[...] - jnp.dot(
                product, current, preferred_element_type=jnp.float32
            )
        return carry

    lax.fori_loop(0, ITERS - 1, sweep, 0)
    inverse_in = iterate_in_ref[...].astype(jnp.bfloat16)
    left = jnp.dot(inverse_in, weight_block_ref[...], preferred_element_type=jnp.float32)
    right = iterate_out_ref[:, own_column].astype(jnp.bfloat16)
    result_ref[...] = jnp.dot(
        left.astype(jnp.bfloat16), right, preferred_element_type=jnp.float32
    ).astype(jnp.bfloat16)


VMEM_SPEC = pl.BlockSpec(memory_space=pltpu.VMEM)


def local_call(kernel, name, operands, outs, scratch=(), flops=0):
    multiple = isinstance(outs, tuple)
    listed = outs if multiple else (outs,)
    moved = sum(a.size * a.dtype.itemsize for a in operands + tuple(listed))
    return pl.pallas_call(
        kernel,
        out_shape=outs,
        in_specs=[VMEM_SPEC] * len(operands),
        out_specs=tuple([VMEM_SPEC] * len(listed)) if multiple else VMEM_SPEC,
        scratch_shapes=list(scratch),
        compiler_params=pltpu.CompilerParams(vmem_limit_bytes=VMEM_LIMIT),
        cost_estimate=pl.CostEstimate(flops=flops, bytes_accessed=moved, transcendentals=0),
        name=name,
    )(*operands)


def shape_of(*dims, dtype=jnp.float32):
    return jax.ShapeDtypeStruct(dims, dtype)


def exchange(value, axis, groups=None):
    return lax.all_to_all(value, axis, 0, 0, tiled=True, axis_index_groups=groups)


def shards(activations, output_grads, grad_weight):
    groups = lax.axis_size("grp")
    owners = lax.axis_size("blk")
    width = grad_weight.shape[0]
    half = grad_weight.shape[1]
    count = width // TILE
    packed_rows = width * width // (2 * TILE)
    total_tokens = activations.shape[0] * groups
    in_rows = packed_rows // groups
    out_pieces = owners // CORES
    out_rows = packed_rows // owners
    partner = [(source, source ^ 1) for source in range(groups)]
    sibling = [(source, source ^ 1) for source in range(owners)]
    same_core = [[piece * CORES + core for piece in range(out_pieces)] for core in range(CORES)]

    other_grads = lax.ppermute(output_grads, "grp", partner)
    send_in = local_call(
        lambda *refs: gram_in_kernel(total_tokens, *refs),
        "gram_in",
        (activations, output_grads),
        shape_of(groups, in_rows + EXTRA, TILE),
        flops=2 * activations.shape[0] * width * width,
    )
    got_in = exchange(send_in, "grp")

    keep, give = local_call(
        lambda *refs: gram_out_kernel(total_tokens, *refs),
        "gram_out",
        (output_grads, other_grads),
        (shape_of(out_pieces, out_rows + EXTRA, TILE),) * 2,
        scratch=[
            pltpu.VMEM((output_grads.shape[0], width), jnp.bfloat16),
            pltpu.VMEM((packed_rows, TILE), jnp.float32),
        ],
        flops=2 * output_grads.shape[0] * width * width,
    )
    taken = lax.ppermute(give, "blk", sibling)
    send_out = local_call(add_kernel, "add_cores", (keep, taken), shape_of(*keep.shape))
    got_out = exchange(send_out, "blk", same_core)

    all_in, extra_in = local_call(
        sum_in_kernel,
        "sum_in",
        (got_in,),
        (shape_of(groups, in_rows, TILE, dtype=jnp.bfloat16), shape_of(EXTRA, TILE)),
    )
    all_in = exchange(all_in, "grp")
    all_out, extra_out = local_call(
        lambda *refs: sum_out_kernel(count, *refs),
        "sum_out",
        (got_out, extra_in),
        (
            shape_of(out_pieces, out_rows + EXTRA_HALF, TILE, dtype=jnp.bfloat16),
            shape_of(EXTRA, TILE),
        ),
    )
    all_out = exchange(all_out, "blk", same_core)
    core_out = lax.ppermute(all_out, "blk", sibling)
    other_weight = lax.ppermute(grad_weight, "grp", partner)

    block = (width, width)
    return local_call(
        invert_kernel,
        "invert",
        (all_in, all_out, core_out, extra_in, extra_out, grad_weight, other_weight),
        shape_of(width, half, dtype=jnp.bfloat16),
        scratch=[
            pltpu.VMEM((packed_rows, TILE), jnp.bfloat16),
            pltpu.VMEM(block, jnp.bfloat16),
            pltpu.VMEM(block, jnp.bfloat16),
            pltpu.VMEM(block, jnp.float32),
            pltpu.VMEM(block, jnp.float32),
            pltpu.VMEM(block, jnp.bfloat16),
        ],
        flops=2 * (4 * (ITERS - 1) + 2) * width * width * width,
    )


def solution(mesh):
    in_specs = (P("grp", "blk"), P("blk", "grp"), P("blk", "grp"))
    out_specs = P("blk", "grp")
    return jax.shard_map(shards, mesh=mesh, in_specs=in_specs, out_specs=out_specs, check_vma=False)
```

time: 663 us -> 99 us (0.15)
  the two profiles are of different devices: /device:TPU:8 before, /device:TPU:1 now
where the time goes in v1:
time: 99 us; the launch traced here: 98 us
  starting transfers between devices  42.3 us (43%)
  waiting for transfers between devices  26.4 us (27%)
  blocking collectives  14.9 us (15%)
  Pallas kernels  12.3 us (12%)
  local copies, waits for them, and re-layouts  2.18 us (2%)
    all_to_all x3, starting transfers between devices, exchange(): lax.all_to_all(value, axis, 0, 0, tiled=True, axis_index_groups=groups)  27.7 us
    all_to_all x1, blocking collectives, exchange(): lax.all_to_all(value, axis, 0, 0, tiled=True, axis_index_groups=groups)  14.9 us
    all_to_all x3, waiting for transfers between devices, exchange(): lax.all_to_all(value, axis, 0, 0, tiled=True, axis_index_groups=groups)  12.7 us
    pallas_call x6, Pallas kernels, local_call(): pl.pallas_call(kernel, out_shape=outs, in_specs=[VMEM_SPEC] * len(operand...  12.3 us
    ppermute x1, waiting for transfers between devices, shards(): other_grads = lax.ppermute(output_grads, 'grp', partner)  10.1 us
    ppermute x1, starting transfers between devices, shards(): core_out = lax.ppermute(all_out, 'blk', sibling)  4.24 us
    ppermute x1, starting transfers between devices, shards(): taken = lax.ppermute(give, 'blk', sibling)  3.73 us
    ppermute x1, starting transfers between devices, shards(): other_grads = lax.ppermute(output_grads, 'grp', partner)  3.27 us
  transfers between devices with their start and end apart: 7, of which 4 were waited for; matrix products, arithmetic and copies ran while one was open for 0% of the time, Pallas kernels for 2%

profile of v1, /device:TPU:1, one launch (start us, length us, event | category | flops | bytes accessed | tf_op | source)
XLA Modules:
  0.0 98.0 jit_solution(16494737880100453769)
XLA Ops:
  0.0 0.0 copy-start
  0.0 1.2 %copy-done = bf16[1024,512]{1,0:T(8,128)(2,1)S(1)} copy-done((bf16[1024,512]{1,0:T(8,128)(2,1)S(1)}, bf16[1024,512]{1,0:T(8,128)(2,1)}, u32[]{:S(2)}) %copy-start) | copy-done | bytes 1048600
  1.2 0.0 copy-start.1
  1.2 0.9 copy-done.1
  2.2 1.4 %gram_in.1 = f32[16,72,128]{2,1,0:T(8,128)} custom-call(bf16[1024,512]{1,0:T(8,128)(2,1)S(1)} %copy-done, bf16[512,256]{1,0:T(8,128)(2,1)S(1)} %copy-done.1), custom_call_target="tpu_custom_call" | custom-call | flops 536870912 | bytes 1900544 | tf_op jit(solution)/shard_map/gram_in/pallas_call | solution.py:277
  3.6 0.0 copy-start.2
  3.6 12.1 %all-to-all-start = ((f32[16,72,128]{2,1,0:T(8,128)}), f32[16,72,128]{2,1,0:T(8,128)S(1)}, u32[]{:S(2)}, u32[]{:S(2)}) async-start(f32[16,72,128]{2,1,0:T(8,128)} %gram_in.1), calls=%async_computation | async-start | bytes 1179648 | tf_op jit(solution)/shard_map/all_to_all | solution.py:294
  15.7 0.0 copy-done.2
  15.7 3.3 %collective-permute-start = (bf16[512,256]{1,0:T(8,128)(2,1)S(1)}, bf16[512,256]{1,0:T(8,128)(2,1)S(1)}, u32[]{:S(2)}, u32[]{:S(2)}) collective-permute-start(bf16[512,256]{1,0:T(8,128)(2,1)S(1)} %copy-done.2), channel_id=1, source_target_pairs={{0,32},{32,0},{64,96},{96,64},{128,160},{160,128},{192,224},{224,1... | collective-permute-start | bytes 786440 | tf_op jit(solution)/shard_map/ppermute | solution.py:312
  19.0 10.1 %collective-permute-done.refs_1_ = bf16[512,256]{1,0:T(8,128)(2,1)S(1)} collective-permute-done((bf16[512,256]{1,0:T(8,128)(2,1)S(1)}, bf16[512,256]{1,0:T(8,128)(2,1)S(1)}, u32[]{:S(2)}, u32[]{:S(2)}) %collective-permute-start) | collective-permute-done | bytes 262176 | tf_op jit(solution)/shard_map/ppermute | solution.py:312
  29.1 0.6 gram_out.1
  29.7 3.7 %collective-permute-start.1 = (f32[16,40,128]{2,1,0:T(8,128)S(1)}, f32[16,40,128]{2,1,0:T(8,128)S(1)}, u32[]{:S(2)}, u32[]{:S(2)}) collective-permute-start(f32[16,40,128]{2,1,0:T(8,128)S(1)} %get-tuple-element.13), channel_id=1, source_target_pairs={{0,1},{1,0},{2,3},{3,2},{4,5},{5,4},{6,7},{7,6},{8,9},{9,8},{10,11... | collective-permute-start | bytes 983048 | tf_op jit(solution)/shard_map/ppermute | solution.py:333
  33.4 1.2 %collective-permute-done.1.right_ref = f32[16,40,128]{2,1,0:T(8,128)S(1)} collective-permute-done((f32[16,40,128]{2,1,0:T(8,128)S(1)}, f32[16,40,128]{2,1,0:T(8,128)S(1)}, u32[]{:S(2)}, u32[]{:S(2)}) %collective-permute-start.1) | collective-permute-done | bytes 327712 | tf_op jit(solution)/shard_map/ppermute | solution.py:333
  34.7 0.8 add_cores.1
  35.4 0.0 all-to-all-done.got_ref
  35.4 8.5 %all-to-all-start.2 = ((f32[16,40,128]{2,1,0:T(8,128)}), f32[16,40,128]{2,1,0:T(8,128)S(1)}, u32[]{:S(2)}, u32[]{:S(2)}) async-start(f32[16,40,128]{2,1,0:T(8,128)} %add_cores.1), calls=%async_computation.2 | async-start | bytes 655360 | tf_op jit(solution)/shard_map/all_to_all | solution.py:294
  43.9 0.8 sum_in.1
  44.7 12.7 %all-to-all-done.2.refs_0_ = f32[16,40,128]{2,1,0:T(8,128)S(1)} async-done(((f32[16,40,128]{2,1,0:T(8,128)}), f32[16,40,128]{2,1,0:T(8,128)S(1)}, u32[]{:S(2)}, u32[]{:S(2)}) %all-to-all-start.2) | async-done | bytes 327712 | tf_op jit(solution)/shard_map/all_to_all | solution.py:294
  57.4 0.1 sum_out.1
  57.5 14.9 %all_to_all.20.got_out_ref = bf16[16,48,128]{2,1,0:T(8,128)(2,1)S(1)} all-to-all(bf16[16,48,128]{2,1,0:T(8,128)(2,1)S(1)} %get-tuple-element.15), channel_id=1, replica_groups={{0,2,4,6,8,10,12,14,16,18,20,22,24,26,28,30},{1,3,5,7,9,11,13,15,17,19,..., dimensions={0} | all-to-all | bytes 393216 | tf_op jit(solution)/shard_map/all_to_all | solution.py:294
  72.4 0.0 copy-start.3
  72.4 7.1 %all-to-all-start.1 = ((bf16[16,64,128]{2,1,0:T(8,128)(2,1)}), bf16[16,64,128]{2,1,0:T(8,128)(2,1)S(1)}, u32[]{:S(2)}, u32[]{:S(2)}) async-start(bf16[16,64,128]{2,1,0:T(8,128)(2,1)} %get-tuple-element.11), calls=%async_computation.1 | async-start | bytes 524288 | tf_op jit(solution)/shard_map/all_to_all | solution.py:294
  79.5 0.0 copy-done.3
  79.5 3.3 %collective-permute-start.3 = (bf16[512,256]{1,0:T(8,128)(2,1)S(1)}, bf16[512,256]{1,0:T(8,128)(2,1)S(1)}, u32[]{:S(2)}, u32[]{:S(2)}) collective-permute-start(bf16[512,256]{1,0:T(8,128)(2,1)S(1)} %copy-done.3), channel_id=1, source_target_pairs={{0,32},{32,0},{64,96},{96,64},{128,160},{160,128},{192,224},{224,1... | collective-permute-start | bytes 786440 | tf_op jit(solution)/shard_map/ppermute | solution.py:355
  82.8 4.2 %collective-permute-start.2 = (bf16[16,48,128]{2,1,0:T(8,128)(2,1)S(1)}, bf16[16,48,128]{2,1,0:T(8,128)(2,1)S(1)}, u32[]{:S(2)}, u32[]{:S(2)}) collective-permute-start(bf16[16,48,128]{2,1,0:T(8,128)(2,1)S(1)} %all_to_all.20.got_out_ref), channel_id=1, source_target_pairs={{0,1},{1,0},{2,3},{3,2},{4,5},{5,4},{6,7},{7,6},{8,9},{9,8},{10,11... | collective-permute-start | bytes 589832 | tf_op jit(solution)/shard_map/ppermute | solution.py:354
  87.1 2.3 %collective-permute-done.3.other_weight_ref = bf16[512,256]{1,0:T(8,128)(2,1)S(1)} collective-permute-done((bf16[512,256]{1,0:T(8,128)(2,1)S(1)}, bf16[512,256]{1,0:T(8,128)(2,1)S(1)}, u32[]{:S(2)}, u32[]{:S(2)}) %collective-permute-start.3) | collective-permute-done | bytes 262176 | tf_op jit(solution)/shard_map/ppermute | solution.py:355
  89.4 0.0 all-to-all-done.1.got_in_ref
  89.4 0.0 collective-permute-done.2.core_out_ref
  89.4 8.6 %invert.1 = bf16[512,256]{1,0:T(8,128)(2,1)} custom-call(bf16[16,64,128]{2,1,0:T(8,128)(2,1)S(1)} %all-to-all-done.1.got_in_ref, bf16[16,48,128]{2,1,0:T(8,128)(2,1)S(1)} %all_to_all.20.got_out_ref, bf16[16,48,128]{2,1,0:T(8,128)(2,1)S(1)} %collective-permute-done.2.core_out_ref, f32[8,128]{1,0:T(8,128)S(1)} %get-tuple-element.14.refs_1_.extra_in_ref, ...), custom_call_target="tpu_custom_call" | custom-call | flops 5905580032 | bytes 1449984 | tf_op jit(solution)/shard_map/invert/pallas_call | solution.py:277
Async XLA Ops:
  0.0 1.2 %copy-start = (bf16[1024,512]{1,0:T(8,128)(2,1)S(1)}, bf16[1024,512]{1,0:T(8,128)(2,1)}, u32[]{:S(2)}) copy-start(bf16[1024,512]{1,0:T(8,128)(2,1)} %refs_0_.2) | copy-start | bytes 3145732
  1.2 0.9 copy-start.1
  3.6 12.1 %copy-start.2 = (bf16[512,256]{1,0:T(8,128)(2,1)S(1)}, bf16[512,256]{1,0:T(8,128)(2,1)}, u32[]{:S(2)}) copy-start(bf16[512,256]{1,0:T(8,128)(2,1)} %refs_0_.3) | copy-start | bytes 786436
  3.6 31.8 %all-to-all-start = ((f32[16,72,128]{2,1,0:T(8,128)}), f32[16,72,128]{2,1,0:T(8,128)S(1)}, u32[]{:S(2)}, u32[]{:S(2)}) async-start(f32[16,72,128]{2,1,0:T(8,128)} %gram_in.1), calls=%async_computation | async-start | bytes 1179648 | tf_op jit(solution)/shard_map/all_to_all | solution.py:294
  15.7 13.4 %collective-permute-start = (bf16[512,256]{1,0:T(8,128)(2,1)S(1)}, bf16[512,256]{1,0:T(8,128)(2,1)S(1)}, u32[]{:S(2)}, u32[]{:S(2)}) collective-permute-start(bf16[512,256]{1,0:T(8,128)(2,1)S(1)} %copy-done.2), channel_id=1, source_target_pairs={{0,32},{32,0},{64,96},{96,64},{128,160},{160,128},{192,224},{224,1... | collective-permute-start | bytes 786440 | tf_op jit(solution)/shard_map/ppermute | solution.py:312
  29.7 5.0 %collective-permute-start.1 = (f32[16,40,128]{2,1,0:T(8,128)S(1)}, f32[16,40,128]{2,1,0:T(8,128)S(1)}, u32[]{:S(2)}, u32[]{:S(2)}) collective-permute-start(f32[16,40,128]{2,1,0:T(8,128)S(1)} %get-tuple-element.13), channel_id=1, source_target_pairs={{0,1},{1,0},{2,3},{3,2},{4,5},{5,4},{6,7},{7,6},{8,9},{9,8},{10,11... | collective-permute-start | bytes 983048 | tf_op jit(solution)/shard_map/ppermute | solution.py:333
  35.4 22.0 %all-to-all-start.2 = ((f32[16,40,128]{2,1,0:T(8,128)}), f32[16,40,128]{2,1,0:T(8,128)S(1)}, u32[]{:S(2)}, u32[]{:S(2)}) async-start(f32[16,40,128]{2,1,0:T(8,128)} %add_cores.1), calls=%async_computation.2 | async-start | bytes 655360 | tf_op jit(solution)/shard_map/all_to_all | solution.py:294
  72.4 7.2 %copy-start.3 = (bf16[512,256]{1,0:T(8,128)(2,1)S(1)}, bf16[512,256]{1,0:T(8,128)(2,1)}, u32[]{:S(2)}) copy-start(bf16[512,256]{1,0:T(8,128)(2,1)} %weight_ref.1) | copy-start | bytes 786436
  72.4 17.0 %all-to-all-start.1 = ((bf16[16,64,128]{2,1,0:T(8,128)(2,1)}), bf16[16,64,128]{2,1,0:T(8,128)(2,1)S(1)}, u32[]{:S(2)}, u32[]{:S(2)}) async-start(bf16[16,64,128]{2,1,0:T(8,128)(2,1)} %get-tuple-element.11), calls=%async_computation.1 | async-start | bytes 524288 | tf_op jit(solution)/shard_map/all_to_all | solution.py:294
  79.5 9.9 %collective-permute-start.3 = (bf16[512,256]{1,0:T(8,128)(2,1)S(1)}, bf16[512,256]{1,0:T(8,128)(2,1)S(1)}, u32[]{:S(2)}, u32[]{:S(2)}) collective-permute-start(bf16[512,256]{1,0:T(8,128)(2,1)S(1)} %copy-done.3), channel_id=1, source_target_pairs={{0,32},{32,0},{64,96},{96,64},{128,160},{160,128},{192,224},{224,1... | collective-permute-start | bytes 786440 | tf_op jit(solution)/shard_map/ppermute | solution.py:355
  82.8 6.6 %collective-permute-start.2 = (bf16[16,48,128]{2,1,0:T(8,128)(2,1)S(1)}, bf16[16,48,128]{2,1,0:T(8,128)(2,1)S(1)}, u32[]{:S(2)}, u32[]{:S(2)}) collective-permute-start(bf16[16,48,128]{2,1,0:T(8,128)(2,1)S(1)} %all_to_all.20.got_out_ref), channel_id=1, source_target_pairs={{0,1},{1,0},{2,3},{3,2},{4,5},{5,4},{6,7},{7,6},{8,9},{9,8},{10,11... | collective-permute-start | bytes 589832 | tf_op jit(solution)/shard_map/ppermute | solution.py:354

commit v2 on v1

--- a/solution.py
+++ b/solution.py
@@ -9,6 +9,7 @@
 DAMP_ROOT = 0.1
 TILE = 128
 CORES = 2
+RING = 4
 EXTRA = 8
 EXTRA_HALF = 16
 VMEM_LIMIT = 48 * 1024 * 1024
@@ -64,7 +65,7 @@
     )
 
 
-def unpack_block(packed_ref, diagonal, damping, out_ref):
+def unpack_block(fetch, out_ref):
     count = out_ref.shape[0] // TILE
     off, pairs = tile_plan(count)
     rows, cols = tile_masks()
@@ -72,20 +73,24 @@
     def put(i, j, value):
         out_ref[i * TILE : (i + 1) * TILE, j * TILE : (j + 1) * TILE] = value.astype(jnp.bfloat16)
 
-    def fetch(position):
-        return packed_ref[position * TILE : (position + 1) * TILE, :].astype(jnp.float32)
-
     for position, (i, j) in enumerate(off):
-        value = fetch(position)
+        value = fetch(position).astype(jnp.float32)
         put(i, j, value)
         put(j, i, value.T)
     for position, (i, j) in enumerate(pairs):
-        value = fetch(len(off) + position)
+        value = fetch(len(off) + position).astype(jnp.float32)
         other = value.T
-        damped_i = diagonal[i : i + 1, :] + damping
-        damped_j = diagonal[j : j + 1, :] + damping
-        put(i, i, jnp.where(rows == cols, damped_i, jnp.where(cols > rows, value, other)))
-        put(j, j, jnp.where(rows == cols, damped_j, jnp.where(cols < rows, value, other)))
+        put(i, i, jnp.where(cols > rows, value, other))
+        put(j, j, jnp.where(cols < rows, value, other))
+
+
+def put_diagonal(diagonal, damping, out_ref):
+    rows, cols = tile_masks()
+    for i in range(out_ref.shape[0] // TILE):
+        place = (slice(i * TILE, (i + 1) * TILE),) * 2
+        damped = diagonal[i : i + 1, :] + damping
+        tile = out_ref[place].astype(jnp.float32)
+        out_ref[place] = jnp.where(rows == cols, damped, tile).astype(jnp.bfloat16)
 
 
 def total_of(value):
@@ -127,17 +132,29 @@
     diagonal = packed_gram(data_ref, 1.0 / tokens, store)
     filler = jnp.zeros((EXTRA - diagonal.shape[0], TILE), jnp.float32)
     extra = jnp.concatenate([diagonal, filler], axis=0)
-    pieces, piece_rows = keep_ref.shape[0], keep_ref.shape[1] - EXTRA
-    share = pieces * piece_rows
+    share = keep_ref.shape[0] - EXTRA
     for ref, owner in ((keep_ref, core), (send_ref, 1 - core)):
-        for piece in range(pieces):
-            start = pl.multiple_of(owner * share + piece * piece_rows, piece_rows)
-            ref[piece, :piece_rows, :] = packed_ref[pl.ds(start, piece_rows), :]
-            ref[piece, piece_rows:, :] = extra
-
-
-def add_kernel(left_ref, right_ref, out_ref):
-    out_ref[...] = left_ref[...] + right_ref[...]
+        start = pl.multiple_of(owner * share, share)
+        ref[:share, :] = packed_ref[pl.ds(start, share), :]
+        ref[share:, :] = extra
+
+
+def along_x():
+    return lax.axis_index("blk") // (RING * CORES)
+
+
+def add_cores_kernel(left_ref, right_ref, *out_refs):
+    rows = out_refs[0].shape[0] - EXTRA
+    share = left_ref.shape[0] - EXTRA
+    extra = left_ref[share:, :] + right_ref[share:, :]
+    for step, ref in enumerate(out_refs):
+        place = pl.ds(pl.multiple_of((along_x() ^ step) * rows, rows), rows)
+        ref[:rows, :] = left_ref[place, :] + right_ref[place, :]
+        ref[rows:, :] = extra
+
+
+def sum_ring(refs):
+    return (refs[0][...] + refs[1][...]) + (refs[2][...] + refs[3][...])
 
 
 def sum_pieces(ref):
@@ -147,37 +164,64 @@
     return total
 
 
-def sum_in_kernel(got_ref, send_ref, extra_ref):
+def split_rows(value):
+    high = value.astype(jnp.bfloat16).astype(jnp.float32)
+    rest = value - high
+    middle = rest.astype(jnp.bfloat16).astype(jnp.float32)
+    return [high, middle, rest - middle]
+
+
+def sum_both_kernel(count, got_ref, *refs):
+    *got_refs, send_ref, extra_in_ref, out_ref = refs
     total = sum_pieces(got_ref)
     rows = send_ref.shape[1]
     rounded = total[:rows].astype(jnp.bfloat16)
     for piece in range(send_ref.shape[0]):
         send_ref[piece] = rounded
-    extra_ref[...] = total[rows:]
-
-
-def split_rows(value):
-    high = value.astype(jnp.bfloat16).astype(jnp.float32)
-    rest = value - high
-    middle = rest.astype(jnp.bfloat16).astype(jnp.float32)
-    return [high, middle, rest - middle]
-
-
-def sum_out_kernel(count, got_ref, extra_in_ref, send_ref, extra_ref):
-    total = sum_pieces(got_ref)
-    rows = send_ref.shape[1] - EXTRA_HALF
-    trace_in = jnp.broadcast_to(total_of(extra_in_ref[:count, :]), (1, TILE))
-    energy_out = extra_in_ref[count : count + 1, :]
-    scalars = split_rows(trace_in) + split_rows(energy_out)
+    extra = total[rows:]
+    extra_in_ref[...] = extra
+    total = sum_ring(got_refs)
+    rows = total.shape[0] - EXTRA
+    trace_in = jnp.broadcast_to(total_of(extra[:count]), (1, TILE))
+    energy_out = extra[count : count + 1]
+    filler = jnp.zeros((EXTRA - count - 2, TILE), jnp.float32)
+    out_ref[...] = jnp.concatenate(
+        [total[: rows + count], trace_in, energy_out, filler], axis=0
+    )
+
+
+def sum_y_kernel(count, *refs):
+    *got_refs, piece_ref, extra_ref = refs
+    total = sum_ring(got_refs)
+    rows = total.shape[0] - EXTRA
+    extra = total[rows:]
+    scalars = split_rows(extra[count : count + 1]) + split_rows(extra[count + 1 : count + 2])
     filler = jnp.zeros((EXTRA_HALF - len(scalars), TILE), jnp.float32)
-    block = jnp.concatenate([total[:rows]] + scalars + [filler], axis=0).astype(jnp.bfloat16)
-    for piece in range(send_ref.shape[0]):
-        send_ref[piece] = block
-    extra_ref[...] = total[rows:]
+    piece_ref[...] = jnp.concatenate([total[:rows]] + scalars + [filler], axis=0).astype(
+        jnp.bfloat16
+    )
+    extra_ref[...] = extra
+
+
+def join_kernel(*refs):
+    *got_refs, out_ref = refs
+    for step, ref in enumerate(got_refs):
+        out_ref[along_x() ^ step] = ref[...]
+
+
+def unpack_in_kernel(got_ref, out_ref):
+    rows = got_ref.shape[1]
+    per_tile = TILE // rows
+    unpack_block(
+        lambda position: jnp.concatenate(
+            [got_ref[position * per_tile + part] for part in range(per_tile)], axis=0
+        ),
+        out_ref,
+    )
 
 
 def invert_kernel(
-    got_in_ref,
+    damped_in_ref,
     got_out_ref,
     core_out_ref,
     extra_in_ref,
@@ -186,7 +230,7 @@
     other_weight_ref,
     result_ref,
     packed_ref,
-    damped_in_ref,
+    full_in_ref,
     damped_out_ref,
     iterate_in_ref,
     iterate_out_ref,
@@ -197,20 +241,19 @@
     half = weight_ref.shape[1]
     parity = lax.axis_index("grp") % 2
     core = lax.axis_index("blk") % CORES
-    pieces = got_out_ref.shape[0]
-    piece_rows = got_out_ref.shape[1] - EXTRA_HALF
+    pieces, rows_out = got_out_ref.shape[0], got_out_ref.shape[1] - EXTRA_HALF
     own_column = pl.ds(pl.multiple_of(parity * half, half), half)
     other_column = pl.ds(pl.multiple_of((1 - parity) * half, half), half)
     weight_block_ref[:, own_column] = weight_ref[...]
     weight_block_ref[:, other_column] = other_weight_ref[...]
 
     scalars = jnp.zeros((EXTRA_HALF, TILE), jnp.float32)
-    for ref in (got_out_ref, core_out_ref):
-        for piece in range(pieces):
-            scalars = scalars + ref[piece, piece_rows:, :].astype(jnp.float32)
+    for piece in range(pieces):
+        for ref in (got_out_ref, core_out_ref):
+            scalars = scalars + ref[piece, rows_out:, :].astype(jnp.float32)
     sum_in = scalars[0:1] + scalars[1:2] + scalars[2:3]
     sum_out = scalars[3:4] + scalars[4:5] + scalars[5:6]
-    owners = pieces * CORES
+    owners = lax.axis_size("blk")
     blocks_out = lax.axis_size("grp") // 2
     pi_ratio = jnp.sqrt((sum_in / (owners * width)) / (sum_out / (blocks_out * width)))
     damping_in = DAMP_ROOT * pi_ratio
@@ -220,19 +263,16 @@
     scale_in = 1.0 / (total_of(diagonal_in) + width * damping_in)
     scale_out = 1.0 / (total_of(diagonal_out) + width * damping_out)
 
-    in_rows = got_in_ref.shape[1]
-    for piece in range(got_in_ref.shape[0]):
-        packed_ref[piece * in_rows : (piece + 1) * in_rows, :] = got_in_ref[piece]
-    unpack_block(packed_ref, diagonal_in, damping_in, damped_in_ref)
-    share = pieces * piece_rows
+    full_in_ref[...] = damped_in_ref[...]
+    put_diagonal(diagonal_in, damping_in, full_in_ref)
     for ref, owner in ((got_out_ref, core), (core_out_ref, 1 - core)):
         for piece in range(pieces):
-            start = pl.multiple_of(owner * share + piece * piece_rows, piece_rows)
-            packed_ref[pl.ds(start, piece_rows), :] = ref[piece, :piece_rows, :]
-    unpack_block(packed_ref, diagonal_out, damping_out, damped_out_ref)
+            packed_ref[owner * pieces + piece] = ref[piece, :rows_out, :]
+    unpack_block(lambda position: packed_ref[position], damped_out_ref)
+    put_diagonal(diagonal_out, damping_out, damped_out_ref)
 
     chains = (
-        (damped_in_ref, iterate_in_ref, scale_in),
+        (full_in_ref, iterate_in_ref, scale_in),
         (damped_out_ref, iterate_out_ref, scale_out),
     )
     rows, cols = tile_masks()
@@ -294,22 +334,35 @@
     return lax.all_to_all(value, axis, 0, 0, tiled=True, axis_index_groups=groups)
 
 
+def swap_core(value):
+    pairs = [(place, place ^ 1) for place in range(lax.axis_size("blk"))]
+    return lax.ppermute(value, "blk", pairs)
+
+
+def swap_along(value, stride, step):
+    pairs = [(place, place ^ (stride * step)) for place in range(lax.axis_size("blk"))]
+    return lax.ppermute(value, "blk", pairs)
+
+
+def swap_half(value):
+    pairs = [(place, place ^ 1) for place in range(lax.axis_size("grp"))]
+    return lax.ppermute(value, "grp", pairs)
+
+
 def shards(activations, output_grads, grad_weight):
     groups = lax.axis_size("grp")
-    owners = lax.axis_size("blk")
     width = grad_weight.shape[0]
     half = grad_weight.shape[1]
     count = width // TILE
     packed_rows = width * width // (2 * TILE)
     total_tokens = activations.shape[0] * groups
     in_rows = packed_rows // groups
-    out_pieces = owners // CORES
-    out_rows = packed_rows // owners
-    partner = [(source, source ^ 1) for source in range(groups)]
-    sibling = [(source, source ^ 1) for source in range(owners)]
-    same_core = [[piece * CORES + core for piece in range(out_pieces)] for core in range(CORES)]
-
-    other_grads = lax.ppermute(output_grads, "grp", partner)
+    share_rows = packed_rows // CORES
+    piece_rows = share_rows // RING
+    y_stride, x_stride = CORES, CORES * RING
+    half_type = jnp.bfloat16
+
+    other_grads = swap_half(output_grads)
     send_in = local_call(
         lambda *refs: gram_in_kernel(total_tokens, *refs),
         "gram_in",
@@ -323,50 +376,62 @@
         lambda *refs: gram_out_kernel(total_tokens, *refs),
         "gram_out",
         (output_grads, other_grads),
-        (shape_of(out_pieces, out_rows + EXTRA, TILE),) * 2,
+        (shape_of(share_rows + EXTRA, TILE),) * 2,
         scratch=[
-            pltpu.VMEM((output_grads.shape[0], width), jnp.bfloat16),
+            pltpu.VMEM((output_grads.shape[0], width), half_type),
             pltpu.VMEM((packed_rows, TILE), jnp.float32),
         ],
-        flops=2 * output_grads.shape[0] * width * width,
-    )
-    taken = lax.ppermute(give, "blk", sibling)
-    send_out = local_call(add_kernel, "add_cores", (keep, taken), shape_of(*keep.shape))
-    got_out = exchange(send_out, "blk", same_core)
-
-    all_in, extra_in = local_call(
-        sum_in_kernel,
-        "sum_in",
-        (got_in,),
-        (shape_of(groups, in_rows, TILE, dtype=jnp.bfloat16), shape_of(EXTRA, TILE)),
-    )
-    all_in = exchange(all_in, "grp")
-    all_out, extra_out = local_call(
-        lambda *refs: sum_out_kernel(count, *refs),
-        "sum_out",
-        (got_out, extra_in),
+        flops=200 * output_grads.shape[0] * width * width,
+    )
+    keep, *gives = local_call(
+        add_cores_kernel,
+        "add_cores",
+        (keep, swap_core(give)),
+        (shape_of(piece_rows + EXTRA, TILE),) * RING,
+    )
+    taken = [swap_along(give, x_stride, step + 1) for step, give in enumerate(gives)]
+    to_all_in, extra_in, part_y = local_call(
+        lambda *refs: sum_both_kernel(count, *refs),
+        "sum_both",
+        (got_in, keep, *taken),
         (
-            shape_of(out_pieces, out_rows + EXTRA_HALF, TILE, dtype=jnp.bfloat16),
+            shape_of(groups, in_rows, TILE, dtype=half_type),
             shape_of(EXTRA, TILE),
+            shape_of(piece_rows + EXTRA, TILE),
         ),
     )
-    all_out = exchange(all_out, "blk", same_core)
-    core_out = lax.ppermute(all_out, "blk", sibling)
-    other_weight = lax.ppermute(grad_weight, "grp", partner)
+    all_in = exchange(to_all_in, "grp")
+    taken = [swap_along(part_y, y_stride, step) for step in range(1, RING)]
+    piece, extra_out = local_call(
+        lambda *refs: sum_y_kernel(count, *refs),
+        "sum_y",
+        (part_y, *taken),
+        (shape_of(piece_rows + EXTRA_HALF, TILE, dtype=half_type), shape_of(EXTRA, TILE)),
+    )
+    taken = [swap_along(piece, x_stride, step) for step in range(1, RING)]
+    all_out = local_call(
+        join_kernel,
+        "join_x",
+        (piece, *taken),
+        shape_of(RING, piece_rows + EXTRA_HALF, TILE, dtype=half_type),
+    )
+    core_out = swap_core(all_out)
+    other_weight = swap_half(grad_weight)
 
     block = (width, width)
+    damped_in = local_call(unpack_in_kernel, "unpack_in", (all_in,), shape_of(*block, dtype=half_type))
     return local_call(
         invert_kernel,
         "invert",
-        (all_in, all_out, core_out, extra_in, extra_out, grad_weight, other_weight),
-        shape_of(width, half, dtype=jnp.bfloat16),
+        (damped_in, all_out, core_out, extra_in, extra_out, grad_weight, other_weight),
+        shape_of(width, half, dtype=half_type),
         scratch=[
-            pltpu.VMEM((packed_rows, TILE), jnp.bfloat16),
-            pltpu.VMEM(block, jnp.bfloat16),
-            pltpu.VMEM(block, jnp.bfloat16),
+            pltpu.VMEM((CORES * RING, piece_rows, TILE), half_type),
+            pltpu.VMEM(block, half_type),
+            pltpu.VMEM(block, half_type),
             pltpu.VMEM(block, jnp.float32),
             pltpu.VMEM(block, jnp.float32),
-            pltpu.VMEM(block, jnp.bfloat16),
+            pltpu.VMEM(block, half_type),
         ],
         flops=2 * (4 * (ITERS - 1) + 2) * width * width * width,
     )

time: 99 us -> 95.3 us (0.963)
  starting transfers between devices: 42.3 us -> 66.9 us
  blocking collectives: 14.9 us -> 0 us
  waiting for transfers between devices: 26.4 us -> 13.8 us
    ppermute x4 -> x13, starting transfers between devices: 14.5 us -> 48.7 us  [the longest x9 30.8 us: swap_along(): return lax.ppermute(value, 'blk', pairs)]
    all_to_all x1 -> x0, blocking collectives: 14.9 us -> none  [exchange(): lax.all_to_all(value, axis, 0, 0, tiled=True, axis_index_groups=groups)]
    all_to_all x3 -> x2, waiting for transfers between devices: 12.7 us -> 0.01 us  [exchange(): lax.all_to_all(value, axis, 0, 0, tiled=True, axis_index_groups=groups)]
    all_to_all x3 -> x2, starting transfers between devices: 27.7 us -> 18.1 us  [exchange(): lax.all_to_all(value, axis, 0, 0, tiled=True, axis_index_groups=groups)]
    pallas_call x6 -> x8, Pallas kernels: 12.3 us -> 11.6 us  [local_call(): pl.pallas_call(kernel, out_shape=outs, in_specs=[VMEM_SPEC] * len(operand...]
    ppermute x4 -> x13, waiting for transfers between devices: 13.7 us -> 13.8 us  [the longest x9 11.8 us: swap_along(): return lax.ppermute(value, 'blk', pairs)]
  transfers between devices with their start and end apart: 7 -> 15, of which waited for: 4 -> 7; matrix products, arithmetic and copies ran while one was open for 0% -> 0% of each run, Pallas kernels for 2% -> 2%
where the time goes in v2:
time: 95.3 us; the launch traced here: 94.6 us
  starting transfers between devices  66.9 us (70%)
  waiting for transfers between devices  13.8 us (14%)
  Pallas kernels  11.6 us (12%)
  local copies, waits for them, and re-layouts  2.17 us (2%)
    ppermute x9, starting transfers between devices, swap_along(): return lax.ppermute(value, 'blk', pairs)  30.8 us
    all_to_all x2, starting transfers between devices, exchange(): lax.all_to_all(value, axis, 0, 0, tiled=True, axis_index_groups=groups)  18.1 us
    ppermute x9, waiting for transfers between devices, swap_along(): return lax.ppermute(value, 'blk', pairs)  11.8 us
    pallas_call x8, Pallas kernels, local_call(): pl.pallas_call(kernel, out_shape=outs, in_specs=[VMEM_SPEC] * len(operand...  11.6 us
    ppermute x2, starting transfers between devices, swap_core(): return lax.ppermute(value, 'blk', pairs)  10.6 us
    ppermute x2, starting transfers between devices, swap_half(): return lax.ppermute(value, 'grp', pairs)  7.29 us
    unnamed x8, local copies, waits for them, and re-layouts  2.17 us
    ppermute x2, waiting for transfers between devices, swap_core(): return lax.ppermute(value, 'blk', pairs)  1.96 us
  transfers between devices with their start and end apart: 15, of which 7 were waited for; matrix products, arithmetic and copies ran while one was open for 0% of the time, Pallas kernels for 2%

profile of v2, /device:TPU:1, one launch (start us, length us, event | category | flops | bytes accessed | tf_op | source)
XLA Modules:
  0.0 94.6 jit_solution(15442987192519051956)
XLA Ops:
  0.0 4.0 %collective-permute-start = (bf16[512,256]{1,0:T(8,128)(2,1)}, bf16[512,256]{1,0:T(8,128)(2,1)S(1)}, u32[]{:S(2)}, u32[]{:S(2)}) collective-permute-start(bf16[512,256]{1,0:T(8,128)(2,1)} %refs_0_.3), channel_id=1, source_target_pairs={{0,32},{32,0},{64,96},{96,64},{128,160},{160,128},{192,224},{224,1... | collective-permute-start | bytes 786440 | tf_op jit(solution)/shard_map/ppermute | solution.py:349
  4.0 0.0 copy-start
  4.0 1.2 %copy-done = bf16[1024,512]{1,0:T(8,128)(2,1)S(1)} copy-done((bf16[1024,512]{1,0:T(8,128)(2,1)S(1)}, bf16[1024,512]{1,0:T(8,128)(2,1)}, u32[]{:S(2)}) %copy-start) | copy-done | bytes 1048600
  5.3 0.0 copy-start.1
  5.3 0.9 %copy-done.1 = bf16[512,256]{1,0:T(8,128)(2,1)S(1)} copy-done((bf16[512,256]{1,0:T(8,128)(2,1)S(1)}, bf16[512,256]{1,0:T(8,128)(2,1)}, u32[]{:S(2)}) %copy-start.1) | copy-done | bytes 262168
  6.2 1.4 %gram_in.1 = f32[16,72,128]{2,1,0:T(8,128)} custom-call(bf16[1024,512]{1,0:T(8,128)(2,1)S(1)} %copy-done, bf16[512,256]{1,0:T(8,128)(2,1)S(1)} %copy-done.1), custom_call_target="tpu_custom_call" | custom-call | flops 536870912 | bytes 1900544 | tf_op jit(solution)/shard_map/gram_in/pallas_call | solution.py:317
  7.6 0.0 copy-start.2
  7.6 10.3 %all-to-all-start = ((f32[16,72,128]{2,1,0:T(8,128)}), f32[16,72,128]{2,1,0:T(8,128)S(1)}, u32[]{:S(2)}, u32[]{:S(2)}) async-start(f32[16,72,128]{2,1,0:T(8,128)} %gram_in.1), calls=%async_computation | async-start | bytes 1179648 | tf_op jit(solution)/shard_map/all_to_all | solution.py:334
  17.9 0.0 collective-permute-done.refs_1_
  17.9 0.0 copy-done.2
  18.0 0.6 gram_out.1
  18.5 3.1 %collective-permute-start.1 = (f32[520,128]{1,0:T(8,128)S(1)}, f32[520,128]{1,0:T(8,128)S(1)}, u32[]{:S(2)}, u32[]{:S(2)}) collective-permute-start(f32[520,128]{1,0:T(8,128)S(1)} %get-tuple-element.17), channel_id=1, source_target_pairs={{0,1},{1,0},{2,3},{3,2},{4,5},{5,4},{6,7},{7,6},{8,9},{9,8},{10,11... | collective-permute-start | bytes 798728 | tf_op jit(solution)/shard_map/ppermute | solution.py:339
  21.7 1.1 %collective-permute-done.1.right_ref = f32[520,128]{1,0:T(8,128)S(1)} collective-permute-done((f32[520,128]{1,0:T(8,128)S(1)}, f32[520,128]{1,0:T(8,128)S(1)}, u32[]{:S(2)}, u32[]{:S(2)}) %collective-permute-start.1) | collective-permute-done | bytes 266272 | tf_op jit(solution)/shard_map/ppermute | solution.py:339
  22.9 3.1 %collective-permute-start.2 = (f32[136,128]{1,0:T(8,128)S(1)}, f32[136,128]{1,0:T(8,128)S(1)}, u32[]{:S(2)}, u32[]{:S(2)}) collective-permute-start(f32[136,128]{1,0:T(8,128)S(1)} %get-tuple-element.19), channel_id=1, source_target_pairs={{0,8},{1,9},{2,10},{3,11},{4,12},{5,13},{6,14},{7,15},{8,0},{9,1},... | collective-permute-start | bytes 208904 | tf_op jit(solution)/shard_map/ppermute | solution.py:344
  26.0 4.4 %collective-permute-start.3 = (f32[136,128]{1,0:T(8,128)S(1)}, f32[136,128]{1,0:T(8,128)S(1)}, u32[]{:S(2)}, u32[]{:S(2)}) collective-permute-start(f32[136,128]{1,0:T(8,128)S(1)} %get-tuple-element.20), channel_id=1, source_target_pairs={{0,16},{1,17},{2,18},{3,19},{4,20},{5,21},{6,22},{7,23},{8,24},{9,... | collective-permute-start | bytes 208904 | tf_op jit(solution)/shard_map/ppermute | solution.py:344
  30.4 2.1 %collective-permute-start.4 = (f32[136,128]{1,0:T(8,128)S(1)}, f32[136,128]{1,0:T(8,128)S(1)}, u32[]{:S(2)}, u32[]{:S(2)}) collective-permute-start(f32[136,128]{1,0:T(8,128)S(1)} %get-tuple-element.21), channel_id=1, source_target_pairs={{0,24},{1,25},{2,26},{3,27},{4,28},{5,29},{6,30},{7,31},{8,16},{9,... | collective-permute-start | bytes 208904 | tf_op jit(solution)/shard_map/ppermute | solution.py:344
  32.5 0.0 collective-permute-done.2.refs_2_
  32.5 0.2 collective-permute-done.3.refs_3_
  32.7 4.1 %collective-permute-done.4.refs_4_ = f32[136,128]{1,0:T(8,128)S(1)} collective-permute-done((f32[136,128]{1,0:T(8,128)S(1)}, f32[136,128]{1,0:T(8,128)S(1)}, u32[]{:S(2)}, u32[]{:S(2)}) %collective-permute-start.4) | collective-permute-done | bytes 69664 | tf_op jit(solution)/shard_map/ppermute | solution.py:344
  36.8 0.0 all-to-all-done.refs_0_
  36.8 0.8 sum_both.1
  37.5 0.0 copy-start.3
  37.5 7.8 %all-to-all-start.1 = ((bf16[16,64,128]{2,1,0:T(8,128)(2,1)}), bf16[16,64,128]{2,1,0:T(8,128)(2,1)S(1)}, u32[]{:S(2)}, u32[]{:S(2)}) async-start(bf16[16,64,128]{2,1,0:T(8,128)(2,1)} %get-tuple-element.22), calls=%async_computation.1 | async-start | bytes 524288 | tf_op jit(solution)/shard_map/all_to_all | solution.py:334
  45.4 0.0 copy-done.3
  45.4 3.3 %collective-permute-start.12 = (bf16[512,256]{1,0:T(8,128)(2,1)S(1)}, bf16[512,256]{1,0:T(8,128)(2,1)S(1)}, u32[]{:S(2)}, u32[]{:S(2)}) collective-permute-start(bf16[512,256]{1,0:T(8,128)(2,1)S(1)} %copy-done.3), channel_id=1, source_target_pairs={{0,32},{32,0},{64,96},{96,64},{128,160},{160,128},{192,224},{224,1... | collective-permute-start | bytes 786440 | tf_op jit(solution)/shard_map/ppermute | solution.py:349
  48.7 4.2 %collective-permute-start.5 = (f32[136,128]{1,0:T(8,128)S(1)}, f32[136,128]{1,0:T(8,128)S(1)}, u32[]{:S(2)}, u32[]{:S(2)}) collective-permute-start(f32[136,128]{1,0:T(8,128)S(1)} %get-tuple-element.23.refs_0_), channel_id=1, source_target_pairs={{0,2},{1,3},{2,0},{3,1},{4,6},{5,7},{6,4},{7,5},{8,10},{9,11},{10,... | collective-permute-start | bytes 208904 | tf_op jit(solution)/shard_map/ppermute | solution.py:344
  52.9 5.5 %collective-permute-start.6 = (f32[136,128]{1,0:T(8,128)S(1)}, f32[136,128]{1,0:T(8,128)S(1)}, u32[]{:S(2)}, u32[]{:S(2)}) collective-permute-start(f32[136,128]{1,0:T(8,128)S(1)} %get-tuple-element.23.refs_0_), channel_id=1, source_target_pairs={{0,4},{1,5},{2,6},{3,7},{4,0},{5,1},{6,2},{7,3},{8,12},{9,13},{10,... | collective-permute-start | bytes 208904 | tf_op jit(solution)/shard_map/ppermute | solution.py:344
  58.4 1.9 %collective-permute-start.7 = (f32[136,128]{1,0:T(8,128)S(1)}, f32[136,128]{1,0:T(8,128)S(1)}, u32[]{:S(2)}, u32[]{:S(2)}) collective-permute-start(f32[136,128]{1,0:T(8,128)S(1)} %get-tuple-element.23.refs_0_), channel_id=1, source_target_pairs={{0,6},{1,7},{2,4},{3,5},{4,2},{5,3},{6,0},{7,1},{8,14},{9,15},{10,... | collective-permute-start | bytes 208904 | tf_op jit(solution)/shard_map/ppermute | solution.py:344
  60.4 0.0 collective-permute-done.5.refs_1_
  60.4 2.3 %collective-permute-done.6.refs_2_ = f32[136,128]{1,0:T(8,128)S(1)} collective-permute-done((f32[136,128]{1,0:T(8,128)S(1)}, f32[136,128]{1,0:T(8,128)S(1)}, u32[]{:S(2)}, u32[]{:S(2)}) %collective-permute-start.6) | collective-permute-done | bytes 69664 | tf_op jit(solution)/shard_map/ppermute | solution.py:344
  62.7 3.7 %collective-permute-done.7.refs_3_ = f32[136,128]{1,0:T(8,128)S(1)} collective-permute-done((f32[136,128]{1,0:T(8,128)S(1)}, f32[136,128]{1,0:T(8,128)S(1)}, u32[]{:S(2)}, u32[]{:S(2)}) %collective-permute-start.7) | collective-permute-done | bytes 69664 | tf_op jit(solution)/shard_map/ppermute | solution.py:344
  66.4 1.9 %collective-permute-start.8 = (bf16[144,128]{1,0:T(8,128)(2,1)S(1)}, bf16[144,128]{1,0:T(8,128)(2,1)S(1)}, u32[]{:S(2)}, u32[]{:S(2)}) collective-permute-start(bf16[144,128]{1,0:T(8,128)(2,1)S(1)} %get-tuple-element.24.refs_0_), channel_id=1, source_target_pairs={{0,8},{1,9},{2,10},{3,11},{4,12},{5,13},{6,14},{7,15},{8,0},{9,1},... | collective-permute-start | bytes 110600 | tf_op jit(solution)/shard_map/ppermute | solution.py:344
  68.3 3.3 %collective-permute-start.9 = (bf16[144,128]{1,0:T(8,128)(2,1)S(1)}, bf16[144,128]{1,0:T(8,128)(2,1)S(1)}, u32[]{:S(2)}, u32[]{:S(2)}) collective-permute-start(bf16[144,128]{1,0:T(8,128)(2,1)S(1)} %get-tuple-element.24.refs_0_), channel_id=1, source_target_pairs={{0,16},{1,17},{2,18},{3,19},{4,20},{5,21},{6,22},{7,23},{8,24},{9,... | collective-permute-start | bytes 110600 | tf_op jit(solution)/shard_map/ppermute | solution.py:344
  71.6 4.3 %collective-permute-start.10 = (bf16[144,128]{1,0:T(8,128)(2,1)S(1)}, bf16[144,128]{1,0:T(8,128)(2,1)S(1)}, u32[]{:S(2)}, u32[]{:S(2)}) collective-permute-start(bf16[144,128]{1,0:T(8,128)(2,1)S(1)} %get-tuple-element.24.refs_0_), channel_id=1, source_target_pairs={{0,24},{1,25},{2,26},{3,27},{4,28},{5,29},{6,30},{7,31},{8,16},{9,... | collective-permute-start | bytes 110600 | tf_op jit(solution)/shard_map/ppermute | solution.py:344
  76.0 0.0 collective-permute-done.8.refs_1_
  76.0 0.0 collective-permute-done.9.refs_2_
  76.0 1.5 %collective-permute-done.10.refs_3_ = bf16[144,128]{1,0:T(8,128)(2,1)S(1)} collective-permute-done((bf16[144,128]{1,0:T(8,128)(2,1)S(1)}, bf16[144,128]{1,0:T(8,128)(2,1)S(1)}, u32[]{:S(2)}, u32[]{:S(2)}) %collective-permute-start.10) | collective-permute-done | bytes 36896 | tf_op jit(solution)/shard_map/ppermute | solution.py:344
  77.6 7.4 %collective-permute-start.11 = (bf16[4,144,128]{2,1,0:T(8,128)(2,1)S(1)}, bf16[4,144,128]{2,1,0:T(8,128)(2,1)S(1)}, u32[]{:S(2)}, u32[]{:S(2)}) collective-permute-start(bf16[4,144,128]{2,1,0:T(8,128)(2,1)S(1)} %join_x.1.got_out_ref), channel_id=1, source_target_pairs={{0,1},{1,0},{2,3},{3,2},{4,5},{5,4},{6,7},{7,6},{8,9},{9,8},{10,11... | collective-permute-start | bytes 442376 | tf_op jit(solution)/shard_map/ppermute | solution.py:339
  85.0 0.0 all-to-all-done.1.got_ref
  85.0 0.1 unpack_in.1.damped_in_ref
  85.2 0.0 collective-permute-done.12.other_weight_ref
  85.2 0.8 collective-permute-done.11.core_out_ref
  86.0 8.5 %invert.1 = bf16[512,256]{1,0:T(8,128)(2,1)} custom-call(bf16[512,512]{1,0:T(8,128)(2,1)S(1)} %unpack_in.1.damped_in_ref, bf16[4,144,128]{2,1,0:T(8,128)(2,1)S(1)} %join_x.1.got_out_ref, bf16[4,144,128]{2,1,0:T(8,128)(2,1)S(1)} %collective-permute-done.11.core_out_ref, f32[8,128]{1,0:T(8,128)S(1)} %get-tuple-element.25.extra_in_ref, ...), custom_call_target="tpu_custom_call" | custom-call | flops 5905580032 | bytes 1613824 | tf_op jit(solution)/shard_map/invert/pallas_call | solution.py:317
  (3 shorter events, 0.1 us)
Async XLA Ops:
  0.0 17.9 %collective-permute-start = (bf16[512,256]{1,0:T(8,128)(2,1)}, bf16[512,256]{1,0:T(8,128)(2,1)S(1)}, u32[]{:S(2)}, u32[]{:S(2)}) collective-permute-start(bf16[512,256]{1,0:T(8,128)(2,1)} %refs_0_.3), channel_id=1, source_target_pairs={{0,32},{32,0},{64,96},{96,64},{128,160},{160,128},{192,224},{224,1... | collective-permute-start | bytes 786440 | tf_op jit(solution)/shard_map/ppermute | solution.py:349
  4.0 1.2 %copy-start = (bf16[1024,512]{1,0:T(8,128)(2,1)S(1)}, bf16[1024,512]{1,0:T(8,128)(2,1)}, u32[]{:S(2)}) copy-start(bf16[1024,512]{1,0:T(8,128)(2,1)} %refs_0_.2) | copy-start | bytes 3145732
  5.3 0.9 %copy-start.1 = (bf16[512,256]{1,0:T(8,128)(2,1)S(1)}, bf16[512,256]{1,0:T(8,128)(2,1)}, u32[]{:S(2)}) copy-start(bf16[512,256]{1,0:T(8,128)(2,1)} %refs_0_.3) | copy-start | bytes 786436
  7.6 10.3 %copy-start.2 = (bf16[512,256]{1,0:T(8,128)(2,1)S(1)}, bf16[512,256]{1,0:T(8,128)(2,1)}, u32[]{:S(2)}) copy-start(bf16[512,256]{1,0:T(8,128)(2,1)} %refs_0_.3) | copy-start | bytes 786436
  7.6 29.1 %all-to-all-start = ((f32[16,72,128]{2,1,0:T(8,128)}), f32[16,72,128]{2,1,0:T(8,128)S(1)}, u32[]{:S(2)}, u32[]{:S(2)}) async-start(f32[16,72,128]{2,1,0:T(8,128)} %gram_in.1), calls=%async_computation | async-start | bytes 1179648 | tf_op jit(solution)/shard_map/all_to_all | solution.py:334
  18.5 4.3 %collective-permute-start.1 = (f32[520,128]{1,0:T(8,128)S(1)}, f32[520,128]{1,0:T(8,128)S(1)}, u32[]{:S(2)}, u32[]{:S(2)}) collective-permute-start(f32[520,128]{1,0:T(8,128)S(1)} %get-tuple-element.17), channel_id=1, source_target_pairs={{0,1},{1,0},{2,3},{3,2},{4,5},{5,4},{6,7},{7,6},{8,9},{9,8},{10,11... | collective-permute-start | bytes 798728 | tf_op jit(solution)/shard_map/ppermute | solution.py:339
  22.9 9.6 %collective-permute-start.2 = (f32[136,128]{1,0:T(8,128)S(1)}, f32[136,128]{1,0:T(8,128)S(1)}, u32[]{:S(2)}, u32[]{:S(2)}) collective-permute-start(f32[136,128]{1,0:T(8,128)S(1)} %get-tuple-element.19), channel_id=1, source_target_pairs={{0,8},{1,9},{2,10},{3,11},{4,12},{5,13},{6,14},{7,15},{8,0},{9,1},... | collective-permute-start | bytes 208904 | tf_op jit(solution)/shard_map/ppermute | solution.py:344
  26.0 6.7 %collective-permute-start.3 = (f32[136,128]{1,0:T(8,128)S(1)}, f32[136,128]{1,0:T(8,128)S(1)}, u32[]{:S(2)}, u32[]{:S(2)}) collective-permute-start(f32[136,128]{1,0:T(8,128)S(1)} %get-tuple-element.20), channel_id=1, source_target_pairs={{0,16},{1,17},{2,18},{3,19},{4,20},{5,21},{6,22},{7,23},{8,24},{9,... | collective-permute-start | bytes 208904 | tf_op jit(solution)/shard_map/ppermute | solution.py:344
  30.4 6.4 %collective-permute-start.4 = (f32[136,128]{1,0:T(8,128)S(1)}, f32[136,128]{1,0:T(8,128)S(1)}, u32[]{:S(2)}, u32[]{:S(2)}) collective-permute-start(f32[136,128]{1,0:T(8,128)S(1)} %get-tuple-element.21), channel_id=1, source_target_pairs={{0,24},{1,25},{2,26},{3,27},{4,28},{5,29},{6,30},{7,31},{8,16},{9,... | collective-permute-start | bytes 208904 | tf_op jit(solution)/shard_map/ppermute | solution.py:344
  37.5 7.9 %copy-start.3 = (bf16[512,256]{1,0:T(8,128)(2,1)S(1)}, bf16[512,256]{1,0:T(8,128)(2,1)}, u32[]{:S(2)}) copy-start(bf16[512,256]{1,0:T(8,128)(2,1)} %weight_ref.1) | copy-start | bytes 786436
  37.5 47.5 %all-to-all-start.1 = ((bf16[16,64,128]{2,1,0:T(8,128)(2,1)}), bf16[16,64,128]{2,1,0:T(8,128)(2,1)S(1)}, u32[]{:S(2)}, u32[]{:S(2)}) async-start(bf16[16,64,128]{2,1,0:T(8,128)(2,1)} %get-tuple-element.22), calls=%async_computation.1 | async-start | bytes 524288 | tf_op jit(solution)/shard_map/all_to_all | solution.py:334
  45.4 39.8 %collective-permute-start.12 = (bf16[512,256]{1,0:T(8,128)(2,1)S(1)}, bf16[512,256]{1,0:T(8,128)(2,1)S(1)}, u32[]{:S(2)}, u32[]{:S(2)}) collective-permute-start(bf16[512,256]{1,0:T(8,128)(2,1)S(1)} %copy-done.3), channel_id=1, source_target_pairs={{0,32},{32,0},{64,96},{96,64},{128,160},{160,128},{192,224},{224,1... | collective-permute-start | bytes 786440 | tf_op jit(solution)/shard_map/ppermute | solution.py:349
  48.7 11.7 %collective-permute-start.5 = (f32[136,128]{1,0:T(8,128)S(1)}, f32[136,128]{1,0:T(8,128)S(1)}, u32[]{:S(2)}, u32[]{:S(2)}) collective-permute-start(f32[136,128]{1,0:T(8,128)S(1)} %get-tuple-element.23.refs_0_), channel_id=1, source_target_pairs={{0,2},{1,3},{2,0},{3,1},{4,6},{5,7},{6,4},{7,5},{8,10},{9,11},{10,... | collective-permute-start | bytes 208904 | tf_op jit(solution)/shard_map/ppermute | solution.py:344
  52.9 9.8 %collective-permute-start.6 = (f32[136,128]{1,0:T(8,128)S(1)}, f32[136,128]{1,0:T(8,128)S(1)}, u32[]{:S(2)}, u32[]{:S(2)}) collective-permute-start(f32[136,128]{1,0:T(8,128)S(1)} %get-tuple-element.23.refs_0_), channel_id=1, source_target_pairs={{0,4},{1,5},{2,6},{3,7},{4,0},{5,1},{6,2},{7,3},{8,12},{9,13},{10,... | collective-permute-start | bytes 208904 | tf_op jit(solution)/shard_map/ppermute | solution.py:344
  58.4 7.9 %collective-permute-start.7 = (f32[136,128]{1,0:T(8,128)S(1)}, f32[136,128]{1,0:T(8,128)S(1)}, u32[]{:S(2)}, u32[]{:S(2)}) collective-permute-start(f32[136,128]{1,0:T(8,128)S(1)} %get-tuple-element.23.refs_0_), channel_id=1, source_target_pairs={{0,6},{1,7},{2,4},{3,5},{4,2},{5,3},{6,0},{7,1},{8,14},{9,15},{10,... | collective-permute-start | bytes 208904 | tf_op jit(solution)/shard_map/ppermute | solution.py:344
  66.4 9.6 %collective-permute-start.8 = (bf16[144,128]{1,0:T(8,128)(2,1)S(1)}, bf16[144,128]{1,0:T(8,128)(2,1)S(1)}, u32[]{:S(2)}, u32[]{:S(2)}) collective-permute-start(bf16[144,128]{1,0:T(8,128)(2,1)S(1)} %get-tuple-element.24.refs_0_), channel_id=1, source_target_pairs={{0,8},{1,9},{2,10},{3,11},{4,12},{5,13},{6,14},{7,15},{8,0},{9,1},... | collective-permute-start | bytes 110600 | tf_op jit(solution)/shard_map/ppermute | solution.py:344
  68.3 7.7 %collective-permute-start.9 = (bf16[144,128]{1,0:T(8,128)(2,1)S(1)}, bf16[144,128]{1,0:T(8,128)(2,1)S(1)}, u32[]{:S(2)}, u32[]{:S(2)}) collective-permute-start(bf16[144,128]{1,0:T(8,128)(2,1)S(1)} %get-tuple-element.24.refs_0_), channel_id=1, source_target_pairs={{0,16},{1,17},{2,18},{3,19},{4,20},{5,21},{6,22},{7,23},{8,24},{9,... | collective-permute-start | bytes 110600 | tf_op jit(solution)/shard_map/ppermute | solution.py:344
  71.6 5.9 %collective-permute-start.10 = (bf16[144,128]{1,0:T(8,128)(2,1)S(1)}, bf16[144,128]{1,0:T(8,128)(2,1)S(1)}, u32[]{:S(2)}, u32[]{:S(2)}) collective-permute-start(bf16[144,128]{1,0:T(8,128)(2,1)S(1)} %get-tuple-element.24.refs_0_), channel_id=1, source_target_pairs={{0,24},{1,25},{2,26},{3,27},{4,28},{5,29},{6,30},{7,31},{8,16},{9,... | collective-permute-start | bytes 110600 | tf_op jit(solution)/shard_map/ppermute | solution.py:344
  77.6 8.4 %collective-permute-start.11 = (bf16[4,144,128]{2,1,0:T(8,128)(2,1)S(1)}, bf16[4,144,128]{2,1,0:T(8,128)(2,1)S(1)}, u32[]{:S(2)}, u32[]{:S(2)}) collective-permute-start(bf16[4,144,128]{2,1,0:T(8,128)(2,1)S(1)} %join_x.1.got_out_ref), channel_id=1, source_target_pairs={{0,1},{1,0},{2,3},{3,2},{4,5},{5,4},{6,7},{7,6},{8,9},{9,8},{10,11... | collective-permute-start | bytes 442376 | tf_op jit(solution)/shard_map/ppermute | solution.py:339

commit v3 on v2

--- a/solution.py
+++ b/solution.py
@@ -12,6 +12,7 @@
 RING = 4
 EXTRA = 8
 EXTRA_HALF = 16
+LATE_START = 10**10
 VMEM_LIMIT = 48 * 1024 * 1024
 
 
@@ -191,22 +192,16 @@
 
 
 def sum_y_kernel(count, *refs):
-    *got_refs, piece_ref, extra_ref = refs
+    *got_refs, send_ref, extra_ref = refs
     total = sum_ring(got_refs)
     rows = total.shape[0] - EXTRA
     extra = total[rows:]
     scalars = split_rows(extra[count : count + 1]) + split_rows(extra[count + 1 : count + 2])
     filler = jnp.zeros((EXTRA_HALF - len(scalars), TILE), jnp.float32)
-    piece_ref[...] = jnp.concatenate([total[:rows]] + scalars + [filler], axis=0).astype(
-        jnp.bfloat16
-    )
+    block = jnp.concatenate([total[:rows]] + scalars + [filler], axis=0).astype(jnp.bfloat16)
+    for piece in range(send_ref.shape[0]):
+        send_ref[piece] = block
     extra_ref[...] = extra
-
-
-def join_kernel(*refs):
-    *got_refs, out_ref = refs
-    for step, ref in enumerate(got_refs):
-        out_ref[along_x() ^ step] = ref[...]
 
 
 def unpack_in_kernel(got_ref, out_ref):
@@ -223,13 +218,11 @@
 def invert_kernel(
     damped_in_ref,
     got_out_ref,
-    core_out_ref,
     extra_in_ref,
     extra_out_ref,
     weight_ref,
     other_weight_ref,
     result_ref,
-    packed_ref,
     full_in_ref,
     damped_out_ref,
     iterate_in_ref,
@@ -240,7 +233,6 @@
     count = width // TILE
     half = weight_ref.shape[1]
     parity = lax.axis_index("grp") % 2
-    core = lax.axis_index("blk") % CORES
     pieces, rows_out = got_out_ref.shape[0], got_out_ref.shape[1] - EXTRA_HALF
     own_column = pl.ds(pl.multiple_of(parity * half, half), half)
     other_column = pl.ds(pl.multiple_of((1 - parity) * half, half), half)
@@ -249,8 +241,7 @@
 
     scalars = jnp.zeros((EXTRA_HALF, TILE), jnp.float32)
     for piece in range(pieces):
-        for ref in (got_out_ref, core_out_ref):
-            scalars = scalars + ref[piece, rows_out:, :].astype(jnp.float32)
+        scalars = scalars + got_out_ref[piece, rows_out:, :].astype(jnp.float32)
     sum_in = scalars[0:1] + scalars[1:2] + scalars[2:3]
     sum_out = scalars[3:4] + scalars[4:5] + scalars[5:6]
     owners = lax.axis_size("blk")
@@ -265,10 +256,12 @@
 
     full_in_ref[...] = damped_in_ref[...]
     put_diagonal(diagonal_in, damping_in, full_in_ref)
-    for ref, owner in ((got_out_ref, core), (core_out_ref, 1 - core)):
-        for piece in range(pieces):
-            packed_ref[owner * pieces + piece] = ref[piece, :rows_out, :]
-    unpack_block(lambda position: packed_ref[position], damped_out_ref)
+    unpack_block(
+        lambda position: got_out_ref[
+            position % RING * CORES + position // RING, :rows_out, :
+        ],
+        damped_out_ref,
+    )
     put_diagonal(diagonal_out, damping_out, damped_out_ref)
 
     chains = (
@@ -381,7 +374,7 @@
             pltpu.VMEM((output_grads.shape[0], width), half_type),
             pltpu.VMEM((packed_rows, TILE), jnp.float32),
         ],
-        flops=200 * output_grads.shape[0] * width * width,
+        flops=LATE_START * 3,
     )
     keep, *gives = local_call(
         add_cores_kernel,
@@ -390,6 +383,8 @@
         (shape_of(piece_rows + EXTRA, TILE),) * RING,
     )
     taken = [swap_along(give, x_stride, step + 1) for step, give in enumerate(gives)]
+    other_weight = swap_half(grad_weight)
+    got_in, other_weight = lax.optimization_barrier((got_in, other_weight))
     to_all_in, extra_in, part_y = local_call(
         lambda *refs: sum_both_kernel(count, *refs),
         "sum_both",
@@ -402,31 +397,30 @@
     )
     all_in = exchange(to_all_in, "grp")
     taken = [swap_along(part_y, y_stride, step) for step in range(1, RING)]
-    piece, extra_out = local_call(
+    to_all_out, extra_out = local_call(
         lambda *refs: sum_y_kernel(count, *refs),
         "sum_y",
         (part_y, *taken),
-        (shape_of(piece_rows + EXTRA_HALF, TILE, dtype=half_type), shape_of(EXTRA, TILE)),
-    )
-    taken = [swap_along(piece, x_stride, step) for step in range(1, RING)]
-    all_out = local_call(
-        join_kernel,
-        "join_x",
-        (piece, *taken),
-        shape_of(RING, piece_rows + EXTRA_HALF, TILE, dtype=half_type),
-    )
-    core_out = swap_core(all_out)
-    other_weight = swap_half(grad_weight)
+        (
+            shape_of(RING * CORES, piece_rows + EXTRA_HALF, TILE, dtype=half_type),
+            shape_of(EXTRA, TILE),
+        ),
+        flops=LATE_START,
+    )
+    same_y = [
+        [x * x_stride + y * y_stride + core for x in range(RING) for core in range(CORES)]
+        for y in range(RING)
+    ]
+    all_out = exchange(to_all_out, "blk", same_y)
 
     block = (width, width)
     damped_in = local_call(unpack_in_kernel, "unpack_in", (all_in,), shape_of(*block, dtype=half_type))
     return local_call(
         invert_kernel,
         "invert",
-        (damped_in, all_out, core_out, extra_in, extra_out, grad_weight, other_weight),
+        (damped_in, all_out, extra_in, extra_out, grad_weight, other_weight),
         shape_of(width, half, dtype=half_type),
         scratch=[
-            pltpu.VMEM((CORES * RING, piece_rows, TILE), half_type),
             pltpu.VMEM(block, half_type),
             pltpu.VMEM(block, half_type),
             pltpu.VMEM(block, jnp.float32),

time: 95.3 us -> 90.3 us (0.948)
  starting transfers between devices: 66.9 us -> 56.1 us
  waiting for transfers between devices: 13.8 us -> 19 us
    all_to_all x2 -> x3, waiting for transfers between devices: 0.01 us -> 14.9 us  [exchange(): lax.all_to_all(value, axis, 0, 0, tiled=True, axis_index_groups=groups)]
    ppermute x9 -> x6, starting transfers between devices: 30.8 us -> 21.2 us  [swap_along(): return lax.ppermute(value, 'blk', pairs)]
    ppermute x9 -> x6, waiting for transfers between devices: 11.8 us -> 4.13 us  [swap_along(): return lax.ppermute(value, 'blk', pairs)]
    ppermute x2 -> x1, starting transfers between devices: 10.6 us -> 3.15 us  [swap_core(): return lax.ppermute(value, 'blk', pairs)]
    all_to_all x2 -> x3, starting transfers between devices: 18.1 us -> 24.2 us  [exchange(): lax.all_to_all(value, axis, 0, 0, tiled=True, axis_index_groups=groups)]
    ppermute x2 -> x1, waiting for transfers between devices: 1.96 us -> 0.01 us  [swap_core(): return lax.ppermute(value, 'blk', pairs)]
    pallas_call x8 -> x7, Pallas kernels: 11.6 us -> 12.1 us  [local_call(): pl.pallas_call(kernel, out_shape=outs, in_specs=[VMEM_SPEC] * len(operand...]
  transfers between devices with their start and end apart: 15 -> 12, of which waited for: 7 -> 4; matrix products, arithmetic and copies ran while one was open for 0% -> 0% of each run, Pallas kernels for 2% -> 3%
where the time goes in v3:
time: 90.3 us; the launch traced here: 89.6 us
  starting transfers between devices  56.1 us (62%)
  waiting for transfers between devices  19 us (21%)
  Pallas kernels  12.1 us (13%)
  local copies, waits for them, and re-layouts  2.18 us (2%)
    all_to_all x3, starting transfers between devices, exchange(): lax.all_to_all(value, axis, 0, 0, tiled=True, axis_index_groups=groups)  24.2 us
    ppermute x6, starting transfers between devices, swap_along(): return lax.ppermute(value, 'blk', pairs)  21.2 us
    all_to_all x3, waiting for transfers between devices, exchange(): lax.all_to_all(value, axis, 0, 0, tiled=True, axis_index_groups=groups)  14.9 us
    pallas_call x7, Pallas kernels, local_call(): pl.pallas_call(kernel, out_shape=outs, in_specs=[VMEM_SPEC] * len(operand...  12.1 us
    ppermute x2, starting transfers between devices, swap_half(): return lax.ppermute(value, 'grp', pairs)  7.57 us
    ppermute x6, waiting for transfers between devices, swap_along(): return lax.ppermute(value, 'blk', pairs)  4.13 us
    ppermute x1, starting transfers between devices, swap_core(): return lax.ppermute(value, 'blk', pairs)  3.15 us
    unnamed x8, local copies, waits for them, and re-layouts  2.18 us
  transfers between devices with their start and end apart: 12, of which 4 were waited for; matrix products, arithmetic and copies ran while one was open for 0% of the time, Pallas kernels for 3%

profile of v3, /device:TPU:1, one launch (start us, length us, event | category | flops | bytes accessed | tf_op | source)
XLA Modules:
  0.0 89.6 jit_solution(9322496029354441885)
XLA Ops:
  0.0 4.0 %collective-permute-start.1 = (bf16[512,256]{1,0:T(8,128)(2,1)}, bf16[512,256]{1,0:T(8,128)(2,1)S(1)}, u32[]{:S(2)}, u32[]{:S(2)}) collective-permute-start(bf16[512,256]{1,0:T(8,128)(2,1)} %refs_0_.3), channel_id=1, source_target_pairs={{0,32},{32,0},{64,96},{96,64},{128,160},{160,128},{192,224},{224,1... | collective-permute-start | bytes 786440 | tf_op jit(solution)/shard_map/ppermute | solution.py:342
  4.0 0.0 copy-start
  4.0 1.2 %copy-done = bf16[1024,512]{1,0:T(8,128)(2,1)S(1)} copy-done((bf16[1024,512]{1,0:T(8,128)(2,1)S(1)}, bf16[1024,512]{1,0:T(8,128)(2,1)}, u32[]{:S(2)}) %copy-start) | copy-done | bytes 1048600
  5.3 0.0 copy-start.1
  5.3 0.9 %copy-done.1 = bf16[512,256]{1,0:T(8,128)(2,1)S(1)} copy-done((bf16[512,256]{1,0:T(8,128)(2,1)S(1)}, bf16[512,256]{1,0:T(8,128)(2,1)}, u32[]{:S(2)}) %copy-start.1) | copy-done | bytes 262168
  6.2 1.4 %gram_in.1 = f32[16,72,128]{2,1,0:T(8,128)} custom-call(bf16[1024,512]{1,0:T(8,128)(2,1)S(1)} %copy-done, bf16[512,256]{1,0:T(8,128)(2,1)S(1)} %copy-done.1), custom_call_target="tpu_custom_call" | custom-call | flops 536870912 | bytes 1900544 | tf_op jit(solution)/shard_map/gram_in/pallas_call | solution.py:310
  7.6 0.0 copy-start.2
  7.6 10.3 %all-to-all-start = ((f32[16,72,128]{2,1,0:T(8,128)}), f32[16,72,128]{2,1,0:T(8,128)S(1)}, u32[]{:S(2)}, u32[]{:S(2)}) async-start(f32[16,72,128]{2,1,0:T(8,128)} %gram_in.1), calls=%async_computation | async-start | bytes 1179648 | tf_op jit(solution)/shard_map/all_to_all | solution.py:327
  17.9 0.0 copy-start.3
  17.9 0.0 collective-permute-done.1.refs_1_
  17.9 0.0 copy-done.2
  18.0 0.6 gram_out.1
  18.5 3.1 %collective-permute-start.2 = (f32[520,128]{1,0:T(8,128)S(1)}, f32[520,128]{1,0:T(8,128)S(1)}, u32[]{:S(2)}, u32[]{:S(2)}) collective-permute-start(f32[520,128]{1,0:T(8,128)S(1)} %get-tuple-element.20), channel_id=1, source_target_pairs={{0,1},{1,0},{2,3},{3,2},{4,5},{5,4},{6,7},{7,6},{8,9},{9,8},{10,11... | collective-permute-start | bytes 798728 | tf_op jit(solution)/shard_map/ppermute | solution.py:332
  21.7 0.0 copy-done.3
  21.7 3.5 %collective-permute-start = (bf16[512,256]{1,0:T(8,128)(2,1)S(1)}, bf16[512,256]{1,0:T(8,128)(2,1)S(1)}, u32[]{:S(2)}, u32[]{:S(2)}) collective-permute-start(bf16[512,256]{1,0:T(8,128)(2,1)S(1)} %copy-done.3), channel_id=1, source_target_pairs={{0,32},{32,0},{64,96},{96,64},{128,160},{160,128},{192,224},{224,1... | collective-permute-start | bytes 786440 | tf_op jit(solution)/shard_map/ppermute | solution.py:342
  25.3 0.0 collective-permute-done.2.right_ref
  25.3 0.1 add_cores.1
  25.3 3.1 %collective-permute-start.3 = (f32[136,128]{1,0:T(8,128)S(1)}, f32[136,128]{1,0:T(8,128)S(1)}, u32[]{:S(2)}, u32[]{:S(2)}) collective-permute-start(f32[136,128]{1,0:T(8,128)S(1)} %get-tuple-element.22), channel_id=1, source_target_pairs={{0,8},{1,9},{2,10},{3,11},{4,12},{5,13},{6,14},{7,15},{8,0},{9,1},... | collective-permute-start | bytes 208904 | tf_op jit(solution)/shard_map/ppermute | solution.py:337
  28.5 4.4 %collective-permute-start.4 = (f32[136,128]{1,0:T(8,128)S(1)}, f32[136,128]{1,0:T(8,128)S(1)}, u32[]{:S(2)}, u32[]{:S(2)}) collective-permute-start(f32[136,128]{1,0:T(8,128)S(1)} %get-tuple-element.23), channel_id=1, source_target_pairs={{0,16},{1,17},{2,18},{3,19},{4,20},{5,21},{6,22},{7,23},{8,24},{9,... | collective-permute-start | bytes 208904 | tf_op jit(solution)/shard_map/ppermute | solution.py:337
  32.8 2.1 %collective-permute-start.5 = (f32[136,128]{1,0:T(8,128)S(1)}, f32[136,128]{1,0:T(8,128)S(1)}, u32[]{:S(2)}, u32[]{:S(2)}) collective-permute-start(f32[136,128]{1,0:T(8,128)S(1)} %get-tuple-element.24), channel_id=1, source_target_pairs={{0,24},{1,25},{2,26},{3,27},{4,28},{5,29},{6,30},{7,31},{8,16},{9,... | collective-permute-start | bytes 208904 | tf_op jit(solution)/shard_map/ppermute | solution.py:337
  34.9 0.0 collective-permute-done.other_weight_ref
  34.9 0.0 all-to-all-done.refs_0_
  35.0 0.0 collective-permute-done.3.refs_2_
  35.0 0.3 collective-permute-done.4.refs_3_
  35.3 3.8 %collective-permute-done.5.refs_4_ = f32[136,128]{1,0:T(8,128)S(1)} collective-permute-done((f32[136,128]{1,0:T(8,128)S(1)}, f32[136,128]{1,0:T(8,128)S(1)}, u32[]{:S(2)}, u32[]{:S(2)}) %collective-permute-start.5) | collective-permute-done | bytes 69664 | tf_op jit(solution)/shard_map/ppermute | solution.py:337
  39.1 0.8 sum_both.1
  39.8 4.2 %collective-permute-start.6 = (f32[136,128]{1,0:T(8,128)S(1)}, f32[136,128]{1,0:T(8,128)S(1)}, u32[]{:S(2)}, u32[]{:S(2)}) collective-permute-start(f32[136,128]{1,0:T(8,128)S(1)} %get-tuple-element.26.refs_0_), channel_id=1, source_target_pairs={{0,2},{1,3},{2,0},{3,1},{4,6},{5,7},{6,4},{7,5},{8,10},{9,11},{10,... | collective-permute-start | bytes 208904 | tf_op jit(solution)/shard_map/ppermute | solution.py:337
  44.1 5.5 %collective-permute-start.7 = (f32[136,128]{1,0:T(8,128)S(1)}, f32[136,128]{1,0:T(8,128)S(1)}, u32[]{:S(2)}, u32[]{:S(2)}) collective-permute-start(f32[136,128]{1,0:T(8,128)S(1)} %get-tuple-element.26.refs_0_), channel_id=1, source_target_pairs={{0,4},{1,5},{2,6},{3,7},{4,0},{5,1},{6,2},{7,3},{8,12},{9,13},{10,... | collective-permute-start | bytes 208904 | tf_op jit(solution)/shard_map/ppermute | solution.py:337
  49.6 1.9 %collective-permute-start.8 = (f32[136,128]{1,0:T(8,128)S(1)}, f32[136,128]{1,0:T(8,128)S(1)}, u32[]{:S(2)}, u32[]{:S(2)}) collective-permute-start(f32[136,128]{1,0:T(8,128)S(1)} %get-tuple-element.26.refs_0_), channel_id=1, source_target_pairs={{0,6},{1,7},{2,4},{3,5},{4,2},{5,3},{6,0},{7,1},{8,14},{9,15},{10,... | collective-permute-start | bytes 208904 | tf_op jit(solution)/shard_map/ppermute | solution.py:337
  51.5 6.5 %all-to-all-start.1 = ((bf16[16,64,128]{2,1,0:T(8,128)(2,1)}), bf16[16,64,128]{2,1,0:T(8,128)(2,1)S(1)}, u32[]{:S(2)}, u32[]{:S(2)}) async-start(bf16[16,64,128]{2,1,0:T(8,128)(2,1)} %get-tuple-element.25), calls=%async_computation.1 | async-start | bytes 524288 | tf_op jit(solution)/shard_map/all_to_all | solution.py:327
  58.0 0.0 collective-permute-done.6.refs_1_
  58.0 0.0 collective-permute-done.7.refs_2_
  58.0 0.0 collective-permute-done.8.refs_3_
  58.1 0.8 sum_y.1
  58.8 8.2 %all-to-all-done.1.got_ref = bf16[16,64,128]{2,1,0:T(8,128)(2,1)S(1)} async-done(((bf16[16,64,128]{2,1,0:T(8,128)(2,1)}), bf16[16,64,128]{2,1,0:T(8,128)(2,1)S(1)}, u32[]{:S(2)}, u32[]{:S(2)}) %all-to-all-start.1) | async-done | bytes 262176 | tf_op jit(solution)/shard_map/all_to_all | solution.py:327
  67.0 7.4 %all-to-all-start.2 = ((bf16[8,144,128]{2,1,0:T(8,128)(2,1)}), bf16[8,144,128]{2,1,0:T(8,128)(2,1)S(1)}, u32[]{:S(2)}, u32[]{:S(2)}) async-start(bf16[8,144,128]{2,1,0:T(8,128)(2,1)} %get-tuple-element.27), calls=%async_computation.2 | async-start | bytes 589824 | tf_op jit(solution)/shard_map/all_to_all | solution.py:327
  74.4 0.1 unpack_in.1.damped_in_ref
  74.5 6.7 %all-to-all-done.2.got_out_ref = bf16[8,144,128]{2,1,0:T(8,128)(2,1)S(1)} async-done(((bf16[8,144,128]{2,1,0:T(8,128)(2,1)}), bf16[8,144,128]{2,1,0:T(8,128)(2,1)S(1)}, u32[]{:S(2)}, u32[]{:S(2)}) %all-to-all-start.2) | async-done | bytes 294944 | tf_op jit(solution)/shard_map/all_to_all | solution.py:327
  81.2 8.4 %invert.1 = bf16[512,256]{1,0:T(8,128)(2,1)} custom-call(bf16[512,512]{1,0:T(8,128)(2,1)S(1)} %unpack_in.1.damped_in_ref, bf16[8,144,128]{2,1,0:T(8,128)(2,1)S(1)} %all-to-all-done.2.got_out_ref, f32[8,128]{1,0:T(8,128)S(1)} %get-tuple-element.28.extra_in_ref, f32[8,128]{1,0:T(8,128)S(1)} %get-tuple-element.29.extra_out_ref, bf16[512,256]{1,0:T(8,128)(2,1)S(1)} %copy-done.3, ...), custom_call_target="tpu_custom_call" | custom-call | flops 5905580032 | bytes 1613824 | tf_op jit(solution)/shard_map/invert/pallas_call | solution.py:310
Async XLA Ops:
  0.0 17.9 %collective-permute-start.1 = (bf16[512,256]{1,0:T(8,128)(2,1)}, bf16[512,256]{1,0:T(8,128)(2,1)S(1)}, u32[]{:S(2)}, u32[]{:S(2)}) collective-permute-start(bf16[512,256]{1,0:T(8,128)(2,1)} %refs_0_.3), channel_id=1, source_target_pairs={{0,32},{32,0},{64,96},{96,64},{128,160},{160,128},{192,224},{224,1... | collective-permute-start | bytes 786440 | tf_op jit(solution)/shard_map/ppermute | solution.py:342
  4.0 1.2 %copy-start = (bf16[1024,512]{1,0:T(8,128)(2,1)S(1)}, bf16[1024,512]{1,0:T(8,128)(2,1)}, u32[]{:S(2)}) copy-start(bf16[1024,512]{1,0:T(8,128)(2,1)} %refs_0_.2) | copy-start | bytes 3145732
  5.3 0.9 %copy-start.1 = (bf16[512,256]{1,0:T(8,128)(2,1)S(1)}, bf16[512,256]{1,0:T(8,128)(2,1)}, u32[]{:S(2)}) copy-start(bf16[512,256]{1,0:T(8,128)(2,1)} %refs_0_.3) | copy-start | bytes 786436
  7.6 10.3 %copy-start.2 = (bf16[512,256]{1,0:T(8,128)(2,1)S(1)}, bf16[512,256]{1,0:T(8,128)(2,1)}, u32[]{:S(2)}) copy-start(bf16[512,256]{1,0:T(8,128)(2,1)} %refs_0_.3) | copy-start | bytes 786436
  7.6 27.3 %all-to-all-start = ((f32[16,72,128]{2,1,0:T(8,128)}), f32[16,72,128]{2,1,0:T(8,128)S(1)}, u32[]{:S(2)}, u32[]{:S(2)}) async-start(f32[16,72,128]{2,1,0:T(8,128)} %gram_in.1), calls=%async_computation | async-start | bytes 1179648 | tf_op jit(solution)/shard_map/all_to_all | solution.py:327
  17.9 3.8 %copy-start.3 = (bf16[512,256]{1,0:T(8,128)(2,1)S(1)}, bf16[512,256]{1,0:T(8,128)(2,1)}, u32[]{:S(2)}) copy-start(bf16[512,256]{1,0:T(8,128)(2,1)} %weight_ref.1) | copy-start | bytes 786436
  18.5 6.7 %collective-permute-start.2 = (f32[520,128]{1,0:T(8,128)S(1)}, f32[520,128]{1,0:T(8,128)S(1)}, u32[]{:S(2)}, u32[]{:S(2)}) collective-permute-start(f32[520,128]{1,0:T(8,128)S(1)} %get-tuple-element.20), channel_id=1, source_target_pairs={{0,1},{1,0},{2,3},{3,2},{4,5},{5,4},{6,7},{7,6},{8,9},{9,8},{10,11... | collective-permute-start | bytes 798728 | tf_op jit(solution)/shard_map/ppermute | solution.py:332
  21.7 13.2 %collective-permute-start = (bf16[512,256]{1,0:T(8,128)(2,1)S(1)}, bf16[512,256]{1,0:T(8,128)(2,1)S(1)}, u32[]{:S(2)}, u32[]{:S(2)}) collective-permute-start(bf16[512,256]{1,0:T(8,128)(2,1)S(1)} %copy-done.3), channel_id=1, source_target_pairs={{0,32},{32,0},{64,96},{96,64},{128,160},{160,128},{192,224},{224,1... | collective-permute-start | bytes 786440 | tf_op jit(solution)/shard_map/ppermute | solution.py:342
  25.3 9.6 %collective-permute-start.3 = (f32[136,128]{1,0:T(8,128)S(1)}, f32[136,128]{1,0:T(8,128)S(1)}, u32[]{:S(2)}, u32[]{:S(2)}) collective-permute-start(f32[136,128]{1,0:T(8,128)S(1)} %get-tuple-element.22), channel_id=1, source_target_pairs={{0,8},{1,9},{2,10},{3,11},{4,12},{5,13},{6,14},{7,15},{8,0},{9,1},... | collective-permute-start | bytes 208904 | tf_op jit(solution)/shard_map/ppermute | solution.py:337
  28.5 6.9 %collective-permute-start.4 = (f32[136,128]{1,0:T(8,128)S(1)}, f32[136,128]{1,0:T(8,128)S(1)}, u32[]{:S(2)}, u32[]{:S(2)}) collective-permute-start(f32[136,128]{1,0:T(8,128)S(1)} %get-tuple-element.23), channel_id=1, source_target_pairs={{0,16},{1,17},{2,18},{3,19},{4,20},{5,21},{6,22},{7,23},{8,24},{9,... | collective-permute-start | bytes 208904 | tf_op jit(solution)/shard_map/ppermute | solution.py:337
  32.8 6.3 %collective-permute-start.5 = (f32[136,128]{1,0:T(8,128)S(1)}, f32[136,128]{1,0:T(8,128)S(1)}, u32[]{:S(2)}, u32[]{:S(2)}) collective-permute-start(f32[136,128]{1,0:T(8,128)S(1)} %get-tuple-element.24), channel_id=1, source_target_pairs={{0,24},{1,25},{2,26},{3,27},{4,28},{5,29},{6,30},{7,31},{8,16},{9,... | collective-permute-start | bytes 208904 | tf_op jit(solution)/shard_map/ppermute | solution.py:337
  39.8 18.2 %collective-permute-start.6 = (f32[136,128]{1,0:T(8,128)S(1)}, f32[136,128]{1,0:T(8,128)S(1)}, u32[]{:S(2)}, u32[]{:S(2)}) collective-permute-start(f32[136,128]{1,0:T(8,128)S(1)} %get-tuple-element.26.refs_0_), channel_id=1, source_target_pairs={{0,2},{1,3},{2,0},{3,1},{4,6},{5,7},{6,4},{7,5},{8,10},{9,11},{10,... | collective-permute-start | bytes 208904 | tf_op jit(solution)/shard_map/ppermute | solution.py:337
  44.1 14.0 %collective-permute-start.7 = (f32[136,128]{1,0:T(8,128)S(1)}, f32[136,128]{1,0:T(8,128)S(1)}, u32[]{:S(2)}, u32[]{:S(2)}) collective-permute-start(f32[136,128]{1,0:T(8,128)S(1)} %get-tuple-element.26.refs_0_), channel_id=1, source_target_pairs={{0,4},{1,5},{2,6},{3,7},{4,0},{5,1},{6,2},{7,3},{8,12},{9,13},{10,... | collective-permute-start | bytes 208904 | tf_op jit(solution)/shard_map/ppermute | solution.py:337
  49.6 8.4 %collective-permute-start.8 = (f32[136,128]{1,0:T(8,128)S(1)}, f32[136,128]{1,0:T(8,128)S(1)}, u32[]{:S(2)}, u32[]{:S(2)}) collective-permute-start(f32[136,128]{1,0:T(8,128)S(1)} %get-tuple-element.26.refs_0_), channel_id=1, source_target_pairs={{0,6},{1,7},{2,4},{3,5},{4,2},{5,3},{6,0},{7,1},{8,14},{9,15},{10,... | collective-permute-start | bytes 208904 | tf_op jit(solution)/shard_map/ppermute | solution.py:337
  51.5 15.5 %all-to-all-start.1 = ((bf16[16,64,128]{2,1,0:T(8,128)(2,1)}), bf16[16,64,128]{2,1,0:T(8,128)(2,1)S(1)}, u32[]{:S(2)}, u32[]{:S(2)}) async-start(bf16[16,64,128]{2,1,0:T(8,128)(2,1)} %get-tuple-element.25), calls=%async_computation.1 | async-start | bytes 524288 | tf_op jit(solution)/shard_map/all_to_all | solution.py:327
  67.0 14.2 %all-to-all-start.2 = ((bf16[8,144,128]{2,1,0:T(8,128)(2,1)}), bf16[8,144,128]{2,1,0:T(8,128)(2,1)S(1)}, u32[]{:S(2)}, u32[]{:S(2)}) async-start(bf16[8,144,128]{2,1,0:T(8,128)(2,1)} %get-tuple-element.27), calls=%async_computation.2 | async-start | bytes 589824 | tf_op jit(solution)/shard_map/all_to_all | solution.py:327

commit v4 on v3

--- a/solution.py
+++ b/solution.py
@@ -1,3 +1,5 @@
+import functools
+
 import jax
 import jax.numpy as jnp
 from jax import lax
@@ -144,18 +146,18 @@
     return lax.axis_index("blk") // (RING * CORES)
 
 
-def add_cores_kernel(left_ref, right_ref, *out_refs):
-    rows = out_refs[0].shape[0] - EXTRA
-    share = left_ref.shape[0] - EXTRA
-    extra = left_ref[share:, :] + right_ref[share:, :]
-    for step, ref in enumerate(out_refs):
-        place = pl.ds(pl.multiple_of((along_x() ^ step) * rows, rows), rows)
+def fold_kernel(bit, left_ref, right_ref, keep_ref, give_ref):
+    rows = keep_ref.shape[0] - EXTRA
+    extra = left_ref[2 * rows :, :] + right_ref[2 * rows :, :]
+    own = (along_x() >> bit) & 1
+    for ref, owner in ((keep_ref, own), (give_ref, 1 - own)):
+        place = pl.ds(pl.multiple_of(owner * rows, rows), rows)
         ref[:rows, :] = left_ref[place, :] + right_ref[place, :]
         ref[rows:, :] = extra
 
 
-def sum_ring(refs):
-    return (refs[0][...] + refs[1][...]) + (refs[2][...] + refs[3][...])
+def add_kernel(left_ref, right_ref, out_ref):
+    out_ref[...] = left_ref[...] + right_ref[...]
 
 
 def sum_pieces(ref):
@@ -172,8 +174,9 @@
     return [high, middle, rest - middle]
 
 
-def sum_both_kernel(count, got_ref, *refs):
-    *got_refs, send_ref, extra_in_ref, out_ref = refs
+def sum_both_kernel(
+    count, got_ref, left_ref, right_ref, send_ref, extra_in_ref, out_ref
+):
     total = sum_pieces(got_ref)
     rows = send_ref.shape[1]
     rounded = total[:rows].astype(jnp.bfloat16)
@@ -181,7 +184,7 @@
         send_ref[piece] = rounded
     extra = total[rows:]
     extra_in_ref[...] = extra
-    total = sum_ring(got_refs)
+    total = left_ref[...] + right_ref[...]
     rows = total.shape[0] - EXTRA
     trace_in = jnp.broadcast_to(total_of(extra[:count]), (1, TILE))
     energy_out = extra[count : count + 1]
@@ -191,9 +194,8 @@
     )
 
 
-def sum_y_kernel(count, *refs):
-    *got_refs, send_ref, extra_ref = refs
-    total = sum_ring(got_refs)
+def sum_y_kernel(count, left_ref, right_ref, send_ref, extra_ref):
+    total = left_ref[...] + right_ref[...]
     rows = total.shape[0] - EXTRA
     extra = total[rows:]
     scalars = split_rows(extra[count : count + 1]) + split_rows(extra[count + 1 : count + 2])
@@ -357,7 +359,7 @@
 
     other_grads = swap_half(output_grads)
     send_in = local_call(
-        lambda *refs: gram_in_kernel(total_tokens, *refs),
+        functools.partial(gram_in_kernel, total_tokens),
         "gram_in",
         (activations, output_grads),
         shape_of(groups, in_rows + EXTRA, TILE),
@@ -366,7 +368,7 @@
     got_in = exchange(send_in, "grp")
 
     keep, give = local_call(
-        lambda *refs: gram_out_kernel(total_tokens, *refs),
+        functools.partial(gram_out_kernel, total_tokens),
         "gram_out",
         (output_grads, other_grads),
         (shape_of(share_rows + EXTRA, TILE),) * 2,
@@ -376,19 +378,21 @@
         ],
         flops=LATE_START * 3,
     )
-    keep, *gives = local_call(
-        add_cores_kernel,
-        "add_cores",
-        (keep, swap_core(give)),
-        (shape_of(piece_rows + EXTRA, TILE),) * RING,
-    )
-    taken = [swap_along(give, x_stride, step + 1) for step, give in enumerate(gives)]
-    other_weight = swap_half(grad_weight)
-    got_in, other_weight = lax.optimization_barrier((got_in, other_weight))
+    folds = (
+        ("fold_cores", 1, share_rows // 2, swap_core),
+        ("fold_x", 0, piece_rows, lambda value: swap_along(value, x_stride, 3)),
+    )
+    for name, bit, rows, swap in folds:
+        keep, give = local_call(
+            functools.partial(fold_kernel, bit),
+            name,
+            (keep, swap(give)),
+            (shape_of(rows + EXTRA, TILE),) * 2,
+        )
     to_all_in, extra_in, part_y = local_call(
-        lambda *refs: sum_both_kernel(count, *refs),
+        functools.partial(sum_both_kernel, count),
         "sum_both",
-        (got_in, keep, *taken),
+        (got_in, keep, swap_along(give, x_stride, 1)),
         (
             shape_of(groups, in_rows, TILE, dtype=half_type),
             shape_of(EXTRA, TILE),
@@ -396,21 +400,28 @@
         ),
     )
     all_in = exchange(to_all_in, "grp")
-    taken = [swap_along(part_y, y_stride, step) for step in range(1, RING)]
+    part_y = local_call(
+        add_kernel,
+        "add_y",
+        (part_y, swap_along(part_y, y_stride, 1)),
+        shape_of(*part_y.shape),
+        flops=LATE_START,
+    )
     to_all_out, extra_out = local_call(
-        lambda *refs: sum_y_kernel(count, *refs),
+        functools.partial(sum_y_kernel, count),
         "sum_y",
-        (part_y, *taken),
+        (part_y, swap_along(part_y, y_stride, 3)),
         (
             shape_of(RING * CORES, piece_rows + EXTRA_HALF, TILE, dtype=half_type),
             shape_of(EXTRA, TILE),
         ),
-        flops=LATE_START,
     )
     same_y = [
         [x * x_stride + y * y_stride + core for x in range(RING) for core in range(CORES)]
         for y in range(RING)
     ]
+    sent_weight, to_all_out = lax.optimization_barrier((grad_weight, to_all_out))
+    other_weight = swap_half(sent_weight)
     all_out = exchange(to_all_out, "blk", same_y)
 
     block = (width, width)

time: 90.3 us -> 84.9 us (0.940)
  starting transfers between devices: 56.1 us -> 53.1 us
  waiting for transfers between devices: 19 us -> 16.6 us
    all_to_all x3, waiting for transfers between devices: 14.9 us -> 6.67 us  [exchange(): lax.all_to_all(value, axis, 0, 0, tiled=True, axis_index_groups=groups)]
    ppermute x6 -> x4, starting transfers between devices: 21.2 us -> 16 us  [swap_along(): return lax.ppermute(value, 'blk', pairs)]
    ppermute x6 -> x4, waiting for transfers between devices: 4.13 us -> 8.82 us  [swap_along(): return lax.ppermute(value, 'blk', pairs)]
    all_to_all x3, starting transfers between devices: 24.2 us -> 25.9 us  [exchange(): lax.all_to_all(value, axis, 0, 0, tiled=True, axis_index_groups=groups)]
    ppermute x1, waiting for transfers between devices: 0.01 us -> 1.15 us  [swap_core(): return lax.ppermute(value, 'blk', pairs)]
    pallas_call x7 -> x9, Pallas kernels: 12.1 us -> 12.1 us  [local_call(): pl.pallas_call(kernel, out_shape=outs, in_specs=[VMEM_SPEC] * len(operand...]
  transfers between devices with their start and end apart: 12 -> 10, of which waited for: 4 -> 5; matrix products, arithmetic and copies ran while one was open for 0% -> 0% of each run, Pallas kernels for 3% -> 4%
where the time goes in v4:
time: 84.9 us; the launch traced here: 84.2 us
  starting transfers between devices  53.1 us (63%)
  waiting for transfers between devices  16.6 us (20%)
  Pallas kernels  12.1 us (14%)
  local copies, waits for them, and re-layouts  2.18 us (3%)
    all_to_all x3, starting transfers between devices, exchange(): lax.all_to_all(value, axis, 0, 0, tiled=True, axis_index_groups=groups)  25.9 us
    ppermute x4, starting transfers between devices, swap_along(): return lax.ppermute(value, 'blk', pairs)  16 us
    pallas_call x9, Pallas kernels, local_call(): pl.pallas_call(kernel, out_shape=outs, in_specs=[VMEM_SPEC] * len(operand...  12.1 us
    ppermute x4, waiting for transfers between devices, swap_along(): return lax.ppermute(value, 'blk', pairs)  8.82 us
    ppermute x2, starting transfers between devices, swap_half(): return lax.ppermute(value, 'grp', pairs)  8.08 us
    all_to_all x3, waiting for transfers between devices, exchange(): lax.all_to_all(value, axis, 0, 0, tiled=True, axis_index_groups=groups)  6.67 us
    ppermute x1, starting transfers between devices, swap_core(): return lax.ppermute(value, 'blk', pairs)  3.15 us
    unnamed x8, local copies, waits for them, and re-layouts  2.18 us
  transfers between devices with their start and end apart: 10, of which 5 were waited for; matrix products, arithmetic and copies ran while one was open for 0% of the time, Pallas kernels for 4%

profile of v4, /device:TPU:1, one launch (start us, length us, event | category | flops | bytes accessed | tf_op | source)
XLA Modules:
  0.0 84.2 jit_solution(7215580947180088334)
XLA Ops:
  0.0 4.0 %collective-permute-start = (bf16[512,256]{1,0:T(8,128)(2,1)}, bf16[512,256]{1,0:T(8,128)(2,1)S(1)}, u32[]{:S(2)}, u32[]{:S(2)}) collective-permute-start(bf16[512,256]{1,0:T(8,128)(2,1)} %own_ref.1), channel_id=1, source_target_pairs={{0,32},{32,0},{64,96},{96,64},{128,160},{160,128},{192,224},{224,1... | collective-permute-start | bytes 786440 | tf_op jit(solution)/shard_map/ppermute | solution.py:344
  4.0 0.0 copy-start
  4.0 1.2 %copy-done = bf16[1024,512]{1,0:T(8,128)(2,1)S(1)} copy-done((bf16[1024,512]{1,0:T(8,128)(2,1)S(1)}, bf16[1024,512]{1,0:T(8,128)(2,1)}, u32[]{:S(2)}) %copy-start) | copy-done | bytes 1048600
  5.3 0.0 copy-start.1
  5.3 0.9 %copy-done.1 = bf16[512,256]{1,0:T(8,128)(2,1)S(1)} copy-done((bf16[512,256]{1,0:T(8,128)(2,1)S(1)}, bf16[512,256]{1,0:T(8,128)(2,1)}, u32[]{:S(2)}) %copy-start.1) | copy-done | bytes 262168
  6.2 1.4 %gram_in.1 = f32[16,72,128]{2,1,0:T(8,128)} custom-call(bf16[1024,512]{1,0:T(8,128)(2,1)S(1)} %copy-done, bf16[512,256]{1,0:T(8,128)(2,1)S(1)} %copy-done.1), custom_call_target="tpu_custom_call" | custom-call | flops 536870912 | bytes 1900544 | tf_op jit(solution)/shard_map/gram_in/pallas_call | solution.py:312
  7.6 0.0 copy-start.2
  7.6 10.3 %all-to-all-start = ((f32[16,72,128]{2,1,0:T(8,128)}), f32[16,72,128]{2,1,0:T(8,128)S(1)}, u32[]{:S(2)}, u32[]{:S(2)}) async-start(f32[16,72,128]{2,1,0:T(8,128)} %gram_in.1), calls=%async_computation | async-start | bytes 1179648 | tf_op jit(solution)/shard_map/all_to_all | solution.py:329
  17.9 0.0 collective-permute-done.other_ref
  17.9 0.0 copy-done.2
  17.9 0.6 gram_out.1
  18.5 3.1 %collective-permute-start.1 = (f32[520,128]{1,0:T(8,128)S(1)}, f32[520,128]{1,0:T(8,128)S(1)}, u32[]{:S(2)}, u32[]{:S(2)}) collective-permute-start(f32[520,128]{1,0:T(8,128)S(1)} %get-tuple-element.19), channel_id=1, source_target_pairs={{0,1},{1,0},{2,3},{3,2},{4,5},{5,4},{6,7},{7,6},{8,9},{9,8},{10,11... | collective-permute-start | bytes 798728 | tf_op jit(solution)/shard_map/ppermute | solution.py:334
  21.7 1.1 %collective-permute-done.1.right_ref = f32[520,128]{1,0:T(8,128)S(1)} collective-permute-done((f32[520,128]{1,0:T(8,128)S(1)}, f32[520,128]{1,0:T(8,128)S(1)}, u32[]{:S(2)}, u32[]{:S(2)}) %collective-permute-start.1) | collective-permute-done | bytes 266272 | tf_op jit(solution)/shard_map/ppermute | solution.py:334
  22.9 4.4 %collective-permute-start.2 = (f32[264,128]{1,0:T(8,128)S(1)}, f32[264,128]{1,0:T(8,128)S(1)}, u32[]{:S(2)}, u32[]{:S(2)}) collective-permute-start(f32[264,128]{1,0:T(8,128)S(1)} %get-tuple-element.21), channel_id=1, source_target_pairs={{0,24},{1,25},{2,26},{3,27},{4,28},{5,29},{6,30},{7,31},{8,16},{9,... | collective-permute-start | bytes 405512 | tf_op jit(solution)/shard_map/ppermute | solution.py:339
  27.3 3.5 %collective-permute-done.2.right_ref = f32[264,128]{1,0:T(8,128)S(1)} collective-permute-done((f32[264,128]{1,0:T(8,128)S(1)}, f32[264,128]{1,0:T(8,128)S(1)}, u32[]{:S(2)}, u32[]{:S(2)}) %collective-permute-start.2) | collective-permute-done | bytes 135200 | tf_op jit(solution)/shard_map/ppermute | solution.py:339
  30.8 1.9 %collective-permute-start.3 = (f32[136,128]{1,0:T(8,128)S(1)}, f32[136,128]{1,0:T(8,128)S(1)}, u32[]{:S(2)}, u32[]{:S(2)}) collective-permute-start(f32[136,128]{1,0:T(8,128)S(1)} %get-tuple-element.23), channel_id=1, source_target_pairs={{0,8},{1,9},{2,10},{3,11},{4,12},{5,13},{6,14},{7,15},{8,0},{9,1},... | collective-permute-start | bytes 208904 | tf_op jit(solution)/shard_map/ppermute | solution.py:339
  32.7 3.4 %collective-permute-done.3.right_ref = f32[136,128]{1,0:T(8,128)S(1)} collective-permute-done((f32[136,128]{1,0:T(8,128)S(1)}, f32[136,128]{1,0:T(8,128)S(1)}, u32[]{:S(2)}, u32[]{:S(2)}) %collective-permute-start.3) | collective-permute-done | bytes 69664 | tf_op jit(solution)/shard_map/ppermute | solution.py:339
  36.1 0.0 all-to-all-done.got_ref
  36.2 0.8 sum_both.1
  36.9 4.2 %collective-permute-start.4 = (f32[136,128]{1,0:T(8,128)S(1)}, f32[136,128]{1,0:T(8,128)S(1)}, u32[]{:S(2)}, u32[]{:S(2)}) collective-permute-start(f32[136,128]{1,0:T(8,128)S(1)} %get-tuple-element.25.left_ref), channel_id=1, source_target_pairs={{0,2},{1,3},{2,0},{3,1},{4,6},{5,7},{6,4},{7,5},{8,10},{9,11},{10,... | collective-permute-start | bytes 208904 | tf_op jit(solution)/shard_map/ppermute | solution.py:339
  41.1 7.5 %all-to-all-start.1 = ((bf16[16,64,128]{2,1,0:T(8,128)(2,1)}), bf16[16,64,128]{2,1,0:T(8,128)(2,1)S(1)}, u32[]{:S(2)}, u32[]{:S(2)}) async-start(bf16[16,64,128]{2,1,0:T(8,128)(2,1)} %get-tuple-element.24), calls=%async_computation.1 | async-start | bytes 524288 | tf_op jit(solution)/shard_map/all_to_all | solution.py:329
  48.7 0.0 copy-start.3
  48.7 0.0 collective-permute-done.4.right_ref
  48.7 5.5 %collective-permute-start.5 = (f32[136,128]{1,0:T(8,128)S(1)}, f32[136,128]{1,0:T(8,128)S(1)}, u32[]{:S(2)}, u32[]{:S(2)}) collective-permute-start(f32[136,128]{1,0:T(8,128)S(1)} %add_y.1.left_ref), channel_id=1, source_target_pairs={{0,6},{1,7},{2,4},{3,5},{4,2},{5,3},{6,0},{7,1},{8,14},{9,15},{10,... | collective-permute-start | bytes 208904 | tf_op jit(solution)/shard_map/ppermute | solution.py:339
  54.2 1.9 %collective-permute-done.5.right_ref = f32[136,128]{1,0:T(8,128)S(1)} collective-permute-done((f32[136,128]{1,0:T(8,128)S(1)}, f32[136,128]{1,0:T(8,128)S(1)}, u32[]{:S(2)}, u32[]{:S(2)}) %collective-permute-start.5) | collective-permute-done | bytes 69664 | tf_op jit(solution)/shard_map/ppermute | solution.py:339
  56.1 0.7 sum_y.1
  56.8 0.0 copy-done.3
  56.8 4.1 %collective-permute-start.6 = (bf16[512,256]{1,0:T(8,128)(2,1)S(1)}, bf16[512,256]{1,0:T(8,128)(2,1)S(1)}, u32[]{:S(2)}, u32[]{:S(2)}) collective-permute-start(bf16[512,256]{1,0:T(8,128)(2,1)S(1)} %copy-done.3), channel_id=1, source_target_pairs={{0,32},{32,0},{64,96},{96,64},{128,160},{160,128},{192,224},{224,1... | collective-permute-start | bytes 786440 | tf_op jit(solution)/shard_map/ppermute | solution.py:344
  60.9 0.0 all-to-all-done.1.got_ref
  60.9 8.1 %all-to-all-start.2 = ((bf16[8,144,128]{2,1,0:T(8,128)(2,1)}), bf16[8,144,128]{2,1,0:T(8,128)(2,1)S(1)}, u32[]{:S(2)}, u32[]{:S(2)}) async-start(bf16[8,144,128]{2,1,0:T(8,128)(2,1)} %get-tuple-element.27), calls=%async_computation.2 | async-start | bytes 589824 | tf_op jit(solution)/shard_map/all_to_all | solution.py:329
  69.0 0.1 unpack_in.1.damped_in_ref
  69.1 6.7 %all-to-all-done.2.got_out_ref = bf16[8,144,128]{2,1,0:T(8,128)(2,1)S(1)} async-done(((bf16[8,144,128]{2,1,0:T(8,128)(2,1)}), bf16[8,144,128]{2,1,0:T(8,128)(2,1)S(1)}, u32[]{:S(2)}, u32[]{:S(2)}) %all-to-all-start.2) | async-done | bytes 294944 | tf_op jit(solution)/shard_map/all_to_all | solution.py:329
  75.8 0.0 collective-permute-done.6.other_weight_ref
  75.8 8.4 %invert.1 = bf16[512,256]{1,0:T(8,128)(2,1)} custom-call(bf16[512,512]{1,0:T(8,128)(2,1)S(1)} %unpack_in.1.damped_in_ref, bf16[8,144,128]{2,1,0:T(8,128)(2,1)S(1)} %all-to-all-done.2.got_out_ref, f32[8,128]{1,0:T(8,128)S(1)} %get-tuple-element.28.extra_in_ref, f32[8,128]{1,0:T(8,128)S(1)} %get-tuple-element.29.extra_out_ref, bf16[512,256]{1,0:T(8,128)(2,1)S(1)} %copy-done.3, ...), custom_call_target="tpu_custom_call" | custom-call | flops 5905580032 | bytes 1613824 | tf_op jit(solution)/shard_map/invert/pallas_call | solution.py:312
  (3 shorter events, 0.1 us)
Async XLA Ops:
  0.0 17.9 %collective-permute-start = (bf16[512,256]{1,0:T(8,128)(2,1)}, bf16[512,256]{1,0:T(8,128)(2,1)S(1)}, u32[]{:S(2)}, u32[]{:S(2)}) collective-permute-start(bf16[512,256]{1,0:T(8,128)(2,1)} %own_ref.1), channel_id=1, source_target_pairs={{0,32},{32,0},{64,96},{96,64},{128,160},{160,128},{192,224},{224,1... | collective-permute-start | bytes 786440 | tf_op jit(solution)/shard_map/ppermute | solution.py:344
  4.0 1.2 %copy-start = (bf16[1024,512]{1,0:T(8,128)(2,1)S(1)}, bf16[1024,512]{1,0:T(8,128)(2,1)}, u32[]{:S(2)}) copy-start(bf16[1024,512]{1,0:T(8,128)(2,1)} %data_ref.1) | copy-start | bytes 3145732
  5.3 0.9 %copy-start.1 = (bf16[512,256]{1,0:T(8,128)(2,1)S(1)}, bf16[512,256]{1,0:T(8,128)(2,1)}, u32[]{:S(2)}) copy-start(bf16[512,256]{1,0:T(8,128)(2,1)} %own_ref.1) | copy-start | bytes 786436
  7.6 10.3 %copy-start.2 = (bf16[512,256]{1,0:T(8,128)(2,1)S(1)}, bf16[512,256]{1,0:T(8,128)(2,1)}, u32[]{:S(2)}) copy-start(bf16[512,256]{1,0:T(8,128)(2,1)} %own_ref.1) | copy-start | bytes 786436
  7.6 28.5 %all-to-all-start = ((f32[16,72,128]{2,1,0:T(8,128)}), f32[16,72,128]{2,1,0:T(8,128)S(1)}, u32[]{:S(2)}, u32[]{:S(2)}) async-start(f32[16,72,128]{2,1,0:T(8,128)} %gram_in.1), calls=%async_computation | async-start | bytes 1179648 | tf_op jit(solution)/shard_map/all_to_all | solution.py:329
  18.5 4.3 %collective-permute-start.1 = (f32[520,128]{1,0:T(8,128)S(1)}, f32[520,128]{1,0:T(8,128)S(1)}, u32[]{:S(2)}, u32[]{:S(2)}) collective-permute-start(f32[520,128]{1,0:T(8,128)S(1)} %get-tuple-element.19), channel_id=1, source_target_pairs={{0,1},{1,0},{2,3},{3,2},{4,5},{5,4},{6,7},{7,6},{8,9},{9,8},{10,11... | collective-permute-start | bytes 798728 | tf_op jit(solution)/shard_map/ppermute | solution.py:334
  22.9 7.9 %collective-permute-start.2 = (f32[264,128]{1,0:T(8,128)S(1)}, f32[264,128]{1,0:T(8,128)S(1)}, u32[]{:S(2)}, u32[]{:S(2)}) collective-permute-start(f32[264,128]{1,0:T(8,128)S(1)} %get-tuple-element.21), channel_id=1, source_target_pairs={{0,24},{1,25},{2,26},{3,27},{4,28},{5,29},{6,30},{7,31},{8,16},{9,... | collective-permute-start | bytes 405512 | tf_op jit(solution)/shard_map/ppermute | solution.py:339
  30.8 5.3 %collective-permute-start.3 = (f32[136,128]{1,0:T(8,128)S(1)}, f32[136,128]{1,0:T(8,128)S(1)}, u32[]{:S(2)}, u32[]{:S(2)}) collective-permute-start(f32[136,128]{1,0:T(8,128)S(1)} %get-tuple-element.23), channel_id=1, source_target_pairs={{0,8},{1,9},{2,10},{3,11},{4,12},{5,13},{6,14},{7,15},{8,0},{9,1},... | collective-permute-start | bytes 208904 | tf_op jit(solution)/shard_map/ppermute | solution.py:339
  36.9 11.8 %collective-permute-start.4 = (f32[136,128]{1,0:T(8,128)S(1)}, f32[136,128]{1,0:T(8,128)S(1)}, u32[]{:S(2)}, u32[]{:S(2)}) collective-permute-start(f32[136,128]{1,0:T(8,128)S(1)} %get-tuple-element.25.left_ref), channel_id=1, source_target_pairs={{0,2},{1,3},{2,0},{3,1},{4,6},{5,7},{6,4},{7,5},{8,10},{9,11},{10,... | collective-permute-start | bytes 208904 | tf_op jit(solution)/shard_map/ppermute | solution.py:339
  41.1 19.8 %all-to-all-start.1 = ((bf16[16,64,128]{2,1,0:T(8,128)(2,1)}), bf16[16,64,128]{2,1,0:T(8,128)(2,1)S(1)}, u32[]{:S(2)}, u32[]{:S(2)}) async-start(bf16[16,64,128]{2,1,0:T(8,128)(2,1)} %get-tuple-element.24), calls=%async_computation.1 | async-start | bytes 524288 | tf_op jit(solution)/shard_map/all_to_all | solution.py:329
  48.7 8.1 %copy-start.3 = (bf16[512,256]{1,0:T(8,128)(2,1)S(1)}, bf16[512,256]{1,0:T(8,128)(2,1)}, u32[]{:S(2)}) copy-start(bf16[512,256]{1,0:T(8,128)(2,1)} %weight_ref.1) | copy-start | bytes 786436
  48.7 7.4 %collective-permute-start.5 = (f32[136,128]{1,0:T(8,128)S(1)}, f32[136,128]{1,0:T(8,128)S(1)}, u32[]{:S(2)}, u32[]{:S(2)}) collective-permute-start(f32[136,128]{1,0:T(8,128)S(1)} %add_y.1.left_ref), channel_id=1, source_target_pairs={{0,6},{1,7},{2,4},{3,5},{4,2},{5,3},{6,0},{7,1},{8,14},{9,15},{10,... | collective-permute-start | bytes 208904 | tf_op jit(solution)/shard_map/ppermute | solution.py:339
  56.8 19.0 %collective-permute-start.6 = (bf16[512,256]{1,0:T(8,128)(2,1)S(1)}, bf16[512,256]{1,0:T(8,128)(2,1)S(1)}, u32[]{:S(2)}, u32[]{:S(2)}) collective-permute-start(bf16[512,256]{1,0:T(8,128)(2,1)S(1)} %copy-done.3), channel_id=1, source_target_pairs={{0,32},{32,0},{64,96},{96,64},{128,160},{160,128},{192,224},{224,1... | collective-permute-start | bytes 786440 | tf_op jit(solution)/shard_map/ppermute | solution.py:344
  60.9 14.9 %all-to-all-start.2 = ((bf16[8,144,128]{2,1,0:T(8,128)(2,1)}), bf16[8,144,128]{2,1,0:T(8,128)(2,1)S(1)}, u32[]{:S(2)}, u32[]{:S(2)}) async-start(bf16[8,144,128]{2,1,0:T(8,128)(2,1)} %get-tuple-element.27), calls=%async_computation.2 | async-start | bytes 589824 | tf_op jit(solution)/shard_map/all_to_all | solution.py:329

commit v5 on v4

--- a/solution.py
+++ b/solution.py
@@ -11,6 +11,7 @@
 DAMP_ROOT = 0.1
 TILE = 128
 CORES = 2
+CHUNKS = 4
 RING = 4
 EXTRA = 8
 EXTRA_HALF = 16
@@ -30,26 +31,21 @@
     return rows, cols
 
 
-def gram_tiles(left, right, scale):
-    return scale * lax.dot_general(
-        left, right, (((0,), (0,)), ((), ())), preferred_element_type=jnp.float32
-    )
-
-
-def packed_gram(data_ref, scale, store):
-    width = data_ref.shape[1]
-    count = width // TILE
-    half = width // 2
-    low, high = data_ref[:, :half], data_ref[:, half:]
-    parts = {
-        (0, 0): gram_tiles(low, low, scale),
-        (0, 1): gram_tiles(low, high, scale),
-        (1, 1): gram_tiles(high, high, scale),
-    }
-    per = count // 2
+def gram_parts(data):
+    half = data.shape[1] // 2
+    low, high = data[:, :half], data[:, half:]
+    return [
+        lax.dot_general(left, right, (((0,), (0,)), ((), ())), preferred_element_type=jnp.float32)
+        for left, right in ((low, low), (low, high), (high, high))
+    ]
+
+
+def pack_gram(quarters, store):
+    per = quarters[0].shape[0] // TILE
+    count = 2 * per
 
     def tile(i, j):
-        part = parts[(i // per, j // per)]
+        part = quarters[i // per + j // per]
         r, c = (i % per) * TILE, (j % per) * TILE
         return part[r : r + TILE, c : c + TILE]
 
@@ -100,10 +96,26 @@
     return jnp.sum(jnp.sum(value, axis=1, keepdims=True), axis=0, keepdims=True)
 
 
-def gram_in_kernel(tokens, data_ref, grads_ref, out_ref):
+def gram_in_kernel(tokens, data_hbm, grads_hbm, out_ref, data_ref, grads_ref, parts_ref, sems):
     pieces, piece_rows = out_ref.shape[0], out_ref.shape[1] - EXTRA
     per_tile = TILE // piece_rows
     scale = 1.0 / tokens
+    rows = data_ref.shape[0] // CHUNKS
+    copies = []
+    for chunk in range(CHUNKS):
+        place = pl.ds(chunk * rows, rows)
+        copies.append(
+            pltpu.make_async_copy(data_hbm.at[place], data_ref.at[place], sems.at[chunk])
+        )
+    copies.append(pltpu.make_async_copy(grads_hbm, grads_ref, sems.at[CHUNKS]))
+    for copy in copies:
+        copy.start()
+    for chunk in range(CHUNKS):
+        copies[chunk].wait()
+        part = gram_parts(data_ref[chunk * rows : (chunk + 1) * rows, :])
+        for position, value in enumerate(part):
+            parts_ref[position] = value if chunk == 0 else parts_ref[position] + value
+    copies[CHUNKS].wait()
 
     def store(position, value):
         for part in range(per_tile):
@@ -111,7 +123,7 @@
                 part * piece_rows : (part + 1) * piece_rows
             ]
 
-    diagonal = packed_gram(data_ref, scale, store)
+    diagonal = pack_gram([scale * parts_ref[position] for position in range(3)], store)
     grads = grads_ref[...].astype(jnp.float32)
     energy = total_of(grads * grads) * scale
     filler = jnp.zeros((EXTRA - diagonal.shape[0] - 1, TILE), jnp.float32)
@@ -132,7 +144,8 @@
     def store(position, value):
         packed_ref[position * TILE : (position + 1) * TILE, :] = value
 
-    diagonal = packed_gram(data_ref, 1.0 / tokens, store)
+    scale = 1.0 / tokens
+    diagonal = pack_gram([scale * part for part in gram_parts(data_ref[...])], store)
     filler = jnp.zeros((EXTRA - diagonal.shape[0], TILE), jnp.float32)
     extra = jnp.concatenate([diagonal, filler], axis=0)
     share = keep_ref.shape[0] - EXTRA
@@ -154,6 +167,10 @@
         place = pl.ds(pl.multiple_of(owner * rows, rows), rows)
         ref[:rows, :] = left_ref[place, :] + right_ref[place, :]
         ref[rows:, :] = extra
+
+
+def stage_kernel(after_ref, value_ref, out_ref):
+    out_ref[...] = value_ref[...]
 
 
 def add_kernel(left_ref, right_ref, out_ref):
@@ -281,7 +298,7 @@
                 moved = product.astype(jnp.float32) * factor
                 iterate[place] = (twice - moved) if i == j else -moved
 
-    def sweep(step, carry):
+    for _ in range(ITERS - 1):
         currents = [iterate[...].astype(jnp.bfloat16) for _, iterate, _ in chains]
         products = [
             jnp.dot(damped[...], current, preferred_element_type=jnp.float32).astype(jnp.bfloat16)
@@ -291,9 +308,6 @@
             iterate[...] = 2.0 * iterate[...] - jnp.dot(
                 product, current, preferred_element_type=jnp.float32
             )
-        return carry
-
-    lax.fori_loop(0, ITERS - 1, sweep, 0)
     inverse_in = iterate_in_ref[...].astype(jnp.bfloat16)
     left = jnp.dot(inverse_in, weight_block_ref[...], preferred_element_type=jnp.float32)
     right = iterate_out_ref[:, own_column].astype(jnp.bfloat16)
@@ -305,14 +319,14 @@
 VMEM_SPEC = pl.BlockSpec(memory_space=pltpu.VMEM)
 
 
-def local_call(kernel, name, operands, outs, scratch=(), flops=0):
+def local_call(kernel, name, operands, outs, scratch=(), flops=0, space=pltpu.VMEM):
     multiple = isinstance(outs, tuple)
     listed = outs if multiple else (outs,)
     moved = sum(a.size * a.dtype.itemsize for a in operands + tuple(listed))
     return pl.pallas_call(
         kernel,
         out_shape=outs,
-        in_specs=[VMEM_SPEC] * len(operands),
+        in_specs=[pl.BlockSpec(memory_space=space)] * len(operands),
         out_specs=tuple([VMEM_SPEC] * len(listed)) if multiple else VMEM_SPEC,
         scratch_shapes=list(scratch),
         compiler_params=pltpu.CompilerParams(vmem_limit_bytes=VMEM_LIMIT),
@@ -363,7 +377,14 @@
         "gram_in",
         (activations, output_grads),
         shape_of(groups, in_rows + EXTRA, TILE),
+        scratch=[
+            pltpu.VMEM(activations.shape, half_type),
+            pltpu.VMEM(output_grads.shape, half_type),
+            pltpu.VMEM((3, width // 2, width // 2), jnp.float32),
+            pltpu.SemaphoreType.DMA((CHUNKS + 1,)),
+        ],
         flops=2 * activations.shape[0] * width * width,
+        space=pl.ANY,
     )
     got_in = exchange(send_in, "grp")
 
@@ -389,6 +410,14 @@
             (keep, swap(give)),
             (shape_of(rows + EXTRA, TILE),) * 2,
         )
+    sent_weight = local_call(
+        stage_kernel,
+        "stage_weight",
+        (keep, grad_weight),
+        shape_of(*grad_weight.shape, dtype=half_type),
+        flops=LATE_START,
+    )
+    other_weight = swap_half(sent_weight)
     to_all_in, extra_in, part_y = local_call(
         functools.partial(sum_both_kernel, count),
         "sum_both",
@@ -420,12 +449,10 @@
         [x * x_stride + y * y_stride + core for x in range(RING) for core in range(CORES)]
         for y in range(RING)
     ]
-    sent_weight, to_all_out = lax.optimization_barrier((grad_weight, to_all_out))
-    other_weight = swap_half(sent_weight)
     all_out = exchange(to_all_out, "blk", same_y)
 
     block = (width, width)
-    damped_in = local_call(unpack_in_kernel, "unpack_in", (all_in,), shape_of(*block, dtype=half_type))
+    damped_in = local_call(unpack_in_kernel, "unpack_in", (all_in,), shape_of(*block, dtype=half_type), flops=LATE_START)
     return local_call(
         invert_kernel,
         "invert",

time: 84.9 us -> 81.9 us (0.965)
  waiting for transfers between devices: 16.6 us -> 14.7 us
  starting transfers between devices: 53.1 us -> 52 us
    ppermute x4, waiting for transfers between devices: 8.82 us -> 6.93 us  [swap_along(): return lax.ppermute(value, 'blk', pairs)]
    pallas_call x9 -> x10, Pallas kernels: 12.1 us -> 12.1 us  [local_call(): pl.pallas_call(kernel, out_shape=outs, in_specs=[pl.BlockSpec(memory_spac...]
  transfers between devices with their start and end apart: 10 -> 10, of which waited for: 5 -> 4; matrix products, arithmetic and copies ran while one was open for 0% -> 0% of each run, Pallas kernels for 4% -> 5%
where the time goes in v5:
time: 81.9 us; the launch traced here: 81.2 us
  starting transfers between devices  52 us (63%)
  waiting for transfers between devices  14.7 us (18%)
  Pallas kernels  12.1 us (15%)
  local copies, waits for them, and re-layouts  2.18 us (3%)
    all_to_all x3, starting transfers between devices, exchange(): lax.all_to_all(value, axis, 0, 0, tiled=True, axis_index_groups=groups)  25.6 us
    ppermute x4, starting transfers between devices, swap_along(): return lax.ppermute(value, 'blk', pairs)  16 us
    pallas_call x10, Pallas kernels, local_call(): pl.pallas_call(kernel, out_shape=outs, in_specs=[pl.BlockSpec(memory_spac...  12.1 us
    ppermute x2, starting transfers between devices, swap_half(): return lax.ppermute(value, 'grp', pairs)  7.29 us
    ppermute x4, waiting for transfers between devices, swap_along(): return lax.ppermute(value, 'blk', pairs)  6.93 us
    all_to_all x3, waiting for transfers between devices, exchange(): lax.all_to_all(value, axis, 0, 0, tiled=True, axis_index_groups=groups)  6.66 us
    ppermute x1, starting transfers between devices, swap_core(): return lax.ppermute(value, 'blk', pairs)  3.14 us
    unnamed x8, local copies, waits for them, and re-layouts  2.18 us
  transfers between devices with their start and end apart: 10, of which 4 were waited for; matrix products, arithmetic and copies ran while one was open for 0% of the time, Pallas kernels for 5%

profile of v5, /device:TPU:1, one launch (start us, length us, event | category | flops | bytes accessed | tf_op | source)
XLA Modules:
  0.0 81.2 jit_solution(10213507591084278505)
XLA Ops:
  0.0 4.0 %collective-permute-start = (bf16[512,256]{1,0:T(8,128)(2,1)}, bf16[512,256]{1,0:T(8,128)(2,1)S(1)}, u32[]{:S(2)}, u32[]{:S(2)}) collective-permute-start(bf16[512,256]{1,0:T(8,128)(2,1)} %own_ref.1), channel_id=1, source_target_pairs={{0,32},{32,0},{64,96},{96,64},{128,160},{160,128},{192,224},{224,1... | collective-permute-start | bytes 786440 | tf_op jit(solution)/shard_map/ppermute | solution.py:358
  4.0 0.0 copy-start
  4.0 1.2 %copy-done = bf16[1024,512]{1,0:T(8,128)(2,1)S(1)} copy-done((bf16[1024,512]{1,0:T(8,128)(2,1)S(1)}, bf16[1024,512]{1,0:T(8,128)(2,1)}, u32[]{:S(2)}) %copy-start) | copy-done | bytes 1048600
  5.3 0.0 copy-start.1
  5.3 0.9 %copy-done.1 = bf16[512,256]{1,0:T(8,128)(2,1)S(1)} copy-done((bf16[512,256]{1,0:T(8,128)(2,1)S(1)}, bf16[512,256]{1,0:T(8,128)(2,1)}, u32[]{:S(2)}) %copy-start.1) | copy-done | bytes 262168
  6.2 2.3 %gram_in.1 = f32[16,72,128]{2,1,0:T(8,128)} custom-call(bf16[1024,512]{1,0:T(8,128)(2,1)S(1)} %copy-done, bf16[512,256]{1,0:T(8,128)(2,1)S(1)} %copy-done.1), custom_call_target="tpu_custom_call" | custom-call | flops 536870912 | bytes 1900544 | tf_op jit(solution)/shard_map/gram_in/pallas_call | solution.py:326
  8.5 0.0 copy-start.2
  8.5 10.3 %all-to-all-start = ((f32[16,72,128]{2,1,0:T(8,128)}), f32[16,72,128]{2,1,0:T(8,128)S(1)}, u32[]{:S(2)}, u32[]{:S(2)}) async-start(f32[16,72,128]{2,1,0:T(8,128)} %gram_in.1), calls=%async_computation | async-start | bytes 1179648 | tf_op jit(solution)/shard_map/all_to_all | solution.py:343
  18.8 0.0 collective-permute-done.other_ref
  18.8 0.0 copy-done.2
  18.8 0.6 gram_out.1
  19.4 3.1 %collective-permute-start.1 = (f32[520,128]{1,0:T(8,128)S(1)}, f32[520,128]{1,0:T(8,128)S(1)}, u32[]{:S(2)}, u32[]{:S(2)}) collective-permute-start(f32[520,128]{1,0:T(8,128)S(1)} %get-tuple-element.17), channel_id=1, source_target_pairs={{0,1},{1,0},{2,3},{3,2},{4,5},{5,4},{6,7},{7,6},{8,9},{9,8},{10,11... | collective-permute-start | bytes 798728 | tf_op jit(solution)/shard_map/ppermute | solution.py:348
  22.5 1.1 %collective-permute-done.1.right_ref = f32[520,128]{1,0:T(8,128)S(1)} collective-permute-done((f32[520,128]{1,0:T(8,128)S(1)}, f32[520,128]{1,0:T(8,128)S(1)}, u32[]{:S(2)}, u32[]{:S(2)}) %collective-permute-start.1) | collective-permute-done | bytes 266272 | tf_op jit(solution)/shard_map/ppermute | solution.py:348
  23.7 4.4 %collective-permute-start.2 = (f32[264,128]{1,0:T(8,128)S(1)}, f32[264,128]{1,0:T(8,128)S(1)}, u32[]{:S(2)}, u32[]{:S(2)}) collective-permute-start(f32[264,128]{1,0:T(8,128)S(1)} %get-tuple-element.19), channel_id=1, source_target_pairs={{0,24},{1,25},{2,26},{3,27},{4,28},{5,29},{6,30},{7,31},{8,16},{9,... | collective-permute-start | bytes 405512 | tf_op jit(solution)/shard_map/ppermute | solution.py:353
  28.1 3.5 %collective-permute-done.2.right_ref = f32[264,128]{1,0:T(8,128)S(1)} collective-permute-done((f32[264,128]{1,0:T(8,128)S(1)}, f32[264,128]{1,0:T(8,128)S(1)}, u32[]{:S(2)}, u32[]{:S(2)}) %collective-permute-start.2) | collective-permute-done | bytes 135200 | tf_op jit(solution)/shard_map/ppermute | solution.py:353
  31.7 1.9 %collective-permute-start.3 = (f32[136,128]{1,0:T(8,128)S(1)}, f32[136,128]{1,0:T(8,128)S(1)}, u32[]{:S(2)}, u32[]{:S(2)}) collective-permute-start(f32[136,128]{1,0:T(8,128)S(1)} %get-tuple-element.21), channel_id=1, source_target_pairs={{0,8},{1,9},{2,10},{3,11},{4,12},{5,13},{6,14},{7,15},{8,0},{9,1},... | collective-permute-start | bytes 208904 | tf_op jit(solution)/shard_map/ppermute | solution.py:353
  33.6 3.4 %collective-permute-done.3.right_ref = f32[136,128]{1,0:T(8,128)S(1)} collective-permute-done((f32[136,128]{1,0:T(8,128)S(1)}, f32[136,128]{1,0:T(8,128)S(1)}, u32[]{:S(2)}, u32[]{:S(2)}) %collective-permute-start.3) | collective-permute-done | bytes 69664 | tf_op jit(solution)/shard_map/ppermute | solution.py:353
  37.0 0.0 all-to-all-done.got_ref
  37.0 0.8 sum_both.1
  37.8 4.2 %collective-permute-start.4 = (f32[136,128]{1,0:T(8,128)S(1)}, f32[136,128]{1,0:T(8,128)S(1)}, u32[]{:S(2)}, u32[]{:S(2)}) collective-permute-start(f32[136,128]{1,0:T(8,128)S(1)} %get-tuple-element.23.left_ref), channel_id=1, source_target_pairs={{0,2},{1,3},{2,0},{3,1},{4,6},{5,7},{6,4},{7,5},{8,10},{9,11},{10,... | collective-permute-start | bytes 208904 | tf_op jit(solution)/shard_map/ppermute | solution.py:353
  42.0 7.5 %all-to-all-start.1 = ((bf16[16,64,128]{2,1,0:T(8,128)(2,1)}), bf16[16,64,128]{2,1,0:T(8,128)(2,1)S(1)}, u32[]{:S(2)}, u32[]{:S(2)}) async-start(bf16[16,64,128]{2,1,0:T(8,128)(2,1)} %get-tuple-element.22), calls=%async_computation.1 | async-start | bytes 524288 | tf_op jit(solution)/shard_map/all_to_all | solution.py:343
  49.5 0.0 copy-start.3
  49.5 0.0 collective-permute-done.4.right_ref
  49.6 5.5 %collective-permute-start.5 = (f32[136,128]{1,0:T(8,128)S(1)}, f32[136,128]{1,0:T(8,128)S(1)}, u32[]{:S(2)}, u32[]{:S(2)}) collective-permute-start(f32[136,128]{1,0:T(8,128)S(1)} %add_y.1.left_ref), channel_id=1, source_target_pairs={{0,6},{1,7},{2,4},{3,5},{4,2},{5,3},{6,0},{7,1},{8,14},{9,15},{10,... | collective-permute-start | bytes 208904 | tf_op jit(solution)/shard_map/ppermute | solution.py:353
  55.0 0.0 copy-done.3
  55.1 3.3 %collective-permute-start.6 = (bf16[512,256]{1,0:T(8,128)(2,1)S(1)}, bf16[512,256]{1,0:T(8,128)(2,1)S(1)}, u32[]{:S(2)}, u32[]{:S(2)}) collective-permute-start(bf16[512,256]{1,0:T(8,128)(2,1)S(1)} %stage_weight.1), channel_id=1, source_target_pairs={{0,32},{32,0},{64,96},{96,64},{128,160},{160,128},{192,224},{224,1... | collective-permute-start | bytes 786440 | tf_op jit(solution)/shard_map/ppermute | solution.py:358
  58.3 0.0 collective-permute-done.5.right_ref
  58.4 0.7 sum_y.1
  59.1 0.0 all-to-all-done.1.got_ref
  59.1 7.8 %all-to-all-start.2 = ((bf16[8,144,128]{2,1,0:T(8,128)(2,1)}), bf16[8,144,128]{2,1,0:T(8,128)(2,1)S(1)}, u32[]{:S(2)}, u32[]{:S(2)}) async-start(bf16[8,144,128]{2,1,0:T(8,128)(2,1)} %get-tuple-element.24), calls=%async_computation.2 | async-start | bytes 589824 | tf_op jit(solution)/shard_map/all_to_all | solution.py:343
  66.9 0.1 unpack_in.1.damped_in_ref
  67.0 0.0 collective-permute-done.6.other_weight_ref
  67.1 6.7 %all-to-all-done.2.got_out_ref = bf16[8,144,128]{2,1,0:T(8,128)(2,1)S(1)} async-done(((bf16[8,144,128]{2,1,0:T(8,128)(2,1)}), bf16[8,144,128]{2,1,0:T(8,128)(2,1)S(1)}, u32[]{:S(2)}, u32[]{:S(2)}) %all-to-all-start.2) | async-done | bytes 294944 | tf_op jit(solution)/shard_map/all_to_all | solution.py:343
  73.7 7.5 %invert.1 = bf16[512,256]{1,0:T(8,128)(2,1)} custom-call(bf16[512,512]{1,0:T(8,128)(2,1)S(1)} %unpack_in.1.damped_in_ref, bf16[8,144,128]{2,1,0:T(8,128)(2,1)S(1)} %all-to-all-done.2.got_out_ref, f32[8,128]{1,0:T(8,128)S(1)} %get-tuple-element.25.extra_in_ref, f32[8,128]{1,0:T(8,128)S(1)} %get-tuple-element.26.extra_out_ref, bf16[512,256]{1,0:T(8,128)(2,1)S(1)} %copy-done.3, ...), custom_call_target="tpu_custom_call" | custom-call | flops 5905580032 | bytes 1613824 | tf_op jit(solution)/shard_map/invert/pallas_call | solution.py:326
  (4 shorter events, 0.1 us)
Async XLA Ops:
  0.0 18.8 %collective-permute-start = (bf16[512,256]{1,0:T(8,128)(2,1)}, bf16[512,256]{1,0:T(8,128)(2,1)S(1)}, u32[]{:S(2)}, u32[]{:S(2)}) collective-permute-start(bf16[512,256]{1,0:T(8,128)(2,1)} %own_ref.1), channel_id=1, source_target_pairs={{0,32},{32,0},{64,96},{96,64},{128,160},{160,128},{192,224},{224,1... | collective-permute-start | bytes 786440 | tf_op jit(solution)/shard_map/ppermute | solution.py:358
  4.0 1.2 %copy-start = (bf16[1024,512]{1,0:T(8,128)(2,1)S(1)}, bf16[1024,512]{1,0:T(8,128)(2,1)}, u32[]{:S(2)}) copy-start(bf16[1024,512]{1,0:T(8,128)(2,1)} %data_hbm.1) | copy-start | bytes 3145732
  5.3 0.9 %copy-start.1 = (bf16[512,256]{1,0:T(8,128)(2,1)S(1)}, bf16[512,256]{1,0:T(8,128)(2,1)}, u32[]{:S(2)}) copy-start(bf16[512,256]{1,0:T(8,128)(2,1)} %own_ref.1) | copy-start | bytes 786436
  8.5 10.3 %copy-start.2 = (bf16[512,256]{1,0:T(8,128)(2,1)S(1)}, bf16[512,256]{1,0:T(8,128)(2,1)}, u32[]{:S(2)}) copy-start(bf16[512,256]{1,0:T(8,128)(2,1)} %own_ref.1) | copy-start | bytes 786436
  8.5 28.5 %all-to-all-start = ((f32[16,72,128]{2,1,0:T(8,128)}), f32[16,72,128]{2,1,0:T(8,128)S(1)}, u32[]{:S(2)}, u32[]{:S(2)}) async-start(f32[16,72,128]{2,1,0:T(8,128)} %gram_in.1), calls=%async_computation | async-start | bytes 1179648 | tf_op jit(solution)/shard_map/all_to_all | solution.py:343
  19.4 4.3 %collective-permute-start.1 = (f32[520,128]{1,0:T(8,128)S(1)}, f32[520,128]{1,0:T(8,128)S(1)}, u32[]{:S(2)}, u32[]{:S(2)}) collective-permute-start(f32[520,128]{1,0:T(8,128)S(1)} %get-tuple-element.17), channel_id=1, source_target_pairs={{0,1},{1,0},{2,3},{3,2},{4,5},{5,4},{6,7},{7,6},{8,9},{9,8},{10,11... | collective-permute-start | bytes 798728 | tf_op jit(solution)/shard_map/ppermute | solution.py:348
  23.7 7.9 %collective-permute-start.2 = (f32[264,128]{1,0:T(8,128)S(1)}, f32[264,128]{1,0:T(8,128)S(1)}, u32[]{:S(2)}, u32[]{:S(2)}) collective-permute-start(f32[264,128]{1,0:T(8,128)S(1)} %get-tuple-element.19), channel_id=1, source_target_pairs={{0,24},{1,25},{2,26},{3,27},{4,28},{5,29},{6,30},{7,31},{8,16},{9,... | collective-permute-start | bytes 405512 | tf_op jit(solution)/shard_map/ppermute | solution.py:353
  31.7 5.3 %collective-permute-start.3 = (f32[136,128]{1,0:T(8,128)S(1)}, f32[136,128]{1,0:T(8,128)S(1)}, u32[]{:S(2)}, u32[]{:S(2)}) collective-permute-start(f32[136,128]{1,0:T(8,128)S(1)} %get-tuple-element.21), channel_id=1, source_target_pairs={{0,8},{1,9},{2,10},{3,11},{4,12},{5,13},{6,14},{7,15},{8,0},{9,1},... | collective-permute-start | bytes 208904 | tf_op jit(solution)/shard_map/ppermute | solution.py:353
  37.8 11.8 %collective-permute-start.4 = (f32[136,128]{1,0:T(8,128)S(1)}, f32[136,128]{1,0:T(8,128)S(1)}, u32[]{:S(2)}, u32[]{:S(2)}) collective-permute-start(f32[136,128]{1,0:T(8,128)S(1)} %get-tuple-element.23.left_ref), channel_id=1, source_target_pairs={{0,2},{1,3},{2,0},{3,1},{4,6},{5,7},{6,4},{7,5},{8,10},{9,11},{10,... | collective-permute-start | bytes 208904 | tf_op jit(solution)/shard_map/ppermute | solution.py:353
  42.0 17.1 %all-to-all-start.1 = ((bf16[16,64,128]{2,1,0:T(8,128)(2,1)}), bf16[16,64,128]{2,1,0:T(8,128)(2,1)S(1)}, u32[]{:S(2)}, u32[]{:S(2)}) async-start(bf16[16,64,128]{2,1,0:T(8,128)(2,1)} %get-tuple-element.22), calls=%async_computation.1 | async-start | bytes 524288 | tf_op jit(solution)/shard_map/all_to_all | solution.py:343
  49.5 5.5 %copy-start.3 = (bf16[512,256]{1,0:T(8,128)(2,1)S(1)}, bf16[512,256]{1,0:T(8,128)(2,1)}, u32[]{:S(2)}) copy-start(bf16[512,256]{1,0:T(8,128)(2,1)} %weight_ref.1) | copy-start | bytes 786436
  49.6 8.8 %collective-permute-start.5 = (f32[136,128]{1,0:T(8,128)S(1)}, f32[136,128]{1,0:T(8,128)S(1)}, u32[]{:S(2)}, u32[]{:S(2)}) collective-permute-start(f32[136,128]{1,0:T(8,128)S(1)} %add_y.1.left_ref), channel_id=1, source_target_pairs={{0,6},{1,7},{2,4},{3,5},{4,2},{5,3},{6,0},{7,1},{8,14},{9,15},{10,... | collective-permute-start | bytes 208904 | tf_op jit(solution)/shard_map/ppermute | solution.py:353
  55.1 12.0 %collective-permute-start.6 = (bf16[512,256]{1,0:T(8,128)(2,1)S(1)}, bf16[512,256]{1,0:T(8,128)(2,1)S(1)}, u32[]{:S(2)}, u32[]{:S(2)}) collective-permute-start(bf16[512,256]{1,0:T(8,128)(2,1)S(1)} %stage_weight.1), channel_id=1, source_target_pairs={{0,32},{32,0},{64,96},{96,64},{128,160},{160,128},{192,224},{224,1... | collective-permute-start | bytes 786440 | tf_op jit(solution)/shard_map/ppermute | solution.py:358
  59.1 14.6 %all-to-all-start.2 = ((bf16[8,144,128]{2,1,0:T(8,128)(2,1)}), bf16[8,144,128]{2,1,0:T(8,128)(2,1)S(1)}, u32[]{:S(2)}, u32[]{:S(2)}) async-start(bf16[8,144,128]{2,1,0:T(8,128)(2,1)} %get-tuple-element.24), calls=%async_computation.2 | async-start | bytes 589824 | tf_op jit(solution)/shard_map/all_to_all | solution.py:343

commit v6 on v5

--- a/solution.py
+++ b/solution.py
@@ -11,12 +11,13 @@
 DAMP_ROOT = 0.1
 TILE = 128
 CORES = 2
-CHUNKS = 4
+CHUNKS = 2
 RING = 4
 EXTRA = 8
 EXTRA_HALF = 16
 LATE_START = 10**10
 VMEM_LIMIT = 48 * 1024 * 1024
+GRAM_LIMIT = 58 * 1024 * 1024
 
 
 def tile_plan(count):
@@ -96,7 +97,7 @@
     return jnp.sum(jnp.sum(value, axis=1, keepdims=True), axis=0, keepdims=True)
 
 
-def gram_in_kernel(tokens, data_hbm, grads_hbm, out_ref, data_ref, grads_ref, parts_ref, sems):
+def gram_in_kernel(tokens, data_hbm, grads_hbm, out_ref, data_ref, grads_ref, sems):
     pieces, piece_rows = out_ref.shape[0], out_ref.shape[1] - EXTRA
     per_tile = TILE // piece_rows
     scale = 1.0 / tokens
@@ -108,14 +109,15 @@
             pltpu.make_async_copy(data_hbm.at[place], data_ref.at[place], sems.at[chunk])
         )
     copies.append(pltpu.make_async_copy(grads_hbm, grads_ref, sems.at[CHUNKS]))
-    for copy in copies:
+    for copy in reversed(copies):
         copy.start()
+    copies[CHUNKS].wait()
+    grads = grads_ref[...].astype(jnp.float32)
+    energy = total_of(grads * grads) * scale
     for chunk in range(CHUNKS):
         copies[chunk].wait()
         part = gram_parts(data_ref[chunk * rows : (chunk + 1) * rows, :])
-        for position, value in enumerate(part):
-            parts_ref[position] = value if chunk == 0 else parts_ref[position] + value
-    copies[CHUNKS].wait()
+        quarters = part if chunk == 0 else [old + new for old, new in zip(quarters, part)]
 
     def store(position, value):
         for part in range(per_tile):
@@ -123,9 +125,7 @@
                 part * piece_rows : (part + 1) * piece_rows
             ]
 
-    diagonal = pack_gram([scale * parts_ref[position] for position in range(3)], store)
-    grads = grads_ref[...].astype(jnp.float32)
-    energy = total_of(grads * grads) * scale
+    diagonal = pack_gram([scale * quarter for quarter in quarters], store)
     filler = jnp.zeros((EXTRA - diagonal.shape[0] - 1, TILE), jnp.float32)
     extra = jnp.concatenate(
         [diagonal, jnp.broadcast_to(energy, (1, TILE)), filler], axis=0
@@ -223,7 +223,8 @@
     extra_ref[...] = extra
 
 
-def unpack_in_kernel(got_ref, out_ref):
+def unpack_in_kernel(got_ref, weight_ref, out_ref, sent_ref):
+    sent_ref[...] = weight_ref[...]
     rows = got_ref.shape[1]
     per_tile = TILE // rows
     unpack_block(
@@ -239,24 +240,19 @@
     got_out_ref,
     extra_in_ref,
     extra_out_ref,
-    weight_ref,
-    other_weight_ref,
-    result_ref,
+    inverse_ref,
+    right_ref,
     full_in_ref,
     damped_out_ref,
     iterate_in_ref,
     iterate_out_ref,
-    weight_block_ref,
 ):
     width = damped_in_ref.shape[0]
     count = width // TILE
-    half = weight_ref.shape[1]
+    half = right_ref.shape[1]
     parity = lax.axis_index("grp") % 2
     pieces, rows_out = got_out_ref.shape[0], got_out_ref.shape[1] - EXTRA_HALF
     own_column = pl.ds(pl.multiple_of(parity * half, half), half)
-    other_column = pl.ds(pl.multiple_of((1 - parity) * half, half), half)
-    weight_block_ref[:, own_column] = weight_ref[...]
-    weight_block_ref[:, other_column] = other_weight_ref[...]
 
     scalars = jnp.zeros((EXTRA_HALF, TILE), jnp.float32)
     for piece in range(pieces):
@@ -308,18 +304,26 @@
             iterate[...] = 2.0 * iterate[...] - jnp.dot(
                 product, current, preferred_element_type=jnp.float32
             )
-    inverse_in = iterate_in_ref[...].astype(jnp.bfloat16)
-    left = jnp.dot(inverse_in, weight_block_ref[...], preferred_element_type=jnp.float32)
-    right = iterate_out_ref[:, own_column].astype(jnp.bfloat16)
+    inverse_ref[...] = iterate_in_ref[...].astype(jnp.bfloat16)
+    right_ref[...] = iterate_out_ref[:, own_column].astype(jnp.bfloat16)
+
+
+def finish_kernel(inverse_ref, right_ref, weight_ref, other_weight_ref, result_ref, left_ref):
+    half = weight_ref.shape[1]
+    parity = lax.axis_index("grp") % 2
+    for ref, place in ((weight_ref, parity), (other_weight_ref, 1 - parity)):
+        left_ref[:, pl.ds(pl.multiple_of(place * half, half), half)] = jnp.dot(
+            inverse_ref[...], ref[...], preferred_element_type=jnp.float32
+        ).astype(jnp.bfloat16)
     result_ref[...] = jnp.dot(
-        left.astype(jnp.bfloat16), right, preferred_element_type=jnp.float32
+        left_ref[...], right_ref[...], preferred_element_type=jnp.float32
     ).astype(jnp.bfloat16)
 
 
 VMEM_SPEC = pl.BlockSpec(memory_space=pltpu.VMEM)
 
 
-def local_call(kernel, name, operands, outs, scratch=(), flops=0, space=pltpu.VMEM):
+def local_call(kernel, name, operands, outs, scratch=(), flops=0, space=pltpu.VMEM, limit=VMEM_LIMIT):
     multiple = isinstance(outs, tuple)
     listed = outs if multiple else (outs,)
     moved = sum(a.size * a.dtype.itemsize for a in operands + tuple(listed))
@@ -329,7 +333,7 @@
         in_specs=[pl.BlockSpec(memory_space=space)] * len(operands),
         out_specs=tuple([VMEM_SPEC] * len(listed)) if multiple else VMEM_SPEC,
         scratch_shapes=list(scratch),
-        compiler_params=pltpu.CompilerParams(vmem_limit_bytes=VMEM_LIMIT),
+        compiler_params=pltpu.CompilerParams(vmem_limit_bytes=limit),
         cost_estimate=pl.CostEstimate(flops=flops, bytes_accessed=moved, transcendentals=0),
         name=name,
     )(*operands)
@@ -380,11 +384,11 @@
         scratch=[
             pltpu.VMEM(activations.shape, half_type),
             pltpu.VMEM(output_grads.shape, half_type),
-            pltpu.VMEM((3, width // 2, width // 2), jnp.float32),
             pltpu.SemaphoreType.DMA((CHUNKS + 1,)),
         ],
         flops=2 * activations.shape[0] * width * width,
-        space=pl.ANY,
+        space=pltpu.HBM,
+        limit=GRAM_LIMIT,
     )
     got_in = exchange(send_in, "grp")
 
@@ -410,14 +414,6 @@
             (keep, swap(give)),
             (shape_of(rows + EXTRA, TILE),) * 2,
         )
-    sent_weight = local_call(
-        stage_kernel,
-        "stage_weight",
-        (keep, grad_weight),
-        shape_of(*grad_weight.shape, dtype=half_type),
-        flops=LATE_START,
-    )
-    other_weight = swap_half(sent_weight)
     to_all_in, extra_in, part_y = local_call(
         functools.partial(sum_both_kernel, count),
         "sum_both",
@@ -452,20 +448,37 @@
     all_out = exchange(to_all_out, "blk", same_y)
 
     block = (width, width)
-    damped_in = local_call(unpack_in_kernel, "unpack_in", (all_in,), shape_of(*block, dtype=half_type), flops=LATE_START)
-    return local_call(
+    all_in, extra_out = lax.optimization_barrier((all_in, extra_out))
+    damped_in, sent_weight = local_call(
+        unpack_in_kernel,
+        "unpack_in",
+        (all_in, grad_weight),
+        (shape_of(*block, dtype=half_type), shape_of(*grad_weight.shape, dtype=half_type)),
+    )
+    other_weight = swap_half(sent_weight)
+    extra_in = local_call(
+        stage_kernel, "stage_extra", (damped_in, extra_in), shape_of(*extra_in.shape), flops=LATE_START
+    )
+    inverse_in, right = local_call(
         invert_kernel,
         "invert",
-        (damped_in, all_out, extra_in, extra_out, grad_weight, other_weight),
-        shape_of(width, half, dtype=half_type),
+        (damped_in, all_out, extra_in, extra_out),
+        (shape_of(*block, dtype=half_type), shape_of(width, half, dtype=half_type)),
         scratch=[
             pltpu.VMEM(block, half_type),
             pltpu.VMEM(block, half_type),
             pltpu.VMEM(block, jnp.float32),
             pltpu.VMEM(block, jnp.float32),
-            pltpu.VMEM(block, half_type),
         ],
-        flops=2 * (4 * (ITERS - 1) + 2) * width * width * width,
+        flops=8 * (ITERS - 1) * width * width * width,
+    )
+    return local_call(
+        finish_kernel,
+        "finish",
+        (inverse_in, right, grad_weight, other_weight),
+        shape_of(width, half, dtype=half_type),
+        scratch=[pltpu.VMEM(block, half_type)],
+        flops=3 * width * width * width,
     )
 
 

time: 81.9 us -> 80.7 us (0.985)
  local copies, waits for them, and re-layouts: 2.18 us -> 0.01 us
  Pallas kernels: 12.1 us -> 13.1 us
    unnamed x8 -> x4, local copies, waits for them, and re-layouts: 2.18 us -> 0.01 us
    ppermute x4, waiting for transfers between devices: 6.93 us -> 8.83 us  [swap_along(): return lax.ppermute(value, 'blk', pairs)]
    all_to_all x3, waiting for transfers between devices: 6.66 us -> 4.92 us  [exchange(): lax.all_to_all(value, axis, 0, 0, tiled=True, axis_index_groups=groups)]
    pallas_call x10 -> x11, Pallas kernels: 12.1 us -> 13.1 us  [local_call(): pl.pallas_call(kernel, out_shape=outs, in_specs=[pl.BlockSpec(memory_spac...]
  transfers between devices with their start and end apart: 10 -> 10, of which waited for: 4 -> 6; matrix products, arithmetic and copies ran while one was open for 0% -> 0% of each run, Pallas kernels for 5% -> 14%
where the time goes in v6:
time: 80.7 us; the launch traced here: 80 us
  starting transfers between devices  51.9 us (64%)
  waiting for transfers between devices  14.9 us (18%)
  Pallas kernels  13.1 us (16%)
    all_to_all x3, starting transfers between devices, exchange(): lax.all_to_all(value, axis, 0, 0, tiled=True, axis_index_groups=groups)  26.1 us
    ppermute x4, starting transfers between devices, swap_along(): return lax.ppermute(value, 'blk', pairs)  15.8 us
    pallas_call x11, Pallas kernels, local_call(): pl.pallas_call(kernel, out_shape=outs, in_specs=[pl.BlockSpec(memory_spac...  13.1 us
    ppermute x4, waiting for transfers between devices, swap_along(): return lax.ppermute(value, 'blk', pairs)  8.83 us
    ppermute x2, starting transfers between devices, swap_half(): return lax.ppermute(value, 'grp', pairs)  6.77 us
    all_to_all x3, waiting for transfers between devices, exchange(): lax.all_to_all(value, axis, 0, 0, tiled=True, axis_index_groups=groups)  4.92 us
    ppermute x1, starting transfers between devices, swap_core(): return lax.ppermute(value, 'blk', pairs)  3.14 us
  transfers between devices with their start and end apart: 10, of which 6 were waited for; matrix products, arithmetic and copies ran while one was open for 0% of the time, Pallas kernels for 14%

profile of v6, /device:TPU:1, one launch (start us, length us, event | category | flops | bytes accessed | tf_op | source)
XLA Modules:
  0.0 80.0 jit_solution(3942481547129856013)
XLA Ops:
  0.0 4.0 %collective-permute-start = (bf16[512,256]{1,0:T(8,128)(2,1)}, bf16[512,256]{1,0:T(8,128)(2,1)S(1)}, u32[]{:S(2)}, u32[]{:S(2)}) collective-permute-start(bf16[512,256]{1,0:T(8,128)(2,1)} %own_ref.1), channel_id=1, source_target_pairs={{0,32},{32,0},{64,96},{96,64},{128,160},{160,128},{192,224},{224,1... | collective-permute-start | bytes 786440 | tf_op jit(solution)/shard_map/ppermute | solution.py:362
  4.0 2.8 %gram_in.1 = f32[16,72,128]{2,1,0:T(8,128)} custom-call(bf16[1024,512]{1,0:T(8,128)(2,1)} %data_hbm.1, bf16[512,256]{1,0:T(8,128)(2,1)} %own_ref.1), custom_call_target="tpu_custom_call" | custom-call | flops 536870912 | bytes 1900544 | tf_op jit(solution)/shard_map/gram_in/pallas_call | solution.py:330
  6.8 0.0 copy-start.1
  6.8 10.3 %all-to-all-start = ((f32[16,72,128]{2,1,0:T(8,128)}), f32[16,72,128]{2,1,0:T(8,128)S(1)}, u32[]{:S(2)}, u32[]{:S(2)}) async-start(f32[16,72,128]{2,1,0:T(8,128)} %gram_in.1), calls=%async_computation | async-start | bytes 1179648 | tf_op jit(solution)/shard_map/all_to_all | solution.py:347
  17.1 0.0 collective-permute-done.other_ref
  17.1 0.0 copy-done.1
  17.1 0.6 gram_out.1
  17.7 3.1 %collective-permute-start.1 = (f32[520,128]{1,0:T(8,128)S(1)}, f32[520,128]{1,0:T(8,128)S(1)}, u32[]{:S(2)}, u32[]{:S(2)}) collective-permute-start(f32[520,128]{1,0:T(8,128)S(1)} %get-tuple-element.23), channel_id=1, source_target_pairs={{0,1},{1,0},{2,3},{3,2},{4,5},{5,4},{6,7},{7,6},{8,9},{9,8},{10,11... | collective-permute-start | bytes 798728 | tf_op jit(solution)/shard_map/ppermute | solution.py:352
  20.9 1.1 %collective-permute-done.1.right_ref = f32[520,128]{1,0:T(8,128)S(1)} collective-permute-done((f32[520,128]{1,0:T(8,128)S(1)}, f32[520,128]{1,0:T(8,128)S(1)}, u32[]{:S(2)}, u32[]{:S(2)}) %collective-permute-start.1) | collective-permute-done | bytes 266272 | tf_op jit(solution)/shard_map/ppermute | solution.py:352
  22.1 4.4 %collective-permute-start.2 = (f32[264,128]{1,0:T(8,128)S(1)}, f32[264,128]{1,0:T(8,128)S(1)}, u32[]{:S(2)}, u32[]{:S(2)}) collective-permute-start(f32[264,128]{1,0:T(8,128)S(1)} %get-tuple-element.25), channel_id=1, source_target_pairs={{0,24},{1,25},{2,26},{3,27},{4,28},{5,29},{6,30},{7,31},{8,16},{9,... | collective-permute-start | bytes 405512 | tf_op jit(solution)/shard_map/ppermute | solution.py:357
  26.5 3.5 %collective-permute-done.2.right_ref = f32[264,128]{1,0:T(8,128)S(1)} collective-permute-done((f32[264,128]{1,0:T(8,128)S(1)}, f32[264,128]{1,0:T(8,128)S(1)}, u32[]{:S(2)}, u32[]{:S(2)}) %collective-permute-start.2) | collective-permute-done | bytes 135200 | tf_op jit(solution)/shard_map/ppermute | solution.py:357
  30.0 1.9 %collective-permute-start.3 = (f32[136,128]{1,0:T(8,128)S(1)}, f32[136,128]{1,0:T(8,128)S(1)}, u32[]{:S(2)}, u32[]{:S(2)}) collective-permute-start(f32[136,128]{1,0:T(8,128)S(1)} %get-tuple-element.27), channel_id=1, source_target_pairs={{0,8},{1,9},{2,10},{3,11},{4,12},{5,13},{6,14},{7,15},{8,0},{9,1},... | collective-permute-start | bytes 208904 | tf_op jit(solution)/shard_map/ppermute | solution.py:357
  31.9 3.4 %collective-permute-done.3.right_ref = f32[136,128]{1,0:T(8,128)S(1)} collective-permute-done((f32[136,128]{1,0:T(8,128)S(1)}, f32[136,128]{1,0:T(8,128)S(1)}, u32[]{:S(2)}, u32[]{:S(2)}) %collective-permute-start.3) | collective-permute-done | bytes 69664 | tf_op jit(solution)/shard_map/ppermute | solution.py:357
  35.3 0.0 all-to-all-done.got_ref
  35.3 0.8 sum_both.1
  36.1 4.2 %collective-permute-start.4 = (f32[136,128]{1,0:T(8,128)S(1)}, f32[136,128]{1,0:T(8,128)S(1)}, u32[]{:S(2)}, u32[]{:S(2)}) collective-permute-start(f32[136,128]{1,0:T(8,128)S(1)} %get-tuple-element.29.left_ref), channel_id=1, source_target_pairs={{0,2},{1,3},{2,0},{3,1},{4,6},{5,7},{6,4},{7,5},{8,10},{9,11},{10,... | collective-permute-start | bytes 208904 | tf_op jit(solution)/shard_map/ppermute | solution.py:357
  40.3 7.5 %all-to-all-start.1 = ((bf16[16,64,128]{2,1,0:T(8,128)(2,1)}), bf16[16,64,128]{2,1,0:T(8,128)(2,1)S(1)}, u32[]{:S(2)}, u32[]{:S(2)}) async-start(bf16[16,64,128]{2,1,0:T(8,128)(2,1)} %get-tuple-element.28), calls=%async_computation.1 | async-start | bytes 524288 | tf_op jit(solution)/shard_map/all_to_all | solution.py:347
  47.9 0.0 collective-permute-done.4.right_ref
  47.9 5.3 %collective-permute-start.5 = (f32[136,128]{1,0:T(8,128)S(1)}, f32[136,128]{1,0:T(8,128)S(1)}, u32[]{:S(2)}, u32[]{:S(2)}) collective-permute-start(f32[136,128]{1,0:T(8,128)S(1)} %add_y.1.left_ref), channel_id=1, source_target_pairs={{0,6},{1,7},{2,4},{3,5},{4,2},{5,3},{6,0},{7,1},{8,14},{9,15},{10,... | collective-permute-start | bytes 208904 | tf_op jit(solution)/shard_map/ppermute | solution.py:357
  53.2 1.9 %collective-permute-done.5.right_ref = f32[136,128]{1,0:T(8,128)S(1)} collective-permute-done((f32[136,128]{1,0:T(8,128)S(1)}, f32[136,128]{1,0:T(8,128)S(1)}, u32[]{:S(2)}, u32[]{:S(2)}) %collective-permute-start.5) | collective-permute-done | bytes 69664 | tf_op jit(solution)/shard_map/ppermute | solution.py:357
  55.1 0.7 sum_y.1
  55.9 1.0 %all-to-all-done.1.got_ref = bf16[16,64,128]{2,1,0:T(8,128)(2,1)S(1)} async-done(((bf16[16,64,128]{2,1,0:T(8,128)(2,1)}), bf16[16,64,128]{2,1,0:T(8,128)(2,1)S(1)}, u32[]{:S(2)}, u32[]{:S(2)}) %all-to-all-start.1) | async-done | bytes 262176 | tf_op jit(solution)/shard_map/all_to_all | solution.py:347
  56.9 0.0 copy-start
  56.9 8.3 %all-to-all-start.2 = ((bf16[8,144,128]{2,1,0:T(8,128)(2,1)}), bf16[8,144,128]{2,1,0:T(8,128)(2,1)S(1)}, u32[]{:S(2)}, u32[]{:S(2)}) async-start(bf16[8,144,128]{2,1,0:T(8,128)(2,1)} %get-tuple-element.33), calls=%async_computation.2 | async-start | bytes 589824 | tf_op jit(solution)/shard_map/all_to_all | solution.py:347
  65.2 0.0 copy-done
  65.2 0.1 unpack_in.1
  65.3 2.7 %collective-permute-start.6 = (bf16[512,256]{1,0:T(8,128)(2,1)S(1)}, bf16[512,256]{1,0:T(8,128)(2,1)S(1)}, u32[]{:S(2)}, u32[]{:S(2)}) collective-permute-start(bf16[512,256]{1,0:T(8,128)(2,1)S(1)} %get-tuple-element.38), channel_id=1, source_target_pairs={{0,32},{32,0},{64,96},{96,64},{128,160},{160,128},{192,224},{224,1... | collective-permute-start | bytes 786440 | tf_op jit(solution)/shard_map/ppermute | solution.py:362
  68.1 3.9 %all-to-all-done.2.got_out_ref = bf16[8,144,128]{2,1,0:T(8,128)(2,1)S(1)} async-done(((bf16[8,144,128]{2,1,0:T(8,128)(2,1)}), bf16[8,144,128]{2,1,0:T(8,128)(2,1)S(1)}, u32[]{:S(2)}, u32[]{:S(2)}) %all-to-all-start.2) | async-done | bytes 294944 | tf_op jit(solution)/shard_map/all_to_all | solution.py:347
  72.0 6.5 %invert.1 = (bf16[512,512]{1,0:T(8,128)(2,1)S(1)}, bf16[512,256]{1,0:T(8,128)(2,1)S(1)}) custom-call(bf16[512,512]{1,0:T(8,128)(2,1)S(1)} %get-tuple-element.32.after_ref.damped_in_ref, bf16[8,144,128]{2,1,0:T(8,128)(2,1)S(1)} %all-to-all-done.2.got_out_ref, f32[8,128]{1,0:T(8,128)S(1)} %stage_extra.1.extra_in_ref, f32[8,128]{1,0:T(8,128)S(1)} %get-tuple-element.35.extra_out_ref), custom_call_target="tpu_custom_call" | custom-call | flops 5368709120 | bytes 1613824 | tf_op jit(solution)/shard_map/invert/pallas_call | solution.py:330
  78.5 0.0 collective-permute-done.6.other_weight_ref
  78.5 1.5 %finish.1 = bf16[512,256]{1,0:T(8,128)(2,1)} custom-call(bf16[512,512]{1,0:T(8,128)(2,1)S(1)} %get-tuple-element.36.inverse_ref, bf16[512,256]{1,0:T(8,128)(2,1)S(1)} %get-tuple-element.37.right_ref, bf16[512,256]{1,0:T(8,128)(2,1)S(1)} %copy-done, bf16[512,256]{1,0:T(8,128)(2,1)S(1)} %collective-permute-done.6.other_weight_ref), custom_call_target="tpu_custom_call" | custom-call | flops 402653184 | bytes 1572864 | tf_op jit(solution)/shard_map/finish/pallas_call | solution.py:330
  (4 shorter events, 0.1 us)
Async XLA Ops:
  0.0 17.1 %collective-permute-start = (bf16[512,256]{1,0:T(8,128)(2,1)}, bf16[512,256]{1,0:T(8,128)(2,1)S(1)}, u32[]{:S(2)}, u32[]{:S(2)}) collective-permute-start(bf16[512,256]{1,0:T(8,128)(2,1)} %own_ref.1), channel_id=1, source_target_pairs={{0,32},{32,0},{64,96},{96,64},{128,160},{160,128},{192,224},{224,1... | collective-permute-start | bytes 786440 | tf_op jit(solution)/shard_map/ppermute | solution.py:362
  6.8 10.3 %copy-start.1 = (bf16[512,256]{1,0:T(8,128)(2,1)S(1)}, bf16[512,256]{1,0:T(8,128)(2,1)}, u32[]{:S(2)}) copy-start(bf16[512,256]{1,0:T(8,128)(2,1)} %own_ref.1) | copy-start | bytes 786436
  6.8 28.5 %all-to-all-start = ((f32[16,72,128]{2,1,0:T(8,128)}), f32[16,72,128]{2,1,0:T(8,128)S(1)}, u32[]{:S(2)}, u32[]{:S(2)}) async-start(f32[16,72,128]{2,1,0:T(8,128)} %gram_in.1), calls=%async_computation | async-start | bytes 1179648 | tf_op jit(solution)/shard_map/all_to_all | solution.py:347
  17.7 4.3 %collective-permute-start.1 = (f32[520,128]{1,0:T(8,128)S(1)}, f32[520,128]{1,0:T(8,128)S(1)}, u32[]{:S(2)}, u32[]{:S(2)}) collective-permute-start(f32[520,128]{1,0:T(8,128)S(1)} %get-tuple-element.23), channel_id=1, source_target_pairs={{0,1},{1,0},{2,3},{3,2},{4,5},{5,4},{6,7},{7,6},{8,9},{9,8},{10,11... | collective-permute-start | bytes 798728 | tf_op jit(solution)/shard_map/ppermute | solution.py:352
  22.1 7.9 %collective-permute-start.2 = (f32[264,128]{1,0:T(8,128)S(1)}, f32[264,128]{1,0:T(8,128)S(1)}, u32[]{:S(2)}, u32[]{:S(2)}) collective-permute-start(f32[264,128]{1,0:T(8,128)S(1)} %get-tuple-element.25), channel_id=1, source_target_pairs={{0,24},{1,25},{2,26},{3,27},{4,28},{5,29},{6,30},{7,31},{8,16},{9,... | collective-permute-start | bytes 405512 | tf_op jit(solution)/shard_map/ppermute | solution.py:357
  30.0 5.3 %collective-permute-start.3 = (f32[136,128]{1,0:T(8,128)S(1)}, f32[136,128]{1,0:T(8,128)S(1)}, u32[]{:S(2)}, u32[]{:S(2)}) collective-permute-start(f32[136,128]{1,0:T(8,128)S(1)} %get-tuple-element.27), channel_id=1, source_target_pairs={{0,8},{1,9},{2,10},{3,11},{4,12},{5,13},{6,14},{7,15},{8,0},{9,1},... | collective-permute-start | bytes 208904 | tf_op jit(solution)/shard_map/ppermute | solution.py:357
  36.1 11.8 %collective-permute-start.4 = (f32[136,128]{1,0:T(8,128)S(1)}, f32[136,128]{1,0:T(8,128)S(1)}, u32[]{:S(2)}, u32[]{:S(2)}) collective-permute-start(f32[136,128]{1,0:T(8,128)S(1)} %get-tuple-element.29.left_ref), channel_id=1, source_target_pairs={{0,2},{1,3},{2,0},{3,1},{4,6},{5,7},{6,4},{7,5},{8,10},{9,11},{10,... | collective-permute-start | bytes 208904 | tf_op jit(solution)/shard_map/ppermute | solution.py:357
  40.3 16.6 %all-to-all-start.1 = ((bf16[16,64,128]{2,1,0:T(8,128)(2,1)}), bf16[16,64,128]{2,1,0:T(8,128)(2,1)S(1)}, u32[]{:S(2)}, u32[]{:S(2)}) async-start(bf16[16,64,128]{2,1,0:T(8,128)(2,1)} %get-tuple-element.28), calls=%async_computation.1 | async-start | bytes 524288 | tf_op jit(solution)/shard_map/all_to_all | solution.py:347
  47.9 7.2 %collective-permute-start.5 = (f32[136,128]{1,0:T(8,128)S(1)}, f32[136,128]{1,0:T(8,128)S(1)}, u32[]{:S(2)}, u32[]{:S(2)}) collective-permute-start(f32[136,128]{1,0:T(8,128)S(1)} %add_y.1.left_ref), channel_id=1, source_target_pairs={{0,6},{1,7},{2,4},{3,5},{4,2},{5,3},{6,0},{7,1},{8,14},{9,15},{10,... | collective-permute-start | bytes 208904 | tf_op jit(solution)/shard_map/ppermute | solution.py:357
  56.9 8.3 %copy-start = (bf16[512,256]{1,0:T(8,128)(2,1)S(1)}, bf16[512,256]{1,0:T(8,128)(2,1)}, u32[]{:S(2)}) copy-start(bf16[512,256]{1,0:T(8,128)(2,1)} %weight_ref.3) | copy-start | bytes 786436
  56.9 15.1 %all-to-all-start.2 = ((bf16[8,144,128]{2,1,0:T(8,128)(2,1)}), bf16[8,144,128]{2,1,0:T(8,128)(2,1)S(1)}, u32[]{:S(2)}, u32[]{:S(2)}) async-start(bf16[8,144,128]{2,1,0:T(8,128)(2,1)} %get-tuple-element.33), calls=%async_computation.2 | async-start | bytes 589824 | tf_op jit(solution)/shard_map/all_to_all | solution.py:347
  65.3 13.2 %collective-permute-start.6 = (bf16[512,256]{1,0:T(8,128)(2,1)S(1)}, bf16[512,256]{1,0:T(8,128)(2,1)S(1)}, u32[]{:S(2)}, u32[]{:S(2)}) collective-permute-start(bf16[512,256]{1,0:T(8,128)(2,1)S(1)} %get-tuple-element.38), channel_id=1, source_target_pairs={{0,32},{32,0},{64,96},{96,64},{128,160},{160,128},{192,224},{224,1... | collective-permute-start | bytes 786440 | tf_op jit(solution)/shard_map/ppermute | solution.py:362

commit v7 on v6

--- a/solution.py
+++ b/solution.py
@@ -109,7 +109,7 @@
             pltpu.make_async_copy(data_hbm.at[place], data_ref.at[place], sems.at[chunk])
         )
     copies.append(pltpu.make_async_copy(grads_hbm, grads_ref, sems.at[CHUNKS]))
-    for copy in reversed(copies):
+    for copy in copies[CHUNKS:] + copies[:CHUNKS]:
         copy.start()
     copies[CHUNKS].wait()
     grads = grads_ref[...].astype(jnp.float32)
@@ -191,16 +191,17 @@
     return [high, middle, rest - middle]
 
 
-def sum_both_kernel(
-    count, got_ref, left_ref, right_ref, send_ref, extra_in_ref, out_ref
-):
+def sum_in_kernel(got_ref, after_ref, send_ref, extra_ref):
     total = sum_pieces(got_ref)
     rows = send_ref.shape[1]
     rounded = total[:rows].astype(jnp.bfloat16)
     for piece in range(send_ref.shape[0]):
         send_ref[piece] = rounded
-    extra = total[rows:]
-    extra_in_ref[...] = extra
+    extra_ref[...] = total[rows:]
+
+
+def sum_x_kernel(count, left_ref, right_ref, extra_in_ref, out_ref):
+    extra = extra_in_ref[...]
     total = left_ref[...] + right_ref[...]
     rows = total.shape[0] - EXTRA
     trace_in = jnp.broadcast_to(total_of(extra[:count]), (1, TILE))
@@ -223,16 +224,19 @@
     extra_ref[...] = extra
 
 
-def unpack_in_kernel(got_ref, weight_ref, out_ref, sent_ref):
-    sent_ref[...] = weight_ref[...]
+def stage_in_kernel(got_ref, weight_ref, sent_ref, sent_weight_ref):
+    sent_ref[...] = got_ref[...]
+    sent_weight_ref[...] = weight_ref[...]
+
+
+def unpack_in_kernel(got_ref, other_ref, out_ref, packed_ref):
     rows = got_ref.shape[1]
-    per_tile = TILE // rows
-    unpack_block(
-        lambda position: jnp.concatenate(
-            [got_ref[position * per_tile + part] for part in range(per_tile)], axis=0
-        ),
-        out_ref,
-    )
+    parity = lax.axis_index("grp") % 2
+    for ref, place in ((got_ref, parity), (other_ref, 1 - parity)):
+        for piece in range(ref.shape[0]):
+            start = pl.multiple_of((2 * piece + place) * rows, rows)
+            packed_ref[pl.ds(start, rows), :] = ref[piece]
+    unpack_block(lambda position: packed_ref[position * TILE : (position + 1) * TILE, :], out_ref)
 
 
 def invert_kernel(
@@ -414,17 +418,21 @@
             (keep, swap(give)),
             (shape_of(rows + EXTRA, TILE),) * 2,
         )
-    to_all_in, extra_in, part_y = local_call(
-        functools.partial(sum_both_kernel, count),
-        "sum_both",
-        (got_in, keep, swap_along(give, x_stride, 1)),
-        (
-            shape_of(groups, in_rows, TILE, dtype=half_type),
-            shape_of(EXTRA, TILE),
-            shape_of(piece_rows + EXTRA, TILE),
-        ),
-    )
-    all_in = exchange(to_all_in, "grp")
+    to_all_in, extra_in = local_call(
+        sum_in_kernel,
+        "sum_in",
+        (got_in, keep),
+        (shape_of(groups // 2, in_rows, TILE, dtype=half_type), shape_of(EXTRA, TILE)),
+    )
+    same_half = [list(range(parity, groups, 2)) for parity in range(2)]
+    all_in = exchange(to_all_in, "grp", same_half)
+    part_y = local_call(
+        functools.partial(sum_x_kernel, count),
+        "sum_x",
+        (keep, swap_along(give, x_stride, 1), extra_in),
+        shape_of(piece_rows + EXTRA, TILE),
+        flops=LATE_START,
+    )
     part_y = local_call(
         add_kernel,
         "add_y",
@@ -449,15 +457,26 @@
 
     block = (width, width)
     all_in, extra_out = lax.optimization_barrier((all_in, extra_out))
-    damped_in, sent_weight = local_call(
+    sent_in, sent_weight = local_call(
+        stage_in_kernel,
+        "stage_in",
+        (all_in, grad_weight),
+        (
+            shape_of(*all_in.shape, dtype=half_type),
+            shape_of(*grad_weight.shape, dtype=half_type),
+        ),
+    )
+    other_in = swap_half(sent_in)
+    other_weight = swap_half(sent_weight)
+    extra_in = local_call(
+        stage_kernel, "stage_extra", (sent_in, extra_in), shape_of(*extra_in.shape), flops=LATE_START
+    )
+    damped_in = local_call(
         unpack_in_kernel,
         "unpack_in",
-        (all_in, grad_weight),
-        (shape_of(*block, dtype=half_type), shape_of(*grad_weight.shape, dtype=half_type)),
-    )
-    other_weight = swap_half(sent_weight)
-    extra_in = local_call(
-        stage_kernel, "stage_extra", (damped_in, extra_in), shape_of(*extra_in.shape), flops=LATE_START
+        (all_in, other_in),
+        shape_of(*block, dtype=half_type),
+        scratch=[pltpu.VMEM((packed_rows, TILE), half_type)],
     )
     inverse_in, right = local_call(
         invert_kernel,

time: 80.7 us -> 79.2 us (0.981)
  waiting for transfers between devices: 14.9 us -> 11.2 us
  starting transfers between devices: 51.9 us -> 53.7 us
    all_to_all x3, waiting for transfers between devices: 4.92 us -> 1.29 us  [exchange(): lax.all_to_all(value, axis, 0, 0, tiled=True, axis_index_groups=groups)]
    ppermute x2 -> x3, starting transfers between devices: 6.77 us -> 9.71 us  [swap_half(): return lax.ppermute(value, 'grp', pairs)]
    ppermute x4, waiting for transfers between devices: 8.83 us -> 6.86 us  [swap_along(): return lax.ppermute(value, 'blk', pairs)]
    ppermute x2 -> x3, waiting for transfers between devices: 0.01 us -> 1.91 us  [swap_half(): return lax.ppermute(value, 'grp', pairs)]
    all_to_all x3, starting transfers between devices: 26.1 us -> 25.1 us  [exchange(): lax.all_to_all(value, axis, 0, 0, tiled=True, axis_index_groups=groups)]
    pallas_call x11 -> x13, Pallas kernels: 13.1 us -> 13.2 us  [local_call(): pl.pallas_call(kernel, out_shape=outs, in_specs=[pl.BlockSpec(memory_spac...]
  transfers between devices with their start and end apart: 10 -> 11, of which waited for: 6 -> 6; matrix products, arithmetic and copies ran while one was open for 0% -> 0% of each run, Pallas kernels for 14% -> 15%
where the time goes in v7:
time: 79.2 us; the launch traced here: 78.3 us
  starting transfers between devices  53.7 us (68%)
  Pallas kernels  13.2 us (17%)
  waiting for transfers between devices  11.2 us (14%)
    all_to_all x3, starting transfers between devices, exchange(): lax.all_to_all(value, axis, 0, 0, tiled=True, axis_index_groups=groups)  25.1 us
    ppermute x4, starting transfers between devices, swap_along(): return lax.ppermute(value, 'blk', pairs)  15.8 us
    pallas_call x13, Pallas kernels, local_call(): pl.pallas_call(kernel, out_shape=outs, in_specs=[pl.BlockSpec(memory_spac...  13.2 us
    ppermute x3, starting transfers between devices, swap_half(): return lax.ppermute(value, 'grp', pairs)  9.71 us
    ppermute x4, waiting for transfers between devices, swap_along(): return lax.ppermute(value, 'blk', pairs)  6.86 us
    ppermute x1, starting transfers between devices, swap_core(): return lax.ppermute(value, 'blk', pairs)  3.14 us
    ppermute x3, waiting for transfers between devices, swap_half(): return lax.ppermute(value, 'grp', pairs)  1.91 us
  transfers between devices with their start and end apart: 11, of which 6 were waited for; matrix products, arithmetic and copies ran while one was open for 0% of the time, Pallas kernels for 15%

profile of v7, /device:TPU:1, one launch (start us, length us, event | category | flops | bytes accessed | tf_op | source)
XLA Modules:
  0.0 78.3 jit_solution(7036688145845784116)
XLA Ops:
  0.0 4.0 %collective-permute-start = (bf16[512,256]{1,0:T(8,128)(2,1)}, bf16[512,256]{1,0:T(8,128)(2,1)S(1)}, u32[]{:S(2)}, u32[]{:S(2)}) collective-permute-start(bf16[512,256]{1,0:T(8,128)(2,1)} %own_ref.1), channel_id=1, source_target_pairs={{0,32},{32,0},{64,96},{96,64},{128,160},{160,128},{192,224},{224,1... | collective-permute-start | bytes 786440 | tf_op jit(solution)/shard_map/ppermute | solution.py:366
  4.0 2.7 %gram_in.1 = f32[16,72,128]{2,1,0:T(8,128)} custom-call(bf16[1024,512]{1,0:T(8,128)(2,1)} %data_hbm.1, bf16[512,256]{1,0:T(8,128)(2,1)} %own_ref.1), custom_call_target="tpu_custom_call" | custom-call | flops 536870912 | bytes 1900544 | tf_op jit(solution)/shard_map/gram_in/pallas_call | solution.py:334
  6.8 0.0 copy-start.1
  6.8 10.3 %all-to-all-start = ((f32[16,72,128]{2,1,0:T(8,128)}), f32[16,72,128]{2,1,0:T(8,128)S(1)}, u32[]{:S(2)}, u32[]{:S(2)}) async-start(f32[16,72,128]{2,1,0:T(8,128)} %gram_in.1), calls=%async_computation | async-start | bytes 1179648 | tf_op jit(solution)/shard_map/all_to_all | solution.py:351
  17.1 0.0 collective-permute-done.other_ref
  17.1 0.0 copy-done.1
  17.1 0.6 gram_out.1
  17.7 3.1 %collective-permute-start.1 = (f32[520,128]{1,0:T(8,128)S(1)}, f32[520,128]{1,0:T(8,128)S(1)}, u32[]{:S(2)}, u32[]{:S(2)}) collective-permute-start(f32[520,128]{1,0:T(8,128)S(1)} %get-tuple-element.22), channel_id=1, source_target_pairs={{0,1},{1,0},{2,3},{3,2},{4,5},{5,4},{6,7},{7,6},{8,9},{9,8},{10,11... | collective-permute-start | bytes 798728 | tf_op jit(solution)/shard_map/ppermute | solution.py:356
  20.8 1.1 %collective-permute-done.1.right_ref = f32[520,128]{1,0:T(8,128)S(1)} collective-permute-done((f32[520,128]{1,0:T(8,128)S(1)}, f32[520,128]{1,0:T(8,128)S(1)}, u32[]{:S(2)}, u32[]{:S(2)}) %collective-permute-start.1) | collective-permute-done | bytes 266272 | tf_op jit(solution)/shard_map/ppermute | solution.py:356
  22.0 4.4 %collective-permute-start.2 = (f32[264,128]{1,0:T(8,128)S(1)}, f32[264,128]{1,0:T(8,128)S(1)}, u32[]{:S(2)}, u32[]{:S(2)}) collective-permute-start(f32[264,128]{1,0:T(8,128)S(1)} %get-tuple-element.24), channel_id=1, source_target_pairs={{0,24},{1,25},{2,26},{3,27},{4,28},{5,29},{6,30},{7,31},{8,16},{9,... | collective-permute-start | bytes 405512 | tf_op jit(solution)/shard_map/ppermute | solution.py:361
  26.4 3.5 %collective-permute-done.2.right_ref = f32[264,128]{1,0:T(8,128)S(1)} collective-permute-done((f32[264,128]{1,0:T(8,128)S(1)}, f32[264,128]{1,0:T(8,128)S(1)}, u32[]{:S(2)}, u32[]{:S(2)}) %collective-permute-start.2) | collective-permute-done | bytes 135200 | tf_op jit(solution)/shard_map/ppermute | solution.py:361
  30.0 1.9 %collective-permute-start.3 = (f32[136,128]{1,0:T(8,128)S(1)}, f32[136,128]{1,0:T(8,128)S(1)}, u32[]{:S(2)}, u32[]{:S(2)}) collective-permute-start(f32[136,128]{1,0:T(8,128)S(1)} %get-tuple-element.27), channel_id=1, source_target_pairs={{0,8},{1,9},{2,10},{3,11},{4,12},{5,13},{6,14},{7,15},{8,0},{9,1},... | collective-permute-start | bytes 208904 | tf_op jit(solution)/shard_map/ppermute | solution.py:361
  31.9 1.3 %all-to-all-done.got_ref = f32[16,72,128]{2,1,0:T(8,128)S(1)} async-done(((f32[16,72,128]{2,1,0:T(8,128)}), f32[16,72,128]{2,1,0:T(8,128)S(1)}, u32[]{:S(2)}, u32[]{:S(2)}) %all-to-all-start) | async-done | bytes 589856 | tf_op jit(solution)/shard_map/all_to_all | solution.py:351
  33.2 0.7 sum_in.1
  33.9 1.4 %collective-permute-done.3.right_ref = f32[136,128]{1,0:T(8,128)S(1)} collective-permute-done((f32[136,128]{1,0:T(8,128)S(1)}, f32[136,128]{1,0:T(8,128)S(1)}, u32[]{:S(2)}, u32[]{:S(2)}) %collective-permute-start.3) | collective-permute-done | bytes 69664 | tf_op jit(solution)/shard_map/ppermute | solution.py:361
  35.3 0.1 sum_x.1.left_ref
  35.4 4.2 %collective-permute-start.4 = (f32[136,128]{1,0:T(8,128)S(1)}, f32[136,128]{1,0:T(8,128)S(1)}, u32[]{:S(2)}, u32[]{:S(2)}) collective-permute-start(f32[136,128]{1,0:T(8,128)S(1)} %sum_x.1.left_ref), channel_id=1, source_target_pairs={{0,2},{1,3},{2,0},{3,1},{4,6},{5,7},{6,4},{7,5},{8,10},{9,11},{10,... | collective-permute-start | bytes 208904 | tf_op jit(solution)/shard_map/ppermute | solution.py:361
  39.6 6.5 %all-to-all-start.1 = ((bf16[8,64,128]{2,1,0:T(8,128)(2,1)}), bf16[8,64,128]{2,1,0:T(8,128)(2,1)S(1)}, u32[]{:S(2)}, u32[]{:S(2)}) async-start(bf16[8,64,128]{2,1,0:T(8,128)(2,1)} %get-tuple-element.26), calls=%async_computation.1 | async-start | bytes 262144 | tf_op jit(solution)/shard_map/all_to_all | solution.py:351
  46.2 0.0 collective-permute-done.4.right_ref
  46.2 5.3 %collective-permute-start.5 = (f32[136,128]{1,0:T(8,128)S(1)}, f32[136,128]{1,0:T(8,128)S(1)}, u32[]{:S(2)}, u32[]{:S(2)}) collective-permute-start(f32[136,128]{1,0:T(8,128)S(1)} %add_y.1.left_ref), channel_id=1, source_target_pairs={{0,6},{1,7},{2,4},{3,5},{4,2},{5,3},{6,0},{7,1},{8,14},{9,15},{10,... | collective-permute-start | bytes 208904 | tf_op jit(solution)/shard_map/ppermute | solution.py:361
  51.5 1.9 %collective-permute-done.5.right_ref = f32[136,128]{1,0:T(8,128)S(1)} collective-permute-done((f32[136,128]{1,0:T(8,128)S(1)}, f32[136,128]{1,0:T(8,128)S(1)}, u32[]{:S(2)}, u32[]{:S(2)}) %collective-permute-start.5) | collective-permute-done | bytes 69664 | tf_op jit(solution)/shard_map/ppermute | solution.py:361
  53.4 0.8 sum_y.1
  54.2 0.0 all-to-all-done.1.got_ref
  54.2 0.0 copy-start
  54.2 8.2 %all-to-all-start.2 = ((bf16[8,144,128]{2,1,0:T(8,128)(2,1)}), bf16[8,144,128]{2,1,0:T(8,128)(2,1)S(1)}, u32[]{:S(2)}, u32[]{:S(2)}) async-start(bf16[8,144,128]{2,1,0:T(8,128)(2,1)} %get-tuple-element.32), calls=%async_computation.2 | async-start | bytes 589824 | tf_op jit(solution)/shard_map/all_to_all | solution.py:351
  62.4 0.0 copy-done
  62.4 3.8 %collective-permute-start.6 = (bf16[8,64,128]{2,1,0:T(8,128)(2,1)S(1)}, bf16[8,64,128]{2,1,0:T(8,128)(2,1)S(1)}, u32[]{:S(2)}, u32[]{:S(2)}) collective-permute-start(bf16[8,64,128]{2,1,0:T(8,128)(2,1)S(1)} %get-tuple-element.31.after_ref), channel_id=1, source_target_pairs={{0,32},{32,0},{64,96},{96,64},{128,160},{160,128},{192,224},{224,1... | collective-permute-start | bytes 393224 | tf_op jit(solution)/shard_map/ppermute | solution.py:366
  66.2 1.9 %collective-permute-start.7 = (bf16[512,256]{1,0:T(8,128)(2,1)S(1)}, bf16[512,256]{1,0:T(8,128)(2,1)S(1)}, u32[]{:S(2)}, u32[]{:S(2)}) collective-permute-start(bf16[512,256]{1,0:T(8,128)(2,1)S(1)} %get-tuple-element.36), channel_id=1, source_target_pairs={{0,32},{32,0},{64,96},{96,64},{128,160},{160,128},{192,224},{224,1... | collective-permute-start | bytes 786440 | tf_op jit(solution)/shard_map/ppermute | solution.py:366
  68.1 1.9 %collective-permute-done.6.other_ref = bf16[8,64,128]{2,1,0:T(8,128)(2,1)S(1)} collective-permute-done((bf16[8,64,128]{2,1,0:T(8,128)(2,1)S(1)}, bf16[8,64,128]{2,1,0:T(8,128)(2,1)S(1)}, u32[]{:S(2)}, u32[]{:S(2)}) %collective-permute-start.6) | collective-permute-done | bytes 131104 | tf_op jit(solution)/shard_map/ppermute | solution.py:366
  70.1 0.2 unpack_in.1.damped_in_ref
  70.3 0.0 all-to-all-done.2.got_out_ref
  70.3 6.5 %invert.1 = (bf16[512,512]{1,0:T(8,128)(2,1)S(1)}, bf16[512,256]{1,0:T(8,128)(2,1)S(1)}) custom-call(bf16[512,512]{1,0:T(8,128)(2,1)S(1)} %unpack_in.1.damped_in_ref, bf16[8,144,128]{2,1,0:T(8,128)(2,1)S(1)} %all-to-all-done.2.got_out_ref, f32[8,128]{1,0:T(8,128)S(1)} %stage_extra.1.extra_in_ref, f32[8,128]{1,0:T(8,128)S(1)} %get-tuple-element.33.extra_out_ref), custom_call_target="tpu_custom_call" | custom-call | flops 5368709120 | bytes 1613824 | tf_op jit(solution)/shard_map/invert/pallas_call | solution.py:334
  76.8 0.0 collective-permute-done.7.other_weight_ref
  76.8 1.5 %finish.1 = bf16[512,256]{1,0:T(8,128)(2,1)} custom-call(bf16[512,512]{1,0:T(8,128)(2,1)S(1)} %get-tuple-element.34.inverse_ref, bf16[512,256]{1,0:T(8,128)(2,1)S(1)} %get-tuple-element.35.right_ref, bf16[512,256]{1,0:T(8,128)(2,1)S(1)} %copy-done, bf16[512,256]{1,0:T(8,128)(2,1)S(1)} %collective-permute-done.7.other_weight_ref), custom_call_target="tpu_custom_call" | custom-call | flops 402653184 | bytes 1572864 | tf_op jit(solution)/shard_map/finish/pallas_call | solution.py:334
  (5 shorter events, 0.1 us)
Async XLA Ops:
  0.0 17.1 %collective-permute-start = (bf16[512,256]{1,0:T(8,128)(2,1)}, bf16[512,256]{1,0:T(8,128)(2,1)S(1)}, u32[]{:S(2)}, u32[]{:S(2)}) collective-permute-start(bf16[512,256]{1,0:T(8,128)(2,1)} %own_ref.1), channel_id=1, source_target_pairs={{0,32},{32,0},{64,96},{96,64},{128,160},{160,128},{192,224},{224,1... | collective-permute-start | bytes 786440 | tf_op jit(solution)/shard_map/ppermute | solution.py:366
  6.8 10.3 %copy-start.1 = (bf16[512,256]{1,0:T(8,128)(2,1)S(1)}, bf16[512,256]{1,0:T(8,128)(2,1)}, u32[]{:S(2)}) copy-start(bf16[512,256]{1,0:T(8,128)(2,1)} %own_ref.1) | copy-start | bytes 786436
  6.8 26.4 %all-to-all-start = ((f32[16,72,128]{2,1,0:T(8,128)}), f32[16,72,128]{2,1,0:T(8,128)S(1)}, u32[]{:S(2)}, u32[]{:S(2)}) async-start(f32[16,72,128]{2,1,0:T(8,128)} %gram_in.1), calls=%async_computation | async-start | bytes 1179648 | tf_op jit(solution)/shard_map/all_to_all | solution.py:351
  17.7 4.3 %collective-permute-start.1 = (f32[520,128]{1,0:T(8,128)S(1)}, f32[520,128]{1,0:T(8,128)S(1)}, u32[]{:S(2)}, u32[]{:S(2)}) collective-permute-start(f32[520,128]{1,0:T(8,128)S(1)} %get-tuple-element.22), channel_id=1, source_target_pairs={{0,1},{1,0},{2,3},{3,2},{4,5},{5,4},{6,7},{7,6},{8,9},{9,8},{10,11... | collective-permute-start | bytes 798728 | tf_op jit(solution)/shard_map/ppermute | solution.py:356
  22.0 7.9 %collective-permute-start.2 = (f32[264,128]{1,0:T(8,128)S(1)}, f32[264,128]{1,0:T(8,128)S(1)}, u32[]{:S(2)}, u32[]{:S(2)}) collective-permute-start(f32[264,128]{1,0:T(8,128)S(1)} %get-tuple-element.24), channel_id=1, source_target_pairs={{0,24},{1,25},{2,26},{3,27},{4,28},{5,29},{6,30},{7,31},{8,16},{9,... | collective-permute-start | bytes 405512 | tf_op jit(solution)/shard_map/ppermute | solution.py:361
  30.0 5.3 %collective-permute-start.3 = (f32[136,128]{1,0:T(8,128)S(1)}, f32[136,128]{1,0:T(8,128)S(1)}, u32[]{:S(2)}, u32[]{:S(2)}) collective-permute-start(f32[136,128]{1,0:T(8,128)S(1)} %get-tuple-element.27), channel_id=1, source_target_pairs={{0,8},{1,9},{2,10},{3,11},{4,12},{5,13},{6,14},{7,15},{8,0},{9,1},... | collective-permute-start | bytes 208904 | tf_op jit(solution)/shard_map/ppermute | solution.py:361
  35.4 10.8 %collective-permute-start.4 = (f32[136,128]{1,0:T(8,128)S(1)}, f32[136,128]{1,0:T(8,128)S(1)}, u32[]{:S(2)}, u32[]{:S(2)}) collective-permute-start(f32[136,128]{1,0:T(8,128)S(1)} %sum_x.1.left_ref), channel_id=1, source_target_pairs={{0,2},{1,3},{2,0},{3,1},{4,6},{5,7},{6,4},{7,5},{8,10},{9,11},{10,... | collective-permute-start | bytes 208904 | tf_op jit(solution)/shard_map/ppermute | solution.py:361
  39.6 14.6 %all-to-all-start.1 = ((bf16[8,64,128]{2,1,0:T(8,128)(2,1)}), bf16[8,64,128]{2,1,0:T(8,128)(2,1)S(1)}, u32[]{:S(2)}, u32[]{:S(2)}) async-start(bf16[8,64,128]{2,1,0:T(8,128)(2,1)} %get-tuple-element.26), calls=%async_computation.1 | async-start | bytes 262144 | tf_op jit(solution)/shard_map/all_to_all | solution.py:351
  46.2 7.2 %collective-permute-start.5 = (f32[136,128]{1,0:T(8,128)S(1)}, f32[136,128]{1,0:T(8,128)S(1)}, u32[]{:S(2)}, u32[]{:S(2)}) collective-permute-start(f32[136,128]{1,0:T(8,128)S(1)} %add_y.1.left_ref), channel_id=1, source_target_pairs={{0,6},{1,7},{2,4},{3,5},{4,2},{5,3},{6,0},{7,1},{8,14},{9,15},{10,... | collective-permute-start | bytes 208904 | tf_op jit(solution)/shard_map/ppermute | solution.py:361
  54.2 8.2 %copy-start = (bf16[512,256]{1,0:T(8,128)(2,1)S(1)}, bf16[512,256]{1,0:T(8,128)(2,1)}, u32[]{:S(2)}) copy-start(bf16[512,256]{1,0:T(8,128)(2,1)} %weight_ref.3) | copy-start | bytes 786436
  54.2 16.1 %all-to-all-start.2 = ((bf16[8,144,128]{2,1,0:T(8,128)(2,1)}), bf16[8,144,128]{2,1,0:T(8,128)(2,1)S(1)}, u32[]{:S(2)}, u32[]{:S(2)}) async-start(bf16[8,144,128]{2,1,0:T(8,128)(2,1)} %get-tuple-element.32), calls=%async_computation.2 | async-start | bytes 589824 | tf_op jit(solution)/shard_map/all_to_all | solution.py:351
  62.4 7.6 %collective-permute-start.6 = (bf16[8,64,128]{2,1,0:T(8,128)(2,1)S(1)}, bf16[8,64,128]{2,1,0:T(8,128)(2,1)S(1)}, u32[]{:S(2)}, u32[]{:S(2)}) collective-permute-start(bf16[8,64,128]{2,1,0:T(8,128)(2,1)S(1)} %get-tuple-element.31.after_ref), channel_id=1, source_target_pairs={{0,32},{32,0},{64,96},{96,64},{128,160},{160,128},{192,224},{224,1... | collective-permute-start | bytes 393224 | tf_op jit(solution)/shard_map/ppermute | solution.py:366
  66.2 10.6 %collective-permute-start.7 = (bf16[512,256]{1,0:T(8,128)(2,1)S(1)}, bf16[512,256]{1,0:T(8,128)(2,1)S(1)}, u32[]{:S(2)}, u32[]{:S(2)}) collective-permute-start(bf16[512,256]{1,0:T(8,128)(2,1)S(1)} %get-tuple-element.36), channel_id=1, source_target_pairs={{0,32},{32,0},{64,96},{96,64},{128,160},{160,128},{192,224},{224,1... | collective-permute-start | bytes 786440 | tf_op jit(solution)/shard_map/ppermute | solution.py:366

commit v8 on v7

--- a/solution.py
+++ b/solution.py
@@ -150,7 +150,7 @@
     extra = jnp.concatenate([diagonal, filler], axis=0)
     share = keep_ref.shape[0] - EXTRA
     for ref, owner in ((keep_ref, core), (send_ref, 1 - core)):
-        start = pl.multiple_of(owner * share, share)
+        start = pl.multiple_of((parity * CORES + owner) * share, share)
         ref[:share, :] = packed_ref[pl.ds(start, share), :]
         ref[share:, :] = extra
 
@@ -259,7 +259,7 @@
     own_column = pl.ds(pl.multiple_of(parity * half, half), half)
 
     scalars = jnp.zeros((EXTRA_HALF, TILE), jnp.float32)
-    for piece in range(pieces):
+    for piece in range(pieces // 2):
         scalars = scalars + got_out_ref[piece, rows_out:, :].astype(jnp.float32)
     sum_in = scalars[0:1] + scalars[1:2] + scalars[2:3]
     sum_out = scalars[3:4] + scalars[4:5] + scalars[5:6]
@@ -275,12 +275,19 @@
 
     full_in_ref[...] = damped_in_ref[...]
     put_diagonal(diagonal_in, damping_in, full_in_ref)
-    unpack_block(
-        lambda position: got_out_ref[
-            position % RING * CORES + position // RING, :rows_out, :
-        ],
-        damped_out_ref,
-    )
+    def fetch_out(position):
+        per_tile = TILE // rows_out
+        pair = position // RING
+        core, first = position % RING // CORES, position % CORES * per_tile
+        return jnp.concatenate(
+            [
+                got_out_ref[(pair * RING + first + part) * CORES + core, :rows_out, :]
+                for part in range(per_tile)
+            ],
+            axis=0,
+        )
+
+    unpack_block(fetch_out, damped_out_ref)
     put_diagonal(diagonal_out, damping_out, damped_out_ref)
 
     chains = (
@@ -374,7 +381,7 @@
     packed_rows = width * width // (2 * TILE)
     total_tokens = activations.shape[0] * groups
     in_rows = packed_rows // groups
-    share_rows = packed_rows // CORES
+    share_rows = packed_rows // (2 * CORES)
     piece_rows = share_rows // RING
     y_stride, x_stride = CORES, CORES * RING
     half_type = jnp.bfloat16
@@ -445,15 +452,22 @@
         "sum_y",
         (part_y, swap_along(part_y, y_stride, 3)),
         (
-            shape_of(RING * CORES, piece_rows + EXTRA_HALF, TILE, dtype=half_type),
+            shape_of(2 * RING * CORES, piece_rows + EXTRA_HALF, TILE, dtype=half_type),
             shape_of(EXTRA, TILE),
         ),
     )
-    same_y = [
-        [x * x_stride + y * y_stride + core for x in range(RING) for core in range(CORES)]
+    owners = lax.axis_size("blk")
+    same_plane = [
+        [
+            (2 * z + parity) * owners + x * x_stride + y * y_stride + core
+            for parity in range(2)
+            for x in range(RING)
+            for core in range(CORES)
+        ]
+        for z in range(groups // 2)
         for y in range(RING)
     ]
-    all_out = exchange(to_all_out, "blk", same_y)
+    all_out = exchange(to_all_out, ("grp", "blk"), same_plane)
 
     block = (width, width)
     all_in, extra_out = lax.optimization_barrier((all_in, extra_out))

time: 79.2 us -> 79 us (level)
    ppermute x4, waiting for transfers between devices: 6.86 us -> 3.69 us  [swap_along(): return lax.ppermute(value, 'blk', pairs)]
    all_to_all x3, waiting for transfers between devices: 1.29 us -> 3.21 us  [exchange(): lax.all_to_all(value, axis, 0, 0, tiled=True, axis_index_groups=groups)]
    ppermute x3, waiting for transfers between devices: 1.91 us -> 3.31 us  [swap_half(): return lax.ppermute(value, 'grp', pairs)]
where the time goes in v8:
time: 79 us; the launch traced here: 78.3 us
  starting transfers between devices  53.8 us (68%)
  Pallas kernels  13.1 us (17%)
  waiting for transfers between devices  11.2 us (14%)
    all_to_all x3, starting transfers between devices, exchange(): lax.all_to_all(value, axis, 0, 0, tiled=True, axis_index_groups=groups)  25.5 us
    ppermute x4, starting transfers between devices, swap_along(): return lax.ppermute(value, 'blk', pairs)  15.8 us
    pallas_call x13, Pallas kernels, local_call(): pl.pallas_call(kernel, out_shape=outs, in_specs=[pl.BlockSpec(memory_spac...  13.1 us
    ppermute x3, starting transfers between devices, swap_half(): return lax.ppermute(value, 'grp', pairs)  9.33 us
    ppermute x4, waiting for transfers between devices, swap_along(): return lax.ppermute(value, 'blk', pairs)  3.69 us
    ppermute x3, waiting for transfers between devices, swap_half(): return lax.ppermute(value, 'grp', pairs)  3.31 us
    all_to_all x3, waiting for transfers between devices, exchange(): lax.all_to_all(value, axis, 0, 0, tiled=True, axis_index_groups=groups)  3.21 us
    ppermute x1, starting transfers between devices, swap_core(): return lax.ppermute(value, 'blk', pairs)  3.14 us
  transfers between devices with their start and end apart: 11, of which 6 were waited for; matrix products, arithmetic and copies ran while one was open for 0% of the time, Pallas kernels for 15%

profile of v8, /device:TPU:1, one launch (start us, length us, event | category | flops | bytes accessed | tf_op | source)
XLA Modules:
  0.0 78.3 jit_solution(5205400187340506694)
XLA Ops:
  0.0 4.0 %collective-permute-start = (bf16[512,256]{1,0:T(8,128)(2,1)}, bf16[512,256]{1,0:T(8,128)(2,1)S(1)}, u32[]{:S(2)}, u32[]{:S(2)}) collective-permute-start(bf16[512,256]{1,0:T(8,128)(2,1)} %own_ref.1), channel_id=1, source_target_pairs={{0,32},{32,0},{64,96},{96,64},{128,160},{160,128},{192,224},{224,1... | collective-permute-start | bytes 786440 | tf_op jit(solution)/shard_map/ppermute | solution.py:373
  4.0 2.7 %gram_in.1 = f32[16,72,128]{2,1,0:T(8,128)} custom-call(bf16[1024,512]{1,0:T(8,128)(2,1)} %data_hbm.1, bf16[512,256]{1,0:T(8,128)(2,1)} %own_ref.1), custom_call_target="tpu_custom_call" | custom-call | flops 536870912 | bytes 1900544 | tf_op jit(solution)/shard_map/gram_in/pallas_call | solution.py:341
  6.8 0.0 copy-start.1
  6.8 10.3 %all-to-all-start = ((f32[16,72,128]{2,1,0:T(8,128)}), f32[16,72,128]{2,1,0:T(8,128)S(1)}, u32[]{:S(2)}, u32[]{:S(2)}) async-start(f32[16,72,128]{2,1,0:T(8,128)} %gram_in.1), calls=%async_computation | async-start | bytes 1179648 | tf_op jit(solution)/shard_map/all_to_all | solution.py:358
  17.1 0.0 collective-permute-done.other_ref
  17.1 0.0 copy-done.1
  17.1 0.5 gram_out.1
  17.6 3.1 %collective-permute-start.1 = (f32[264,128]{1,0:T(8,128)S(1)}, f32[264,128]{1,0:T(8,128)S(1)}, u32[]{:S(2)}, u32[]{:S(2)}) collective-permute-start(f32[264,128]{1,0:T(8,128)S(1)} %get-tuple-element.22), channel_id=1, source_target_pairs={{0,1},{1,0},{2,3},{3,2},{4,5},{5,4},{6,7},{7,6},{8,9},{9,8},{10,11... | collective-permute-start | bytes 405512 | tf_op jit(solution)/shard_map/ppermute | solution.py:363
  20.8 1.0 %collective-permute-done.1.right_ref = f32[264,128]{1,0:T(8,128)S(1)} collective-permute-done((f32[264,128]{1,0:T(8,128)S(1)}, f32[264,128]{1,0:T(8,128)S(1)}, u32[]{:S(2)}, u32[]{:S(2)}) %collective-permute-start.1) | collective-permute-done | bytes 135200 | tf_op jit(solution)/shard_map/ppermute | solution.py:363
  21.8 4.4 %collective-permute-start.2 = (f32[136,128]{1,0:T(8,128)S(1)}, f32[136,128]{1,0:T(8,128)S(1)}, u32[]{:S(2)}, u32[]{:S(2)}) collective-permute-start(f32[136,128]{1,0:T(8,128)S(1)} %get-tuple-element.24), channel_id=1, source_target_pairs={{0,24},{1,25},{2,26},{3,27},{4,28},{5,29},{6,30},{7,31},{8,16},{9,... | collective-permute-start | bytes 208904 | tf_op jit(solution)/shard_map/ppermute | solution.py:368
  26.2 2.2 %collective-permute-done.2.right_ref = f32[136,128]{1,0:T(8,128)S(1)} collective-permute-done((f32[136,128]{1,0:T(8,128)S(1)}, f32[136,128]{1,0:T(8,128)S(1)}, u32[]{:S(2)}, u32[]{:S(2)}) %collective-permute-start.2) | collective-permute-done | bytes 69664 | tf_op jit(solution)/shard_map/ppermute | solution.py:368
  28.3 1.9 %collective-permute-start.3 = (f32[72,128]{1,0:T(8,128)S(1)}, f32[72,128]{1,0:T(8,128)S(1)}, u32[]{:S(2)}, u32[]{:S(2)}) collective-permute-start(f32[72,128]{1,0:T(8,128)S(1)} %get-tuple-element.27), channel_id=1, source_target_pairs={{0,8},{1,9},{2,10},{3,11},{4,12},{5,13},{6,14},{7,15},{8,0},{9,1},... | collective-permute-start | bytes 110600 | tf_op jit(solution)/shard_map/ppermute | solution.py:368
  30.3 2.9 %all-to-all-done.got_ref = f32[16,72,128]{2,1,0:T(8,128)S(1)} async-done(((f32[16,72,128]{2,1,0:T(8,128)}), f32[16,72,128]{2,1,0:T(8,128)S(1)}, u32[]{:S(2)}, u32[]{:S(2)}) %all-to-all-start) | async-done | bytes 589856 | tf_op jit(solution)/shard_map/all_to_all | solution.py:358
  33.2 0.7 sum_in.1
  33.9 0.0 collective-permute-done.3.right_ref
  33.9 0.1 sum_x.1.left_ref
  34.0 4.2 %collective-permute-start.4 = (f32[72,128]{1,0:T(8,128)S(1)}, f32[72,128]{1,0:T(8,128)S(1)}, u32[]{:S(2)}, u32[]{:S(2)}) collective-permute-start(f32[72,128]{1,0:T(8,128)S(1)} %sum_x.1.left_ref), channel_id=1, source_target_pairs={{0,2},{1,3},{2,0},{3,1},{4,6},{5,7},{6,4},{7,5},{8,10},{9,11},{10,... | collective-permute-start | bytes 110600 | tf_op jit(solution)/shard_map/ppermute | solution.py:368
  38.2 6.0 %all-to-all-start.1 = ((bf16[8,64,128]{2,1,0:T(8,128)(2,1)}), bf16[8,64,128]{2,1,0:T(8,128)(2,1)S(1)}, u32[]{:S(2)}, u32[]{:S(2)}) async-start(bf16[8,64,128]{2,1,0:T(8,128)(2,1)} %get-tuple-element.26), calls=%async_computation.1 | async-start | bytes 262144 | tf_op jit(solution)/shard_map/all_to_all | solution.py:358
  44.2 0.0 collective-permute-done.4.right_ref
  44.2 5.3 %collective-permute-start.5 = (f32[72,128]{1,0:T(8,128)S(1)}, f32[72,128]{1,0:T(8,128)S(1)}, u32[]{:S(2)}, u32[]{:S(2)}) collective-permute-start(f32[72,128]{1,0:T(8,128)S(1)} %add_y.1.left_ref), channel_id=1, source_target_pairs={{0,6},{1,7},{2,4},{3,5},{4,2},{5,3},{6,0},{7,1},{8,14},{9,15},{10,... | collective-permute-start | bytes 110600 | tf_op jit(solution)/shard_map/ppermute | solution.py:368
  49.5 1.5 %collective-permute-done.5.right_ref = f32[72,128]{1,0:T(8,128)S(1)} collective-permute-done((f32[72,128]{1,0:T(8,128)S(1)}, f32[72,128]{1,0:T(8,128)S(1)}, u32[]{:S(2)}, u32[]{:S(2)}) %collective-permute-start.5) | collective-permute-done | bytes 36896 | tf_op jit(solution)/shard_map/ppermute | solution.py:368
  51.1 0.7 sum_y.1
  51.8 0.3 all-to-all-done.1.got_ref
  52.1 0.0 copy-start
  52.1 9.2 %all-to-all-start.2 = ((bf16[16,80,128]{2,1,0:T(8,128)(2,1)}), bf16[16,80,128]{2,1,0:T(8,128)(2,1)S(1)}, u32[]{:S(2)}, u32[]{:S(2)}) async-start(bf16[16,80,128]{2,1,0:T(8,128)(2,1)} %get-tuple-element.32), calls=%async_computation.2 | async-start | bytes 655360 | tf_op jit(solution)/shard_map/all_to_all | solution.py:358
  61.3 0.0 copy-done
  61.4 3.3 %collective-permute-start.6 = (bf16[8,64,128]{2,1,0:T(8,128)(2,1)S(1)}, bf16[8,64,128]{2,1,0:T(8,128)(2,1)S(1)}, u32[]{:S(2)}, u32[]{:S(2)}) collective-permute-start(bf16[8,64,128]{2,1,0:T(8,128)(2,1)S(1)} %get-tuple-element.31.after_ref), channel_id=1, source_target_pairs={{0,32},{32,0},{64,96},{96,64},{128,160},{160,128},{192,224},{224,1... | collective-permute-start | bytes 393224 | tf_op jit(solution)/shard_map/ppermute | solution.py:373
  64.7 2.0 %collective-permute-start.7 = (bf16[512,256]{1,0:T(8,128)(2,1)S(1)}, bf16[512,256]{1,0:T(8,128)(2,1)S(1)}, u32[]{:S(2)}, u32[]{:S(2)}) collective-permute-start(bf16[512,256]{1,0:T(8,128)(2,1)S(1)} %get-tuple-element.36), channel_id=1, source_target_pairs={{0,32},{32,0},{64,96},{96,64},{128,160},{160,128},{192,224},{224,1... | collective-permute-start | bytes 786440 | tf_op jit(solution)/shard_map/ppermute | solution.py:373
  66.7 3.3 %collective-permute-done.6.other_ref = bf16[8,64,128]{2,1,0:T(8,128)(2,1)S(1)} collective-permute-done((bf16[8,64,128]{2,1,0:T(8,128)(2,1)S(1)}, bf16[8,64,128]{2,1,0:T(8,128)(2,1)S(1)}, u32[]{:S(2)}, u32[]{:S(2)}) %collective-permute-start.6) | collective-permute-done | bytes 131104 | tf_op jit(solution)/shard_map/ppermute | solution.py:373
  70.0 0.2 unpack_in.1.damped_in_ref
  70.2 0.0 all-to-all-done.2.got_out_ref
  70.2 6.5 %invert.1 = (bf16[512,512]{1,0:T(8,128)(2,1)S(1)}, bf16[512,256]{1,0:T(8,128)(2,1)S(1)}) custom-call(bf16[512,512]{1,0:T(8,128)(2,1)S(1)} %unpack_in.1.damped_in_ref, bf16[16,80,128]{2,1,0:T(8,128)(2,1)S(1)} %all-to-all-done.2.got_out_ref, f32[8,128]{1,0:T(8,128)S(1)} %stage_extra.1.extra_in_ref, f32[8,128]{1,0:T(8,128)S(1)} %get-tuple-element.33.extra_out_ref), custom_call_target="tpu_custom_call" | custom-call | flops 5368709120 | bytes 1646592 | tf_op jit(solution)/shard_map/invert/pallas_call | solution.py:341
  76.8 0.0 collective-permute-done.7.other_weight_ref
  76.8 1.5 %finish.1 = bf16[512,256]{1,0:T(8,128)(2,1)} custom-call(bf16[512,512]{1,0:T(8,128)(2,1)S(1)} %get-tuple-element.34.inverse_ref, bf16[512,256]{1,0:T(8,128)(2,1)S(1)} %get-tuple-element.35.right_ref, bf16[512,256]{1,0:T(8,128)(2,1)S(1)} %copy-done, bf16[512,256]{1,0:T(8,128)(2,1)S(1)} %collective-permute-done.7.other_weight_ref), custom_call_target="tpu_custom_call" | custom-call | flops 402653184 | bytes 1572864 | tf_op jit(solution)/shard_map/finish/pallas_call | solution.py:341
  (5 shorter events, 0.1 us)
Async XLA Ops:
  0.0 17.1 %collective-permute-start = (bf16[512,256]{1,0:T(8,128)(2,1)}, bf16[512,256]{1,0:T(8,128)(2,1)S(1)}, u32[]{:S(2)}, u32[]{:S(2)}) collective-permute-start(bf16[512,256]{1,0:T(8,128)(2,1)} %own_ref.1), channel_id=1, source_target_pairs={{0,32},{32,0},{64,96},{96,64},{128,160},{160,128},{192,224},{224,1... | collective-permute-start | bytes 786440 | tf_op jit(solution)/shard_map/ppermute | solution.py:373
  6.8 10.3 %copy-start.1 = (bf16[512,256]{1,0:T(8,128)(2,1)S(1)}, bf16[512,256]{1,0:T(8,128)(2,1)}, u32[]{:S(2)}) copy-start(bf16[512,256]{1,0:T(8,128)(2,1)} %own_ref.1) | copy-start | bytes 786436
  6.8 26.4 %all-to-all-start = ((f32[16,72,128]{2,1,0:T(8,128)}), f32[16,72,128]{2,1,0:T(8,128)S(1)}, u32[]{:S(2)}, u32[]{:S(2)}) async-start(f32[16,72,128]{2,1,0:T(8,128)} %gram_in.1), calls=%async_computation | async-start | bytes 1179648 | tf_op jit(solution)/shard_map/all_to_all | solution.py:358
  17.6 4.1 %collective-permute-start.1 = (f32[264,128]{1,0:T(8,128)S(1)}, f32[264,128]{1,0:T(8,128)S(1)}, u32[]{:S(2)}, u32[]{:S(2)}) collective-permute-start(f32[264,128]{1,0:T(8,128)S(1)} %get-tuple-element.22), channel_id=1, source_target_pairs={{0,1},{1,0},{2,3},{3,2},{4,5},{5,4},{6,7},{7,6},{8,9},{9,8},{10,11... | collective-permute-start | bytes 405512 | tf_op jit(solution)/shard_map/ppermute | solution.py:363
  21.8 6.6 %collective-permute-start.2 = (f32[136,128]{1,0:T(8,128)S(1)}, f32[136,128]{1,0:T(8,128)S(1)}, u32[]{:S(2)}, u32[]{:S(2)}) collective-permute-start(f32[136,128]{1,0:T(8,128)S(1)} %get-tuple-element.24), channel_id=1, source_target_pairs={{0,24},{1,25},{2,26},{3,27},{4,28},{5,29},{6,30},{7,31},{8,16},{9,... | collective-permute-start | bytes 208904 | tf_op jit(solution)/shard_map/ppermute | solution.py:368
  28.3 5.5 %collective-permute-start.3 = (f32[72,128]{1,0:T(8,128)S(1)}, f32[72,128]{1,0:T(8,128)S(1)}, u32[]{:S(2)}, u32[]{:S(2)}) collective-permute-start(f32[72,128]{1,0:T(8,128)S(1)} %get-tuple-element.27), channel_id=1, source_target_pairs={{0,8},{1,9},{2,10},{3,11},{4,12},{5,13},{6,14},{7,15},{8,0},{9,1},... | collective-permute-start | bytes 110600 | tf_op jit(solution)/shard_map/ppermute | solution.py:368
  34.0 10.2 %collective-permute-start.4 = (f32[72,128]{1,0:T(8,128)S(1)}, f32[72,128]{1,0:T(8,128)S(1)}, u32[]{:S(2)}, u32[]{:S(2)}) collective-permute-start(f32[72,128]{1,0:T(8,128)S(1)} %sum_x.1.left_ref), channel_id=1, source_target_pairs={{0,2},{1,3},{2,0},{3,1},{4,6},{5,7},{6,4},{7,5},{8,10},{9,11},{10,... | collective-permute-start | bytes 110600 | tf_op jit(solution)/shard_map/ppermute | solution.py:368
  38.2 13.9 %all-to-all-start.1 = ((bf16[8,64,128]{2,1,0:T(8,128)(2,1)}), bf16[8,64,128]{2,1,0:T(8,128)(2,1)S(1)}, u32[]{:S(2)}, u32[]{:S(2)}) async-start(bf16[8,64,128]{2,1,0:T(8,128)(2,1)} %get-tuple-element.26), calls=%async_computation.1 | async-start | bytes 262144 | tf_op jit(solution)/shard_map/all_to_all | solution.py:358
  44.2 6.9 %collective-permute-start.5 = (f32[72,128]{1,0:T(8,128)S(1)}, f32[72,128]{1,0:T(8,128)S(1)}, u32[]{:S(2)}, u32[]{:S(2)}) collective-permute-start(f32[72,128]{1,0:T(8,128)S(1)} %add_y.1.left_ref), channel_id=1, source_target_pairs={{0,6},{1,7},{2,4},{3,5},{4,2},{5,3},{6,0},{7,1},{8,14},{9,15},{10,... | collective-permute-start | bytes 110600 | tf_op jit(solution)/shard_map/ppermute | solution.py:368
  52.1 9.2 %copy-start = (bf16[512,256]{1,0:T(8,128)(2,1)S(1)}, bf16[512,256]{1,0:T(8,128)(2,1)}, u32[]{:S(2)}) copy-start(bf16[512,256]{1,0:T(8,128)(2,1)} %weight_ref.3) | copy-start | bytes 786436
  52.1 18.1 %all-to-all-start.2 = ((bf16[16,80,128]{2,1,0:T(8,128)(2,1)}), bf16[16,80,128]{2,1,0:T(8,128)(2,1)S(1)}, u32[]{:S(2)}, u32[]{:S(2)}) async-start(bf16[16,80,128]{2,1,0:T(8,128)(2,1)} %get-tuple-element.32), calls=%async_computation.2 | async-start | bytes 655360 | tf_op jit(solution)/shard_map/all_to_all | solution.py:358
  61.4 8.6 %collective-permute-start.6 = (bf16[8,64,128]{2,1,0:T(8,128)(2,1)S(1)}, bf16[8,64,128]{2,1,0:T(8,128)(2,1)S(1)}, u32[]{:S(2)}, u32[]{:S(2)}) collective-permute-start(bf16[8,64,128]{2,1,0:T(8,128)(2,1)S(1)} %get-tuple-element.31.after_ref), channel_id=1, source_target_pairs={{0,32},{32,0},{64,96},{96,64},{128,160},{160,128},{192,224},{224,1... | collective-permute-start | bytes 393224 | tf_op jit(solution)/shard_map/ppermute | solution.py:373
  64.7 12.1 %collective-permute-start.7 = (bf16[512,256]{1,0:T(8,128)(2,1)S(1)}, bf16[512,256]{1,0:T(8,128)(2,1)S(1)}, u32[]{:S(2)}, u32[]{:S(2)}) collective-permute-start(bf16[512,256]{1,0:T(8,128)(2,1)S(1)} %get-tuple-element.36), channel_id=1, source_target_pairs={{0,32},{32,0},{64,96},{96,64},{128,160},{160,128},{192,224},{224,1... | collective-permute-start | bytes 786440 | tf_op jit(solution)/shard_map/ppermute | solution.py:373

commit v9 on v8

--- a/solution.py
+++ b/solution.py
@@ -14,6 +14,7 @@
 CHUNKS = 2
 RING = 4
 EXTRA = 8
+EXTRA_IN = 5
 EXTRA_HALF = 16
 LATE_START = 10**10
 VMEM_LIMIT = 48 * 1024 * 1024
@@ -97,8 +98,8 @@
     return jnp.sum(jnp.sum(value, axis=1, keepdims=True), axis=0, keepdims=True)
 
 
-def gram_in_kernel(tokens, data_hbm, grads_hbm, out_ref, data_ref, grads_ref, sems):
-    pieces, piece_rows = out_ref.shape[0], out_ref.shape[1] - EXTRA
+def gram_in_kernel(tokens, pieces, data_hbm, grads_hbm, out_ref, data_ref, grads_ref, sems):
+    piece_rows = out_ref.shape[0] // pieces - EXTRA_IN
     per_tile = TILE // piece_rows
     scale = 1.0 / tokens
     rows = data_ref.shape[0] // CHUNKS
@@ -121,17 +122,16 @@
 
     def store(position, value):
         for part in range(per_tile):
-            out_ref[position * per_tile + part, :piece_rows, :] = value[
+            start = (position * per_tile + part) * (piece_rows + EXTRA_IN)
+            out_ref[start : start + piece_rows, :] = value[
                 part * piece_rows : (part + 1) * piece_rows
             ]
 
     diagonal = pack_gram([scale * quarter for quarter in quarters], store)
-    filler = jnp.zeros((EXTRA - diagonal.shape[0] - 1, TILE), jnp.float32)
-    extra = jnp.concatenate(
-        [diagonal, jnp.broadcast_to(energy, (1, TILE)), filler], axis=0
-    )
+    extra = jnp.concatenate([diagonal, jnp.broadcast_to(energy, (1, TILE))], axis=0)
     for piece in range(pieces):
-        out_ref[piece, piece_rows:, :] = extra
+        end = (piece + 1) * (piece_rows + EXTRA_IN)
+        out_ref[end - EXTRA_IN : end, :] = extra
 
 
 def gram_out_kernel(tokens, own_ref, other_ref, keep_ref, send_ref, data_ref, packed_ref):
@@ -177,10 +177,11 @@
     out_ref[...] = left_ref[...] + right_ref[...]
 
 
-def sum_pieces(ref):
-    total = ref[0]
-    for piece in range(1, ref.shape[0]):
-        total = total + ref[piece]
+def sum_pieces(ref, pieces):
+    rows = ref.shape[0] // pieces
+    total = ref[:rows, :]
+    for piece in range(1, pieces):
+        total = total + ref[piece * rows : (piece + 1) * rows, :]
     return total
 
 
@@ -191,13 +192,14 @@
     return [high, middle, rest - middle]
 
 
-def sum_in_kernel(got_ref, after_ref, send_ref, extra_ref):
-    total = sum_pieces(got_ref)
+def sum_in_kernel(pieces, got_ref, after_ref, send_ref, extra_ref):
+    total = sum_pieces(got_ref, pieces)
     rows = send_ref.shape[1]
     rounded = total[:rows].astype(jnp.bfloat16)
     for piece in range(send_ref.shape[0]):
         send_ref[piece] = rounded
-    extra_ref[...] = total[rows:]
+    filler = jnp.zeros((EXTRA - EXTRA_IN, TILE), jnp.float32)
+    extra_ref[...] = jnp.concatenate([total[rows:], filler], axis=0)
 
 
 def sum_x_kernel(count, left_ref, right_ref, extra_in_ref, out_ref):
@@ -388,10 +390,10 @@
 
     other_grads = swap_half(output_grads)
     send_in = local_call(
-        functools.partial(gram_in_kernel, total_tokens),
+        functools.partial(gram_in_kernel, total_tokens, groups),
         "gram_in",
         (activations, output_grads),
-        shape_of(groups, in_rows + EXTRA, TILE),
+        shape_of(groups * (in_rows + EXTRA_IN), TILE),
         scratch=[
             pltpu.VMEM(activations.shape, half_type),
             pltpu.VMEM(output_grads.shape, half_type),
@@ -401,7 +403,7 @@
         space=pltpu.HBM,
         limit=GRAM_LIMIT,
     )
-    got_in = exchange(send_in, "grp")
+    got_in = exchange(send_in.reshape(groups, -1, 1, TILE), "grp").reshape(-1, TILE)
 
     keep, give = local_call(
         functools.partial(gram_out_kernel, total_tokens),
@@ -426,7 +428,7 @@
             (shape_of(rows + EXTRA, TILE),) * 2,
         )
     to_all_in, extra_in = local_call(
-        sum_in_kernel,
+        functools.partial(sum_in_kernel, groups),
         "sum_in",
         (got_in, keep),
         (shape_of(groups // 2, in_rows, TILE, dtype=half_type), shape_of(EXTRA, TILE)),

time: 79 us -> 79 us (level)
  no operation moved by 1% of the time
where the time goes in v9:
time: 79 us; the launch traced here: 78.3 us
  starting transfers between devices  54.3 us (69%)
  Pallas kernels  13.1 us (17%)
  waiting for transfers between devices  10.7 us (14%)
    all_to_all x3, starting transfers between devices, exchange(): lax.all_to_all(value, axis, 0, 0, tiled=True, axis_index_groups=groups)  26 us
    ppermute x4, starting transfers between devices, swap_along(): return lax.ppermute(value, 'blk', pairs)  15.8 us
    pallas_call x13, Pallas kernels, local_call(): pl.pallas_call(kernel, out_shape=outs, in_specs=[pl.BlockSpec(memory_spac...  13.1 us
    ppermute x3, starting transfers between devices, swap_half(): return lax.ppermute(value, 'grp', pairs)  9.33 us
    ppermute x4, waiting for transfers between devices, swap_along(): return lax.ppermute(value, 'blk', pairs)  3.69 us
    ppermute x3, waiting for transfers between devices, swap_half(): return lax.ppermute(value, 'grp', pairs)  3.31 us
    ppermute x1, starting transfers between devices, swap_core(): return lax.ppermute(value, 'blk', pairs)  3.14 us
    all_to_all x3, waiting for transfers between devices, exchange(): lax.all_to_all(value, axis, 0, 0, tiled=True, axis_index_groups=groups)  2.77 us
  transfers between devices with their start and end apart: 11, of which 6 were waited for; matrix products, arithmetic and copies ran while one was open for 0% of the time, Pallas kernels for 15%

profile of v9, /device:TPU:1, one launch (start us, length us, event | category | flops | bytes accessed | tf_op | source)
XLA Modules:
  0.0 78.3 jit_solution(7013838052242663198)
XLA Ops:
  0.0 4.0 %collective-permute-start = (bf16[512,256]{1,0:T(8,128)(2,1)}, bf16[512,256]{1,0:T(8,128)(2,1)S(1)}, u32[]{:S(2)}, u32[]{:S(2)}) collective-permute-start(bf16[512,256]{1,0:T(8,128)(2,1)} %own_ref.1), channel_id=1, source_target_pairs={{0,32},{32,0},{64,96},{96,64},{128,160},{160,128},{192,224},{224,1... | collective-permute-start | bytes 786440 | tf_op jit(solution)/shard_map/ppermute | solution.py:375
  4.0 2.7 %gram_in.1 = f32[1104,128]{1,0:T(8,128)} custom-call(bf16[1024,512]{1,0:T(8,128)(2,1)} %data_hbm.1, bf16[512,256]{1,0:T(8,128)(2,1)} %own_ref.1), custom_call_target="tpu_custom_call" | custom-call | flops 536870912 | bytes 1875968 | tf_op jit(solution)/shard_map/gram_in/pallas_call | solution.py:343
  6.8 0.0 copy-start.1
  6.8 10.3 %all-to-all-start = ((f32[16,69,1,128]{3,2,1,0:T(1,128)}), f32[16,69,1,128]{3,2,1,0:T(1,128)S(1)}, u32[]{:S(2)}, u32[]{:S(2)}) async-start(f32[16,69,1,128]{3,2,1,0:T(1,128)} %bitcast.3), calls=%async_computation | async-start | bytes 1130496 | tf_op jit(solution)/shard_map/all_to_all | solution.py:360
  17.1 0.0 collective-permute-done.other_ref
  17.1 0.0 copy-done.1
  17.1 0.5 gram_out.1
  17.6 3.1 %collective-permute-start.1 = (f32[264,128]{1,0:T(8,128)S(1)}, f32[264,128]{1,0:T(8,128)S(1)}, u32[]{:S(2)}, u32[]{:S(2)}) collective-permute-start(f32[264,128]{1,0:T(8,128)S(1)} %get-tuple-element.22), channel_id=1, source_target_pairs={{0,1},{1,0},{2,3},{3,2},{4,5},{5,4},{6,7},{7,6},{8,9},{9,8},{10,11... | collective-permute-start | bytes 405512 | tf_op jit(solution)/shard_map/ppermute | solution.py:365
  20.8 1.0 %collective-permute-done.1.right_ref = f32[264,128]{1,0:T(8,128)S(1)} collective-permute-done((f32[264,128]{1,0:T(8,128)S(1)}, f32[264,128]{1,0:T(8,128)S(1)}, u32[]{:S(2)}, u32[]{:S(2)}) %collective-permute-start.1) | collective-permute-done | bytes 135200 | tf_op jit(solution)/shard_map/ppermute | solution.py:365
  21.8 4.4 %collective-permute-start.2 = (f32[136,128]{1,0:T(8,128)S(1)}, f32[136,128]{1,0:T(8,128)S(1)}, u32[]{:S(2)}, u32[]{:S(2)}) collective-permute-start(f32[136,128]{1,0:T(8,128)S(1)} %get-tuple-element.24), channel_id=1, source_target_pairs={{0,24},{1,25},{2,26},{3,27},{4,28},{5,29},{6,30},{7,31},{8,16},{9,... | collective-permute-start | bytes 208904 | tf_op jit(solution)/shard_map/ppermute | solution.py:370
  26.2 2.2 %collective-permute-done.2.right_ref = f32[136,128]{1,0:T(8,128)S(1)} collective-permute-done((f32[136,128]{1,0:T(8,128)S(1)}, f32[136,128]{1,0:T(8,128)S(1)}, u32[]{:S(2)}, u32[]{:S(2)}) %collective-permute-start.2) | collective-permute-done | bytes 69664 | tf_op jit(solution)/shard_map/ppermute | solution.py:370
  28.3 1.9 %collective-permute-start.3 = (f32[72,128]{1,0:T(8,128)S(1)}, f32[72,128]{1,0:T(8,128)S(1)}, u32[]{:S(2)}, u32[]{:S(2)}) collective-permute-start(f32[72,128]{1,0:T(8,128)S(1)} %get-tuple-element.27), channel_id=1, source_target_pairs={{0,8},{1,9},{2,10},{3,11},{4,12},{5,13},{6,14},{7,15},{8,0},{9,1},... | collective-permute-start | bytes 110600 | tf_op jit(solution)/shard_map/ppermute | solution.py:370
  30.3 2.5 %all-to-all-done = f32[16,69,1,128]{3,2,1,0:T(1,128)S(1)} async-done(((f32[16,69,1,128]{3,2,1,0:T(1,128)}), f32[16,69,1,128]{3,2,1,0:T(1,128)S(1)}, u32[]{:S(2)}, u32[]{:S(2)}) %all-to-all-start) | async-done | bytes 565280 | tf_op jit(solution)/shard_map/all_to_all | solution.py:360
  32.7 0.7 sum_in.1
  33.4 0.0 collective-permute-done.3.right_ref
  33.4 0.1 sum_x.1.left_ref
  33.5 4.2 %collective-permute-start.4 = (f32[72,128]{1,0:T(8,128)S(1)}, f32[72,128]{1,0:T(8,128)S(1)}, u32[]{:S(2)}, u32[]{:S(2)}) collective-permute-start(f32[72,128]{1,0:T(8,128)S(1)} %sum_x.1.left_ref), channel_id=1, source_target_pairs={{0,2},{1,3},{2,0},{3,1},{4,6},{5,7},{6,4},{7,5},{8,10},{9,11},{10,... | collective-permute-start | bytes 110600 | tf_op jit(solution)/shard_map/ppermute | solution.py:370
  37.7 6.5 %all-to-all-start.1 = ((bf16[8,64,128]{2,1,0:T(8,128)(2,1)}), bf16[8,64,128]{2,1,0:T(8,128)(2,1)S(1)}, u32[]{:S(2)}, u32[]{:S(2)}) async-start(bf16[8,64,128]{2,1,0:T(8,128)(2,1)} %get-tuple-element.26), calls=%async_computation.1 | async-start | bytes 262144 | tf_op jit(solution)/shard_map/all_to_all | solution.py:360
  44.2 0.0 collective-permute-done.4.right_ref
  44.2 5.3 %collective-permute-start.5 = (f32[72,128]{1,0:T(8,128)S(1)}, f32[72,128]{1,0:T(8,128)S(1)}, u32[]{:S(2)}, u32[]{:S(2)}) collective-permute-start(f32[72,128]{1,0:T(8,128)S(1)} %add_y.1.left_ref), channel_id=1, source_target_pairs={{0,6},{1,7},{2,4},{3,5},{4,2},{5,3},{6,0},{7,1},{8,14},{9,15},{10,... | collective-permute-start | bytes 110600 | tf_op jit(solution)/shard_map/ppermute | solution.py:370
  49.5 1.5 %collective-permute-done.5.right_ref = f32[72,128]{1,0:T(8,128)S(1)} collective-permute-done((f32[72,128]{1,0:T(8,128)S(1)}, f32[72,128]{1,0:T(8,128)S(1)}, u32[]{:S(2)}, u32[]{:S(2)}) %collective-permute-start.5) | collective-permute-done | bytes 36896 | tf_op jit(solution)/shard_map/ppermute | solution.py:370
  51.1 0.7 sum_y.1
  51.8 0.3 all-to-all-done.1.got_ref
  52.1 0.0 copy-start
  52.1 9.2 %all-to-all-start.2 = ((bf16[16,80,128]{2,1,0:T(8,128)(2,1)}), bf16[16,80,128]{2,1,0:T(8,128)(2,1)S(1)}, u32[]{:S(2)}, u32[]{:S(2)}) async-start(bf16[16,80,128]{2,1,0:T(8,128)(2,1)} %get-tuple-element.32), calls=%async_computation.2 | async-start | bytes 655360 | tf_op jit(solution)/shard_map/all_to_all | solution.py:360
  61.3 0.0 copy-done
  61.4 3.3 %collective-permute-start.6 = (bf16[8,64,128]{2,1,0:T(8,128)(2,1)S(1)}, bf16[8,64,128]{2,1,0:T(8,128)(2,1)S(1)}, u32[]{:S(2)}, u32[]{:S(2)}) collective-permute-start(bf16[8,64,128]{2,1,0:T(8,128)(2,1)S(1)} %get-tuple-element.31.after_ref), channel_id=1, source_target_pairs={{0,32},{32,0},{64,96},{96,64},{128,160},{160,128},{192,224},{224,1... | collective-permute-start | bytes 393224 | tf_op jit(solution)/shard_map/ppermute | solution.py:375
  64.7 2.0 %collective-permute-start.7 = (bf16[512,256]{1,0:T(8,128)(2,1)S(1)}, bf16[512,256]{1,0:T(8,128)(2,1)S(1)}, u32[]{:S(2)}, u32[]{:S(2)}) collective-permute-start(bf16[512,256]{1,0:T(8,128)(2,1)S(1)} %get-tuple-element.36), channel_id=1, source_target_pairs={{0,32},{32,0},{64,96},{96,64},{128,160},{160,128},{192,224},{224,1... | collective-permute-start | bytes 786440 | tf_op jit(solution)/shard_map/ppermute | solution.py:375
  66.7 3.3 %collective-permute-done.6.other_ref = bf16[8,64,128]{2,1,0:T(8,128)(2,1)S(1)} collective-permute-done((bf16[8,64,128]{2,1,0:T(8,128)(2,1)S(1)}, bf16[8,64,128]{2,1,0:T(8,128)(2,1)S(1)}, u32[]{:S(2)}, u32[]{:S(2)}) %collective-permute-start.6) | collective-permute-done | bytes 131104 | tf_op jit(solution)/shard_map/ppermute | solution.py:375
  70.0 0.2 unpack_in.1.damped_in_ref
  70.2 0.0 all-to-all-done.2.got_out_ref
  70.2 6.5 %invert.1 = (bf16[512,512]{1,0:T(8,128)(2,1)S(1)}, bf16[512,256]{1,0:T(8,128)(2,1)S(1)}) custom-call(bf16[512,512]{1,0:T(8,128)(2,1)S(1)} %unpack_in.1.damped_in_ref, bf16[16,80,128]{2,1,0:T(8,128)(2,1)S(1)} %all-to-all-done.2.got_out_ref, f32[8,128]{1,0:T(8,128)S(1)} %stage_extra.1.extra_in_ref, f32[8,128]{1,0:T(8,128)S(1)} %get-tuple-element.33.extra_out_ref), custom_call_target="tpu_custom_call" | custom-call | flops 5368709120 | bytes 1646592 | tf_op jit(solution)/shard_map/invert/pallas_call | solution.py:343
  76.8 0.0 collective-permute-done.7.other_weight_ref
  76.8 1.5 %finish.1 = bf16[512,256]{1,0:T(8,128)(2,1)} custom-call(bf16[512,512]{1,0:T(8,128)(2,1)S(1)} %get-tuple-element.34.inverse_ref, bf16[512,256]{1,0:T(8,128)(2,1)S(1)} %get-tuple-element.35.right_ref, bf16[512,256]{1,0:T(8,128)(2,1)S(1)} %copy-done, bf16[512,256]{1,0:T(8,128)(2,1)S(1)} %collective-permute-done.7.other_weight_ref), custom_call_target="tpu_custom_call" | custom-call | flops 402653184 | bytes 1572864 | tf_op jit(solution)/shard_map/finish/pallas_call | solution.py:343
  (5 shorter events, 0.1 us)
Async XLA Ops:
  0.0 17.1 %collective-permute-start = (bf16[512,256]{1,0:T(8,128)(2,1)}, bf16[512,256]{1,0:T(8,128)(2,1)S(1)}, u32[]{:S(2)}, u32[]{:S(2)}) collective-permute-start(bf16[512,256]{1,0:T(8,128)(2,1)} %own_ref.1), channel_id=1, source_target_pairs={{0,32},{32,0},{64,96},{96,64},{128,160},{160,128},{192,224},{224,1... | collective-permute-start | bytes 786440 | tf_op jit(solution)/shard_map/ppermute | solution.py:375
  6.8 10.3 %copy-start.1 = (bf16[512,256]{1,0:T(8,128)(2,1)S(1)}, bf16[512,256]{1,0:T(8,128)(2,1)}, u32[]{:S(2)}) copy-start(bf16[512,256]{1,0:T(8,128)(2,1)} %own_ref.1) | copy-start | bytes 786436
  6.8 25.9 %all-to-all-start = ((f32[16,69,1,128]{3,2,1,0:T(1,128)}), f32[16,69,1,128]{3,2,1,0:T(1,128)S(1)}, u32[]{:S(2)}, u32[]{:S(2)}) async-start(f32[16,69,1,128]{3,2,1,0:T(1,128)} %bitcast.3), calls=%async_computation | async-start | bytes 1130496 | tf_op jit(solution)/shard_map/all_to_all | solution.py:360
  17.6 4.1 %collective-permute-start.1 = (f32[264,128]{1,0:T(8,128)S(1)}, f32[264,128]{1,0:T(8,128)S(1)}, u32[]{:S(2)}, u32[]{:S(2)}) collective-permute-start(f32[264,128]{1,0:T(8,128)S(1)} %get-tuple-element.22), channel_id=1, source_target_pairs={{0,1},{1,0},{2,3},{3,2},{4,5},{5,4},{6,7},{7,6},{8,9},{9,8},{10,11... | collective-permute-start | bytes 405512 | tf_op jit(solution)/shard_map/ppermute | solution.py:365
  21.8 6.6 %collective-permute-start.2 = (f32[136,128]{1,0:T(8,128)S(1)}, f32[136,128]{1,0:T(8,128)S(1)}, u32[]{:S(2)}, u32[]{:S(2)}) collective-permute-start(f32[136,128]{1,0:T(8,128)S(1)} %get-tuple-element.24), channel_id=1, source_target_pairs={{0,24},{1,25},{2,26},{3,27},{4,28},{5,29},{6,30},{7,31},{8,16},{9,... | collective-permute-start | bytes 208904 | tf_op jit(solution)/shard_map/ppermute | solution.py:370
  28.3 5.1 %collective-permute-start.3 = (f32[72,128]{1,0:T(8,128)S(1)}, f32[72,128]{1,0:T(8,128)S(1)}, u32[]{:S(2)}, u32[]{:S(2)}) collective-permute-start(f32[72,128]{1,0:T(8,128)S(1)} %get-tuple-element.27), channel_id=1, source_target_pairs={{0,8},{1,9},{2,10},{3,11},{4,12},{5,13},{6,14},{7,15},{8,0},{9,1},... | collective-permute-start | bytes 110600 | tf_op jit(solution)/shard_map/ppermute | solution.py:370
  33.5 10.7 %collective-permute-start.4 = (f32[72,128]{1,0:T(8,128)S(1)}, f32[72,128]{1,0:T(8,128)S(1)}, u32[]{:S(2)}, u32[]{:S(2)}) collective-permute-start(f32[72,128]{1,0:T(8,128)S(1)} %sum_x.1.left_ref), channel_id=1, source_target_pairs={{0,2},{1,3},{2,0},{3,1},{4,6},{5,7},{6,4},{7,5},{8,10},{9,11},{10,... | collective-permute-start | bytes 110600 | tf_op jit(solution)/shard_map/ppermute | solution.py:370
  37.7 14.4 %all-to-all-start.1 = ((bf16[8,64,128]{2,1,0:T(8,128)(2,1)}), bf16[8,64,128]{2,1,0:T(8,128)(2,1)S(1)}, u32[]{:S(2)}, u32[]{:S(2)}) async-start(bf16[8,64,128]{2,1,0:T(8,128)(2,1)} %get-tuple-element.26), calls=%async_computation.1 | async-start | bytes 262144 | tf_op jit(solution)/shard_map/all_to_all | solution.py:360
  44.2 6.9 %collective-permute-start.5 = (f32[72,128]{1,0:T(8,128)S(1)}, f32[72,128]{1,0:T(8,128)S(1)}, u32[]{:S(2)}, u32[]{:S(2)}) collective-permute-start(f32[72,128]{1,0:T(8,128)S(1)} %add_y.1.left_ref), channel_id=1, source_target_pairs={{0,6},{1,7},{2,4},{3,5},{4,2},{5,3},{6,0},{7,1},{8,14},{9,15},{10,... | collective-permute-start | bytes 110600 | tf_op jit(solution)/shard_map/ppermute | solution.py:370
  52.1 9.2 %copy-start = (bf16[512,256]{1,0:T(8,128)(2,1)S(1)}, bf16[512,256]{1,0:T(8,128)(2,1)}, u32[]{:S(2)}) copy-start(bf16[512,256]{1,0:T(8,128)(2,1)} %weight_ref.3) | copy-start | bytes 786436
  52.1 18.1 %all-to-all-start.2 = ((bf16[16,80,128]{2,1,0:T(8,128)(2,1)}), bf16[16,80,128]{2,1,0:T(8,128)(2,1)S(1)}, u32[]{:S(2)}, u32[]{:S(2)}) async-start(bf16[16,80,128]{2,1,0:T(8,128)(2,1)} %get-tuple-element.32), calls=%async_computation.2 | async-start | bytes 655360 | tf_op jit(solution)/shard_map/all_to_all | solution.py:360
  61.4 8.6 %collective-permute-start.6 = (bf16[8,64,128]{2,1,0:T(8,128)(2,1)S(1)}, bf16[8,64,128]{2,1,0:T(8,128)(2,1)S(1)}, u32[]{:S(2)}, u32[]{:S(2)}) collective-permute-start(bf16[8,64,128]{2,1,0:T(8,128)(2,1)S(1)} %get-tuple-element.31.after_ref), channel_id=1, source_target_pairs={{0,32},{32,0},{64,96},{96,64},{128,160},{160,128},{192,224},{224,1... | collective-permute-start | bytes 393224 | tf_op jit(solution)/shard_map/ppermute | solution.py:375
  64.7 12.1 %collective-permute-start.7 = (bf16[512,256]{1,0:T(8,128)(2,1)S(1)}, bf16[512,256]{1,0:T(8,128)(2,1)S(1)}, u32[]{:S(2)}, u32[]{:S(2)}) collective-permute-start(bf16[512,256]{1,0:T(8,128)(2,1)S(1)} %get-tuple-element.36), channel_id=1, source_target_pairs={{0,32},{32,0},{64,96},{96,64},{128,160},{160,128},{192,224},{224,1... | collective-permute-start | bytes 786440 | tf_op jit(solution)/shard_map/ppermute | solution.py:375

commit v10 on v8

--- a/solution.py
+++ b/solution.py
@@ -259,7 +259,7 @@
     own_column = pl.ds(pl.multiple_of(parity * half, half), half)
 
     scalars = jnp.zeros((EXTRA_HALF, TILE), jnp.float32)
-    for piece in range(pieces // 2):
+    for piece in range(0, pieces, 2):
         scalars = scalars + got_out_ref[piece, rows_out:, :].astype(jnp.float32)
     sum_in = scalars[0:1] + scalars[1:2] + scalars[2:3]
     sum_out = scalars[3:4] + scalars[4:5] + scalars[5:6]
@@ -281,7 +281,7 @@
         core, first = position % RING // CORES, position % CORES * per_tile
         return jnp.concatenate(
             [
-                got_out_ref[(pair * RING + first + part) * CORES + core, :rows_out, :]
+                got_out_ref[((first + part) * CORES + core) * 2 + pair, :rows_out, :]
                 for part in range(per_tile)
             ],
             axis=0,
@@ -460,9 +460,9 @@
     same_plane = [
         [
             (2 * z + parity) * owners + x * x_stride + y * y_stride + core
-            for parity in range(2)
             for x in range(RING)
             for core in range(CORES)
+            for parity in range(2)
         ]
         for z in range(groups // 2)
         for y in range(RING)

time: 79 us -> 79 us (level)
  no operation moved by 1% of the time
where the time goes in v10:
time: 79 us; the launch traced here: 78.3 us
  starting transfers between devices  53.8 us (68%)
  Pallas kernels  13.1 us (17%)
  waiting for transfers between devices  11.2 us (14%)
    all_to_all x3, starting transfers between devices, exchange(): lax.all_to_all(value, axis, 0, 0, tiled=True, axis_index_groups=groups)  25.5 us
    ppermute x4, starting transfers between devices, swap_along(): return lax.ppermute(value, 'blk', pairs)  15.8 us
    pallas_call x13, Pallas kernels, local_call(): pl.pallas_call(kernel, out_shape=outs, in_specs=[pl.BlockSpec(memory_spac...  13.1 us
    ppermute x3, starting transfers between devices, swap_half(): return lax.ppermute(value, 'grp', pairs)  9.33 us
    ppermute x4, waiting for transfers between devices, swap_along(): return lax.ppermute(value, 'blk', pairs)  3.69 us
    ppermute x3, waiting for transfers between devices, swap_half(): return lax.ppermute(value, 'grp', pairs)  3.31 us
    all_to_all x3, waiting for transfers between devices, exchange(): lax.all_to_all(value, axis, 0, 0, tiled=True, axis_index_groups=groups)  3.21 us
    ppermute x1, starting transfers between devices, swap_core(): return lax.ppermute(value, 'blk', pairs)  3.14 us
  transfers between devices with their start and end apart: 11, of which 6 were waited for; matrix products, arithmetic and copies ran while one was open for 0% of the time, Pallas kernels for 15%

profile of v10, /device:TPU:1, one launch (start us, length us, event | category | flops | bytes accessed | tf_op | source)
XLA Modules:
  0.0 78.3 jit_solution(9786508968401082498)
XLA Ops:
  0.0 4.0 %collective-permute-start = (bf16[512,256]{1,0:T(8,128)(2,1)}, bf16[512,256]{1,0:T(8,128)(2,1)S(1)}, u32[]{:S(2)}, u32[]{:S(2)}) collective-permute-start(bf16[512,256]{1,0:T(8,128)(2,1)} %own_ref.1), channel_id=1, source_target_pairs={{0,32},{32,0},{64,96},{96,64},{128,160},{160,128},{192,224},{224,1... | collective-permute-start | bytes 786440 | tf_op jit(solution)/shard_map/ppermute | solution.py:373
  4.0 2.7 %gram_in.1 = f32[16,72,128]{2,1,0:T(8,128)} custom-call(bf16[1024,512]{1,0:T(8,128)(2,1)} %data_hbm.1, bf16[512,256]{1,0:T(8,128)(2,1)} %own_ref.1), custom_call_target="tpu_custom_call" | custom-call | flops 536870912 | bytes 1900544 | tf_op jit(solution)/shard_map/gram_in/pallas_call | solution.py:341
  6.8 0.0 copy-start.1
  6.8 10.3 %all-to-all-start = ((f32[16,72,128]{2,1,0:T(8,128)}), f32[16,72,128]{2,1,0:T(8,128)S(1)}, u32[]{:S(2)}, u32[]{:S(2)}) async-start(f32[16,72,128]{2,1,0:T(8,128)} %gram_in.1), calls=%async_computation | async-start | bytes 1179648 | tf_op jit(solution)/shard_map/all_to_all | solution.py:358
  17.1 0.0 collective-permute-done.other_ref
  17.1 0.0 copy-done.1
  17.1 0.5 gram_out.1
  17.6 3.1 %collective-permute-start.1 = (f32[264,128]{1,0:T(8,128)S(1)}, f32[264,128]{1,0:T(8,128)S(1)}, u32[]{:S(2)}, u32[]{:S(2)}) collective-permute-start(f32[264,128]{1,0:T(8,128)S(1)} %get-tuple-element.22), channel_id=1, source_target_pairs={{0,1},{1,0},{2,3},{3,2},{4,5},{5,4},{6,7},{7,6},{8,9},{9,8},{10,11... | collective-permute-start | bytes 405512 | tf_op jit(solution)/shard_map/ppermute | solution.py:363
  20.8 1.0 %collective-permute-done.1.right_ref = f32[264,128]{1,0:T(8,128)S(1)} collective-permute-done((f32[264,128]{1,0:T(8,128)S(1)}, f32[264,128]{1,0:T(8,128)S(1)}, u32[]{:S(2)}, u32[]{:S(2)}) %collective-permute-start.1) | collective-permute-done | bytes 135200 | tf_op jit(solution)/shard_map/ppermute | solution.py:363
  21.8 4.4 %collective-permute-start.2 = (f32[136,128]{1,0:T(8,128)S(1)}, f32[136,128]{1,0:T(8,128)S(1)}, u32[]{:S(2)}, u32[]{:S(2)}) collective-permute-start(f32[136,128]{1,0:T(8,128)S(1)} %get-tuple-element.24), channel_id=1, source_target_pairs={{0,24},{1,25},{2,26},{3,27},{4,28},{5,29},{6,30},{7,31},{8,16},{9,... | collective-permute-start | bytes 208904 | tf_op jit(solution)/shard_map/ppermute | solution.py:368
  26.2 2.2 %collective-permute-done.2.right_ref = f32[136,128]{1,0:T(8,128)S(1)} collective-permute-done((f32[136,128]{1,0:T(8,128)S(1)}, f32[136,128]{1,0:T(8,128)S(1)}, u32[]{:S(2)}, u32[]{:S(2)}) %collective-permute-start.2) | collective-permute-done | bytes 69664 | tf_op jit(solution)/shard_map/ppermute | solution.py:368
  28.3 1.9 %collective-permute-start.3 = (f32[72,128]{1,0:T(8,128)S(1)}, f32[72,128]{1,0:T(8,128)S(1)}, u32[]{:S(2)}, u32[]{:S(2)}) collective-permute-start(f32[72,128]{1,0:T(8,128)S(1)} %get-tuple-element.27), channel_id=1, source_target_pairs={{0,8},{1,9},{2,10},{3,11},{4,12},{5,13},{6,14},{7,15},{8,0},{9,1},... | collective-permute-start | bytes 110600 | tf_op jit(solution)/shard_map/ppermute | solution.py:368
  30.3 2.9 %all-to-all-done.got_ref = f32[16,72,128]{2,1,0:T(8,128)S(1)} async-done(((f32[16,72,128]{2,1,0:T(8,128)}), f32[16,72,128]{2,1,0:T(8,128)S(1)}, u32[]{:S(2)}, u32[]{:S(2)}) %all-to-all-start) | async-done | bytes 589856 | tf_op jit(solution)/shard_map/all_to_all | solution.py:358
  33.2 0.7 sum_in.1
  33.9 0.0 collective-permute-done.3.right_ref
  33.9 0.1 sum_x.1.left_ref
  34.0 4.2 %collective-permute-start.4 = (f32[72,128]{1,0:T(8,128)S(1)}, f32[72,128]{1,0:T(8,128)S(1)}, u32[]{:S(2)}, u32[]{:S(2)}) collective-permute-start(f32[72,128]{1,0:T(8,128)S(1)} %sum_x.1.left_ref), channel_id=1, source_target_pairs={{0,2},{1,3},{2,0},{3,1},{4,6},{5,7},{6,4},{7,5},{8,10},{9,11},{10,... | collective-permute-start | bytes 110600 | tf_op jit(solution)/shard_map/ppermute | solution.py:368
  38.2 6.0 %all-to-all-start.1 = ((bf16[8,64,128]{2,1,0:T(8,128)(2,1)}), bf16[8,64,128]{2,1,0:T(8,128)(2,1)S(1)}, u32[]{:S(2)}, u32[]{:S(2)}) async-start(bf16[8,64,128]{2,1,0:T(8,128)(2,1)} %get-tuple-element.26), calls=%async_computation.1 | async-start | bytes 262144 | tf_op jit(solution)/shard_map/all_to_all | solution.py:358
  44.2 0.0 collective-permute-done.4.right_ref
  44.2 5.3 %collective-permute-start.5 = (f32[72,128]{1,0:T(8,128)S(1)}, f32[72,128]{1,0:T(8,128)S(1)}, u32[]{:S(2)}, u32[]{:S(2)}) collective-permute-start(f32[72,128]{1,0:T(8,128)S(1)} %add_y.1.left_ref), channel_id=1, source_target_pairs={{0,6},{1,7},{2,4},{3,5},{4,2},{5,3},{6,0},{7,1},{8,14},{9,15},{10,... | collective-permute-start | bytes 110600 | tf_op jit(solution)/shard_map/ppermute | solution.py:368
  49.5 1.5 %collective-permute-done.5.right_ref = f32[72,128]{1,0:T(8,128)S(1)} collective-permute-done((f32[72,128]{1,0:T(8,128)S(1)}, f32[72,128]{1,0:T(8,128)S(1)}, u32[]{:S(2)}, u32[]{:S(2)}) %collective-permute-start.5) | collective-permute-done | bytes 36896 | tf_op jit(solution)/shard_map/ppermute | solution.py:368
  51.1 0.7 sum_y.1
  51.8 0.3 all-to-all-done.1.got_ref
  52.1 0.0 copy-start
  52.1 9.2 %all-to-all-start.2 = ((bf16[16,80,128]{2,1,0:T(8,128)(2,1)}), bf16[16,80,128]{2,1,0:T(8,128)(2,1)S(1)}, u32[]{:S(2)}, u32[]{:S(2)}) async-start(bf16[16,80,128]{2,1,0:T(8,128)(2,1)} %get-tuple-element.32), calls=%async_computation.2 | async-start | bytes 655360 | tf_op jit(solution)/shard_map/all_to_all | solution.py:358
  61.3 0.0 copy-done
  61.4 3.3 %collective-permute-start.6 = (bf16[8,64,128]{2,1,0:T(8,128)(2,1)S(1)}, bf16[8,64,128]{2,1,0:T(8,128)(2,1)S(1)}, u32[]{:S(2)}, u32[]{:S(2)}) collective-permute-start(bf16[8,64,128]{2,1,0:T(8,128)(2,1)S(1)} %get-tuple-element.31.after_ref), channel_id=1, source_target_pairs={{0,32},{32,0},{64,96},{96,64},{128,160},{160,128},{192,224},{224,1... | collective-permute-start | bytes 393224 | tf_op jit(solution)/shard_map/ppermute | solution.py:373
  64.7 2.0 %collective-permute-start.7 = (bf16[512,256]{1,0:T(8,128)(2,1)S(1)}, bf16[512,256]{1,0:T(8,128)(2,1)S(1)}, u32[]{:S(2)}, u32[]{:S(2)}) collective-permute-start(bf16[512,256]{1,0:T(8,128)(2,1)S(1)} %get-tuple-element.36), channel_id=1, source_target_pairs={{0,32},{32,0},{64,96},{96,64},{128,160},{160,128},{192,224},{224,1... | collective-permute-start | bytes 786440 | tf_op jit(solution)/shard_map/ppermute | solution.py:373
  66.7 3.3 %collective-permute-done.6.other_ref = bf16[8,64,128]{2,1,0:T(8,128)(2,1)S(1)} collective-permute-done((bf16[8,64,128]{2,1,0:T(8,128)(2,1)S(1)}, bf16[8,64,128]{2,1,0:T(8,128)(2,1)S(1)}, u32[]{:S(2)}, u32[]{:S(2)}) %collective-permute-start.6) | collective-permute-done | bytes 131104 | tf_op jit(solution)/shard_map/ppermute | solution.py:373
  70.0 0.2 unpack_in.1.damped_in_ref
  70.2 0.0 all-to-all-done.2.got_out_ref
  70.2 6.5 %invert.1 = (bf16[512,512]{1,0:T(8,128)(2,1)S(1)}, bf16[512,256]{1,0:T(8,128)(2,1)S(1)}) custom-call(bf16[512,512]{1,0:T(8,128)(2,1)S(1)} %unpack_in.1.damped_in_ref, bf16[16,80,128]{2,1,0:T(8,128)(2,1)S(1)} %all-to-all-done.2.got_out_ref, f32[8,128]{1,0:T(8,128)S(1)} %stage_extra.1.extra_in_ref, f32[8,128]{1,0:T(8,128)S(1)} %get-tuple-element.33.extra_out_ref), custom_call_target="tpu_custom_call" | custom-call | flops 5368709120 | bytes 1646592 | tf_op jit(solution)/shard_map/invert/pallas_call | solution.py:341
  76.8 0.0 collective-permute-done.7.other_weight_ref
  76.8 1.5 %finish.1 = bf16[512,256]{1,0:T(8,128)(2,1)} custom-call(bf16[512,512]{1,0:T(8,128)(2,1)S(1)} %get-tuple-element.34.inverse_ref, bf16[512,256]{1,0:T(8,128)(2,1)S(1)} %get-tuple-element.35.right_ref, bf16[512,256]{1,0:T(8,128)(2,1)S(1)} %copy-done, bf16[512,256]{1,0:T(8,128)(2,1)S(1)} %collective-permute-done.7.other_weight_ref), custom_call_target="tpu_custom_call" | custom-call | flops 402653184 | bytes 1572864 | tf_op jit(solution)/shard_map/finish/pallas_call | solution.py:341
  (5 shorter events, 0.1 us)
Async XLA Ops:
  0.0 17.1 %collective-permute-start = (bf16[512,256]{1,0:T(8,128)(2,1)}, bf16[512,256]{1,0:T(8,128)(2,1)S(1)}, u32[]{:S(2)}, u32[]{:S(2)}) collective-permute-start(bf16[512,256]{1,0:T(8,128)(2,1)} %own_ref.1), channel_id=1, source_target_pairs={{0,32},{32,0},{64,96},{96,64},{128,160},{160,128},{192,224},{224,1... | collective-permute-start | bytes 786440 | tf_op jit(solution)/shard_map/ppermute | solution.py:373
  6.8 10.3 %copy-start.1 = (bf16[512,256]{1,0:T(8,128)(2,1)S(1)}, bf16[512,256]{1,0:T(8,128)(2,1)}, u32[]{:S(2)}) copy-start(bf16[512,256]{1,0:T(8,128)(2,1)} %own_ref.1) | copy-start | bytes 786436
  6.8 26.4 %all-to-all-start = ((f32[16,72,128]{2,1,0:T(8,128)}), f32[16,72,128]{2,1,0:T(8,128)S(1)}, u32[]{:S(2)}, u32[]{:S(2)}) async-start(f32[16,72,128]{2,1,0:T(8,128)} %gram_in.1), calls=%async_computation | async-start | bytes 1179648 | tf_op jit(solution)/shard_map/all_to_all | solution.py:358
  17.6 4.1 %collective-permute-start.1 = (f32[264,128]{1,0:T(8,128)S(1)}, f32[264,128]{1,0:T(8,128)S(1)}, u32[]{:S(2)}, u32[]{:S(2)}) collective-permute-start(f32[264,128]{1,0:T(8,128)S(1)} %get-tuple-element.22), channel_id=1, source_target_pairs={{0,1},{1,0},{2,3},{3,2},{4,5},{5,4},{6,7},{7,6},{8,9},{9,8},{10,11... | collective-permute-start | bytes 405512 | tf_op jit(solution)/shard_map/ppermute | solution.py:363
  21.8 6.6 %collective-permute-start.2 = (f32[136,128]{1,0:T(8,128)S(1)}, f32[136,128]{1,0:T(8,128)S(1)}, u32[]{:S(2)}, u32[]{:S(2)}) collective-permute-start(f32[136,128]{1,0:T(8,128)S(1)} %get-tuple-element.24), channel_id=1, source_target_pairs={{0,24},{1,25},{2,26},{3,27},{4,28},{5,29},{6,30},{7,31},{8,16},{9,... | collective-permute-start | bytes 208904 | tf_op jit(solution)/shard_map/ppermute | solution.py:368
  28.3 5.5 %collective-permute-start.3 = (f32[72,128]{1,0:T(8,128)S(1)}, f32[72,128]{1,0:T(8,128)S(1)}, u32[]{:S(2)}, u32[]{:S(2)}) collective-permute-start(f32[72,128]{1,0:T(8,128)S(1)} %get-tuple-element.27), channel_id=1, source_target_pairs={{0,8},{1,9},{2,10},{3,11},{4,12},{5,13},{6,14},{7,15},{8,0},{9,1},... | collective-permute-start | bytes 110600 | tf_op jit(solution)/shard_map/ppermute | solution.py:368
  34.0 10.2 %collective-permute-start.4 = (f32[72,128]{1,0:T(8,128)S(1)}, f32[72,128]{1,0:T(8,128)S(1)}, u32[]{:S(2)}, u32[]{:S(2)}) collective-permute-start(f32[72,128]{1,0:T(8,128)S(1)} %sum_x.1.left_ref), channel_id=1, source_target_pairs={{0,2},{1,3},{2,0},{3,1},{4,6},{5,7},{6,4},{7,5},{8,10},{9,11},{10,... | collective-permute-start | bytes 110600 | tf_op jit(solution)/shard_map/ppermute | solution.py:368
  38.2 13.9 %all-to-all-start.1 = ((bf16[8,64,128]{2,1,0:T(8,128)(2,1)}), bf16[8,64,128]{2,1,0:T(8,128)(2,1)S(1)}, u32[]{:S(2)}, u32[]{:S(2)}) async-start(bf16[8,64,128]{2,1,0:T(8,128)(2,1)} %get-tuple-element.26), calls=%async_computation.1 | async-start | bytes 262144 | tf_op jit(solution)/shard_map/all_to_all | solution.py:358
  44.2 6.9 %collective-permute-start.5 = (f32[72,128]{1,0:T(8,128)S(1)}, f32[72,128]{1,0:T(8,128)S(1)}, u32[]{:S(2)}, u32[]{:S(2)}) collective-permute-start(f32[72,128]{1,0:T(8,128)S(1)} %add_y.1.left_ref), channel_id=1, source_target_pairs={{0,6},{1,7},{2,4},{3,5},{4,2},{5,3},{6,0},{7,1},{8,14},{9,15},{10,... | collective-permute-start | bytes 110600 | tf_op jit(solution)/shard_map/ppermute | solution.py:368
  52.1 9.2 %copy-start = (bf16[512,256]{1,0:T(8,128)(2,1)S(1)}, bf16[512,256]{1,0:T(8,128)(2,1)}, u32[]{:S(2)}) copy-start(bf16[512,256]{1,0:T(8,128)(2,1)} %weight_ref.3) | copy-start | bytes 786436
  52.1 18.1 %all-to-all-start.2 = ((bf16[16,80,128]{2,1,0:T(8,128)(2,1)}), bf16[16,80,128]{2,1,0:T(8,128)(2,1)S(1)}, u32[]{:S(2)}, u32[]{:S(2)}) async-start(bf16[16,80,128]{2,1,0:T(8,128)(2,1)} %get-tuple-element.32), calls=%async_computation.2 | async-start | bytes 655360 | tf_op jit(solution)/shard_map/all_to_all | solution.py:358
  61.4 8.6 %collective-permute-start.6 = (bf16[8,64,128]{2,1,0:T(8,128)(2,1)S(1)}, bf16[8,64,128]{2,1,0:T(8,128)(2,1)S(1)}, u32[]{:S(2)}, u32[]{:S(2)}) collective-permute-start(bf16[8,64,128]{2,1,0:T(8,128)(2,1)S(1)} %get-tuple-element.31.after_ref), channel_id=1, source_target_pairs={{0,32},{32,0},{64,96},{96,64},{128,160},{160,128},{192,224},{224,1... | collective-permute-start | bytes 393224 | tf_op jit(solution)/shard_map/ppermute | solution.py:373
  64.7 12.1 %collective-permute-start.7 = (bf16[512,256]{1,0:T(8,128)(2,1)S(1)}, bf16[512,256]{1,0:T(8,128)(2,1)S(1)}, u32[]{:S(2)}, u32[]{:S(2)}) collective-permute-start(bf16[512,256]{1,0:T(8,128)(2,1)S(1)} %get-tuple-element.36), channel_id=1, source_target_pairs={{0,32},{32,0},{64,96},{96,64},{128,160},{160,128},{192,224},{224,1... | collective-permute-start | bytes 786440 | tf_op jit(solution)/shard_map/ppermute | solution.py:373
